TPU v7x, 128 devices: a whole 4x4x4 slice. The times are simulated.
128 devices in a mesh: dp: 16 (over y, x), expert: 4 (over z), et: 2 (over core).
Axes of the slice: x: 4, y: 4, z: 4, core: 2. Of those that a mesh axis runs over, the one named last changes fastest.
Arguments:
- tokens: bfloat16 [4096, 3072], P(('dp', 'expert'), 'et'), may hold values from -6 to 6
- expert_ids: int32 [4096, 2], P(('dp', 'expert')), may hold values from 0 to 3, all different within a row; in each aligned block of 64 rows (0 to 63, 64 to 127, ...) at most 40 rows name the same one
- gate_scores: float32 [4096, 2], P(('dp', 'expert')), may hold values from 0.1 to 1
- w_gate: bfloat16 [4, 3072, 8192], P('expert', None, ('dp', 'et')), may hold values from -0.109375 to 0.109375
- w_up: bfloat16 [4, 3072, 8192], P('expert', None, ('dp', 'et')), may hold values from -0.109375 to 0.109375
- w_down: bfloat16 [4, 8192, 3072], P('expert', 'dp', 'et'), may hold values from -0.0625 to 0.0625
Outputs:
- mixed: bfloat16 [4096, 3072], P(('dp', 'expert'), 'et')
Inputs may be any that keep to these rules, and one draw needn't show every extreme that they name: `expert_ids`: the two experts of a token differ. Among the 64 tokens of one index pair of dp and expert (aligned blocks of rows) no expert is named more than 40 times, and in every draw some block names some expert exactly 40 times.
All inputs are finite; a program needn't handle non-finite values.
Results may differ from a plain program's by a relative error of at most 0.02.
Values may be sent and summed in bfloat16 or wider, within the bound.
No kernel may reach another device: no remote copies, remote signals or barrier semaphores. Data moves between devices by JAX's collectives and lax.ppermute only.
A program may use at most 128 MiB of HBM per device.

v0:
```python
import jax
import jax.numpy as jnp
from jax import lax
from jax.sharding import PartitionSpec as P


def on_device(tokens, expert_ids, gate_scores, w_gate, w_up, w_down):
    tok_rows = tokens.shape[0]
    width = tokens.shape[1]
    n_expert = lax.axis_size("expert")
    capacity = max(2, 5 * tok_rows // (2 * n_expert))
    flat = expert_ids.reshape(-1)
    routed = flat.shape[0]
    order = jnp.arange(routed, dtype=jnp.int32)
    earlier = (order[None, :] < order[:, None]) & (flat[None, :] == flat[:, None])
    position = jnp.sum(earlier.astype(jnp.int32), axis=1)
    slot = flat * capacity + position
    select = (jnp.arange(n_expert * capacity, dtype=jnp.int32)[:, None] == slot[None, :]).astype(
        jnp.bfloat16
    )
    doubled = jnp.repeat(tokens, 2, axis=0)
    outgoing = jnp.dot(select, doubled, preferred_element_type=jnp.float32).astype(jnp.bfloat16)
    arrived = lax.all_to_all(outgoing, "expert", split_axis=0, concat_axis=0, tiled=True)
    full_rows = lax.all_gather(arrived, "et", axis=1, tiled=True)
    piece = lax.all_gather(full_rows, "dp", axis=0, tiled=True)
    gate = jnp.dot(piece, w_gate[0], preferred_element_type=jnp.float32)
    up = jnp.dot(piece, w_up[0], preferred_element_type=jnp.float32)
    local_hidden = (jax.nn.silu(gate) * up).astype(jnp.bfloat16)
    hidden = lax.all_gather(local_hidden, "et", axis=1, tiled=True)
    down_local = w_down[0]
    summed = lax.psum_scatter(
        jnp.dot(hidden, down_local, preferred_element_type=jnp.float32).astype(jnp.bfloat16),
        "dp",
        scatter_dimension=0,
        tiled=True,
    )
    returned = lax.all_to_all(summed, "expert", split_axis=0, concat_axis=0, tiled=True)
    picked = returned[slot].astype(jnp.float32)
    weighted = picked * gate_scores.reshape(-1)[:, None]
    return weighted.reshape(tok_rows, 2, width).sum(axis=1).astype(jnp.bfloat16)


def solution(mesh):
    placed = (
        P(("dp", "expert"), "et"),
        P(("dp", "expert"), None),
        P(("dp", "expert"), None),
        P("expert", None, ("dp", "et")),
        P("expert", None, ("dp", "et")),
        P("expert", "dp", "et"),
    )
    return jax.shard_map(
        on_device, mesh=mesh, in_specs=placed, out_specs=P(("dp", "expert"), "et"), check_vma=False
    )
```

profile of v0, /device:TPU:1, one launch (start us, length us, event | category | flops | bytes accessed | tf_op | source)
XLA Modules:
  0.0 275.8 jit_solution(3660674468895420077)
XLA Ops:
  6.5 0.0 copy-start
  6.5 0.9 copy.13
  7.4 0.1 reshape.58
  7.6 0.2 convert_reduce_fusion
  7.8 1.1 broadcast_in_dim.2
  8.9 0.1 reshape.59
  9.1 0.0 copy-start.4
  9.1 0.3 convolution_convert_fusion.1
  9.3 14.0 %all_to_all.24 = bf16[4,40,1536]{2,1,0:T(8,128)(2,1)S(1)} all-to-all(bf16[4,40,1536]{2,1,0:T(8,128)(2,1)S(1)} %bitcast.24), channel_id=1, replica_groups=mesh['dp'=16,'expert'=4,'et'=2] {'expert'}, dimensions={0} | all-to-all | bytes 983040 | tf_op jit(solution)/shard_map/all_to_all | solution.py:23
  23.4 4.1 %all_gather.9 = bf16[160,3072]{1,0:T(8,128)(2,1)} all-gather(bf16[160,1536]{1,0:T(8,128)(2,1)S(1)} %bitcast.25), channel_id=1, replica_groups=mesh['dp'=16,'expert'=4,'et'=2] {'et'}, dimensions={1}, use_global_device_ids=true | all-gather | bytes 1474560 | tf_op jit(solution)/shard_map/all_gather | solution.py:24
  27.5 0.0 all-gather.3.cloned.1.call-update
  27.5 0.0 all-gather.5.cloned.1.call-start
  27.5 105.1 %all-gather.3.cloned.1.call-done = bf16[2560,3072]{1,0:T(8,128)(2,1)} async-done(((bf16[160,3072]{1,0:T(8,128)(2,1)}), bf16[2560,3072]{1,0:T(8,128)(2,1)}) %all-gather.3.cloned.1.call-update) | async-done | bytes 15728656 | tf_op jit(solution)/shard_map/all_gather | solution.py:25
  132.7 9.5 %fusion.3 = f32[2560,256]{1,0:T(8,128)S(1)} fusion(bf16[2560,3072]{1,0:T(8,128)(2,1)} %all-gather.3.cloned.1.call-done, bf16[1,3072,256]{2,1,0:T(8,128)(2,1)S(1)} %copy-done.4), kind=kOutput, calls=%fused_computation.7 | convolution fusion | flops 4026531840 | bytes 19922944 | tf_op jit(solution)/shard_map/dot_general | solution.py:26
  142.2 0.4 copy-done.3
  142.6 0.4 copy-done.5
  143.0 6.2 %fusion = bf16[2560,256]{1,0:T(8,128)(2,1)} fusion(bf16[2560,3072]{1,0:T(8,128)(2,1)S(1)} %copy-done.3, f32[2560,256]{1,0:T(8,128)S(1)} %fusion.3, bf16[1,3072,256]{2,1,0:T(8,128)(2,1)S(1)} %copy-done.5), kind=kOutput, calls=%fused_computation.3 | convolution fusion | flops 4030464000 | bytes 21233664 | tf_op jit(solution)/shard_map/dot_general | solution.py:27
  149.3 0.0 all-gather.5.cloned.1.call-update
  149.3 0.0 reduce-scatter.2.cloned.1.call-start
  149.3 14.0 %all-gather.5.cloned.1.call-done = bf16[2560,512]{1,0:T(8,128)(2,1)} async-done(((bf16[2560,256]{1,0:T(8,128)(2,1)}), bf16[2560,512]{1,0:T(8,128)(2,1)}) %all-gather.5.cloned.1.call-update) | async-done | bytes 2621456 | tf_op jit(solution)/shard_map/all_gather | solution.py:29
  163.3 0.0 copy-done
  163.3 8.1 %convolution_convert_fusion = bf16[2560,1536]{1,0:T(8,128)(2,1)} fusion(bf16[2560,512]{1,0:T(8,128)(2,1)} %all-gather.5.cloned.1.call-done, bf16[1,512,1536]{2,1,0:T(8,128)(2,1)S(1)} %copy-done), kind=kOutput, calls=%fused_computation.1 | convolution fusion | flops 4030464000 | bytes 12058624 | tf_op jit(solution)/shard_map/dot_general | solution.py:32
  171.4 0.0 reduce-scatter.2.cloned.1.call-update
  171.4 83.8 %reduce-scatter.2.cloned.1.call-done = bf16[160,1536]{1,0:T(8,128)(2,1)} async-done(((bf16[2560,1536]{1,0:T(8,128)(2,1)}), bf16[160,1536]{1,0:T(8,128)(2,1)}) %reduce-scatter.2.cloned.1.call-update) | async-done | bytes 491536 | tf_op jit(solution)/shard_map/reduce_scatter | solution.py:31
  255.3 4.0 %all-to-all-start.1 = ((bf16[4,40,1536]{2,1,0:T(8,128)(2,1)}), bf16[4,40,1536]{2,1,0:T(8,128)(2,1)S(1)}, u32[]{:S(2)}, u32[]{:S(2)}) async-start(bf16[4,40,1536]{2,1,0:T(8,128)(2,1)} %bitcast.26), calls=%async_computation.2 | async-start | bytes 983040 | tf_op jit(solution)/shard_map/all_to_all | solution.py:37
  259.3 0.1 copy.14
  259.4 0.1 mul.46
  259.5 0.1 copy.15
  259.6 6.4 %all-to-all-done.1 = bf16[4,40,1536]{2,1,0:T(8,128)(2,1)S(1)} async-done(((bf16[4,40,1536]{2,1,0:T(8,128)(2,1)}), bf16[4,40,1536]{2,1,0:T(8,128)(2,1)S(1)}, u32[]{:S(2)}, u32[]{:S(2)}) %all-to-all-start.1) | async-done | bytes 491552 | tf_op jit(solution)/shard_map/all_to_all | solution.py:37
  266.1 0.9 gather_fusion
  267.0 0.5 reshape.60
  267.5 1.8 multiply_reduce_fusion
  (12 shorter events, 0.0 us)
Async XLA Ops:
  6.5 156.8 %copy-start = (bf16[1,512,1536]{2,1,0:T(8,128)(2,1)S(1)}, bf16[1,512,1536]{2,1,0:T(8,128)(2,1)}, u32[]{:S(2)}) copy-start(bf16[1,512,1536]{2,1,0:T(8,128)(2,1)} %param.11) | copy-start | bytes 4718596
  6.5 126.1 %all-gather.3.cloned.1.call-start = ((), (), s32[]{:S(2)}) async-start(), calls=%async_computation.3 | async-start | bytes 16711680 | tf_op jit(solution)/shard_map/all_gather | solution.py:25
  9.1 123.6 %copy-start.4 = (bf16[1,3072,256]{2,1,0:T(8,128)(2,1)S(1)}, bf16[1,3072,256]{2,1,0:T(8,128)(2,1)}, u32[]{:S(2)}) copy-start(bf16[1,3072,256]{2,1,0:T(8,128)(2,1)} %param.9) | copy-start | bytes 4718596
  27.5 135.8 %all-gather.5.cloned.1.call-start = ((), (), s32[]{:S(2)}) async-start(), calls=%async_computation.4 | async-start | bytes 3932160 | tf_op jit(solution)/shard_map/all_gather | solution.py:29
  132.7 9.9 %copy-start.3 = (bf16[2560,3072]{1,0:T(8,128)(2,1)S(1)}, bf16[2560,3072]{1,0:T(8,128)(2,1)}, u32[]{:S(2)}) copy-start(bf16[2560,3072]{1,0:T(8,128)(2,1)} %all-gather.3.cloned.1.call-done) | copy-start | bytes 47185924
  132.7 10.4 %copy-start.5 = (bf16[1,3072,256]{2,1,0:T(8,128)(2,1)S(1)}, bf16[1,3072,256]{2,1,0:T(8,128)(2,1)}, u32[]{:S(2)}) copy-start(bf16[1,3072,256]{2,1,0:T(8,128)(2,1)} %param.10) | copy-start | bytes 4718596
  149.3 106.0 %reduce-scatter.2.cloned.1.call-start = ((), (), s32[]{:S(2)}) async-start(), calls=%async_computation.5 | async-start | bytes 8355840 | tf_op jit(solution)/shard_map/reduce_scatter | solution.py:31
  171.4 87.9 %copy-start.1 = (s32[64,2]{0,1:T(2,128)S(1)}, s32[64,2]{0,1:T(2,128)}, u32[]{:S(2)}) copy-start(s32[64,2]{0,1:T(2,128)} %param.7) | copy-start | bytes 1540
  171.4 88.1 %copy-start.2 = (f32[64,2]{0,1:T(2,128)S(1)}, f32[64,2]{0,1:T(2,128)}, u32[]{:S(2)}) copy-start(f32[64,2]{0,1:T(2,128)} %param.8) | copy-start | bytes 1540
  255.3 10.8 %all-to-all-start.1 = ((bf16[4,40,1536]{2,1,0:T(8,128)(2,1)}), bf16[4,40,1536]{2,1,0:T(8,128)(2,1)S(1)}, u32[]{:S(2)}, u32[]{:S(2)}) async-start(bf16[4,40,1536]{2,1,0:T(8,128)(2,1)} %bitcast.26), calls=%async_computation.2 | async-start | bytes 983040 | tf_op jit(solution)/shard_map/all_to_all | solution.py:37
Sparse Core Ops, SparseCore 0:
  27.6 104.9 all-gather.2
  149.4 13.8 all-gather.4
  171.5 83.6 reduce-scatter.1
where the time goes:
time: 278 us; the launch traced here: 276 us
  waiting for transfers between devices  209 us (75%)
  matrix products  24.1 us (9%)
  blocking collectives  18.1 us (7%)
  between operations  13.2 us (5%)
  local copies, waits for them, and re-layouts  4.86 us (2%)
  starting transfers between devices  4.1 us (1%)
    all_gather x1, waiting for transfers between devices, on_device(): piece = lax.all_gather(full_rows, 'dp', axis=0, tiled=True)  105 us
    reduce_scatter x1, waiting for transfers between devices, on_device(): lax.psum_scatter(jnp.dot(hidden, down_local, preferred_element_type=jnp.f...  83.8 us
    all_to_all x1, blocking collectives, on_device(): lax.all_to_all(outgoing, 'expert', split_axis=0, concat_axis=0, tiled=True)  14 us
    all_gather x1, waiting for transfers between devices, on_device(): hidden = lax.all_gather(local_hidden, 'et', axis=1, tiled=True)  14 us
    dot_general x1, matrix products, on_device(): gate = jnp.dot(piece, w_gate[0], preferred_element_type=jnp.float32)  9.54 us
    dot_general x1, matrix products, on_device(): jnp.dot(hidden, down_local, preferred_element_type=jnp.float32)  8.07 us
    all_to_all x1, waiting for transfers between devices, on_device(): lax.all_to_all(summed, 'expert', split_axis=0, concat_axis=0, tiled=True)  6.42 us
    dot_general x1, matrix products, on_device(): up = jnp.dot(piece, w_up[0], preferred_element_type=jnp.float32)  6.24 us
  transfers between devices with their start and end apart: 4, of which 4 were waited for; matrix products, arithmetic and copies ran while one was open for 0% of the time, Pallas kernels for 0%

commit v1 on v0

v1 whole, which is shorter than its diff:
```python
import jax
import jax.numpy as jnp
from jax import lax
from jax.experimental import pallas as pl
from jax.experimental.pallas import tpu as pltpu
from jax.sharding import PartitionSpec as P

SIDE = 4
BF = jnp.bfloat16
F32 = jnp.float32


def plane_perm(first, step):
    pairs = []
    for y in range(SIDE):
        for x in range(SIDE):
            for c in range(2):
                along_x = (c == 0) == first
                ty, tx = (y, (x + step) % SIDE) if along_x else ((y + step) % SIDE, x)
                pairs.append(((y * SIDE + x) * 2 + c, (ty * SIDE + tx) * 2 + c))
    return pairs


def shift(a, first, step):
    return lax.ppermute(a, ("dp", "et"), plane_perm(first, step))


def swap(a):
    return lax.ppermute(a, "et", [(0, 1), (1, 0)])


def gather_ring(a, first):
    half = a.shape[1] // 2
    left = shift(a, first, 1)
    right = shift(a, first, -1)
    far_a = shift(left[:, :half], first, 1)
    far_b = shift(right[:, half:], first, -1)
    return a, left, right, far_a, far_b


def add(*terms):
    total = terms[0].astype(F32)
    for t in terms[1:]:
        total = total + t.astype(F32)
    return total.astype(BF)


def scatter_ring(own, left, right, far_a, far_b, first):
    half = far_a.shape[1]
    got_a = shift(far_a, first, 1)
    got_b = shift(far_b, first, -1)
    right = jnp.concatenate([add(right[:, :half], got_a), right[:, half:]], axis=1)
    left = jnp.concatenate([left[:, :half], add(left[:, half:], got_b)], axis=1)
    from_left = shift(right, first, 1)
    from_right = shift(left, first, -1)
    return add(own, from_left, from_right)


def ffn_body(core, own, left, right, far_a, far_b, wg0, wg1, wu0, wu1, wd0, wd1,
             p_own, p_left, p_right, p_far_a, p_far_b, rows, hidden):
    c = core[0]
    n = own.shape[0]
    half = far_a.shape[1]
    hid = wg0.shape[1]
    rows[pl.ds(0, n), :] = own[...]
    rows[pl.ds(n, n), :] = left[...]
    rows[pl.ds(2 * n, n), :] = right[...]
    rows[pl.ds(3 * n, n), pl.ds(0, half)] = far_a[...]
    rows[pl.ds(3 * n, n), pl.ds(half, half)] = far_b[...]
    mine = pl.multiple_of(c * half, half)
    other = pl.multiple_of((1 - c) * half, half)

    def up_step(i, carry):
        at = pl.ds(pl.multiple_of(i * 2 * n, 2 * n), 2 * n)
        for k, (wg, wu) in enumerate(((wg0, wu0), (wg1, wu1))):
            def proj(w):
                return jnp.dot(
                    rows[at, pl.ds(0, half)], w[pl.ds(mine, half), :], preferred_element_type=F32
                ) + jnp.dot(
                    rows[at, pl.ds(half, half)], w[pl.ds(other, half), :], preferred_element_type=F32
                )

            g = proj(wg)
            u = proj(wu)
            hidden[at, pl.ds(k * hid, hid)] = (g / (1.0 + jnp.exp(-g)) * u).astype(BF)
        return carry

    lax.fori_loop(0, 2, up_step, 0)
    mine_h = pl.multiple_of(c * hid, hid)
    other_h = pl.multiple_of((1 - c) * hid, hid)

    def down(first, w):
        h = hidden[pl.ds(first, 2 * n), :]
        return jnp.dot(h[:, :hid], w[pl.ds(mine_h, hid), :], preferred_element_type=F32) + jnp.dot(
            h[:, hid:], w[pl.ds(other_h, hid), :], preferred_element_type=F32
        )

    a = down(0, wd0)
    p_own[:, pl.ds(0, half)] = a[:n].astype(BF)
    p_left[:, pl.ds(0, half)] = a[n:].astype(BF)
    a = down(0, wd1)
    p_own[:, pl.ds(half, half)] = a[:n].astype(BF)
    p_left[:, pl.ds(half, half)] = a[n:].astype(BF)
    a = down(2 * n, wd0)
    p_right[:, pl.ds(0, half)] = a[:n].astype(BF)
    p_far_a[...] = a[n:].astype(BF)
    a = down(2 * n, wd1)
    p_right[:, pl.ds(half, half)] = a[:n].astype(BF)
    p_far_b[...] = a[n:].astype(BF)


def ffn(core, groups, weights):
    n, d = groups[0].shape
    half = d // 2
    hid = weights[0].shape[1]
    whole = pl.BlockSpec(memory_space=pltpu.VMEM)
    full = jax.ShapeDtypeStruct((n, d), BF)
    part = jax.ShapeDtypeStruct((n, half), BF)
    return pl.pallas_call(
        ffn_body,
        in_specs=[pl.BlockSpec(memory_space=pltpu.SMEM)] + [whole] * 11,
        out_specs=[whole] * 5,
        out_shape=[full, full, full, part, part],
        scratch_shapes=[pltpu.VMEM((4 * n, d), BF), pltpu.VMEM((4 * n, 2 * hid), BF)],
        compiler_params=pltpu.CompilerParams(vmem_limit_bytes=48 * 1024 * 1024),
        cost_estimate=pl.CostEstimate(
            flops=2 * 4 * n * d * hid * 6, bytes_accessed=16 * n * d + 12 * d * hid,
            transcendentals=8 * n * hid,
        ),
        name="ffn",
    )(core, *groups, *weights)


def on_device(tokens, expert_ids, gate_scores, w_gate, w_up, w_down):
    tok_rows, half = tokens.shape
    n_expert = lax.axis_size("expert")
    capacity = max(2, 5 * tok_rows // (2 * n_expert))
    z = lax.axis_index("expert")
    c = lax.axis_index("et")
    core = c.astype(jnp.int32).reshape(1)

    other_tokens = swap(tokens)
    weights = []
    for w in (w_gate[0], w_up[0], w_down[0]):
        weights += [w, swap(w)]

    t = jnp.arange(tok_rows, dtype=jnp.int32)
    slots = jnp.arange(capacity, dtype=jnp.int32)
    before = (t[:, None] < t[None, :]).astype(F32)

    def choose(e):
        named = expert_ids == e
        mask = jnp.any(named, axis=1)
        rank = jnp.dot(mask.astype(F32)[None, :], before, preferred_element_type=F32)[0].astype(jnp.int32)
        pick = (slots[:, None] == rank[None, :]) & mask[None, :]
        return pick.astype(BF), jnp.sum(jnp.where(named, gate_scores, 0.0), axis=1)

    send = [
        [(s * 2, s * 2) for s in range(n_expert)] + [(s * 2 + 1, (s - 1) % n_expert * 2 + 1) for s in range(n_expert)],
        [(s * 2, (s + 2) % n_expert * 2) for s in range(n_expert)]
        + [(s * 2 + 1, (s + 1) % n_expert * 2 + 1) for s in range(n_expert)],
    ]
    picks = [choose((z - c) % n_expert), choose((z + 2 - c) % n_expert)]

    arrived = []
    for (pick, _), pairs in zip(picks, send):
        out = jnp.concatenate(
            [jnp.dot(pick, v, preferred_element_type=F32).astype(BF) for v in (tokens, other_tokens)], axis=1
        )
        arrived.append(lax.ppermute(out, ("expert", "et"), pairs))

    total = jnp.zeros((tok_rows, 2 * half), F32)
    for a, (pick, score), pairs in zip(arrived, picks, send):
        own, left, right, far_a, far_b = gather_ring(a, True)
        line = jnp.concatenate([own, left, right, jnp.concatenate([far_a, far_b], axis=1)], axis=0)
        parts = ffn(core, gather_ring(line, False), weights)
        s = scatter_ring(*parts, False).reshape(SIDE, capacity, 2 * half)
        done = scatter_ring(s[0], s[1], s[2], s[3, :, :half], s[3, :, half:], True)
        back = lax.ppermute(done, ("expert", "et"), [(b, a_) for a_, b in pairs])
        rows = lax.dot_general(pick, back, (((0,), (0,)), ((), ())), preferred_element_type=F32)
        total = total + rows * score[:, None]
    theirs = swap(total[:, half:].astype(BF))
    return (total[:, :half] + theirs.astype(F32)).astype(BF)


def solution(mesh):
    placed = (
        P(("dp", "expert"), "et"),
        P(("dp", "expert"), None),
        P(("dp", "expert"), None),
        P("expert", None, ("dp", "et")),
        P("expert", None, ("dp", "et")),
        P("expert", "dp", "et"),
    )
    return jax.shard_map(
        on_device, mesh=mesh, in_specs=placed, out_specs=P(("dp", "expert"), "et"), check_vma=False
    )
```

time: 278 us -> 158 us (0.57)
  waiting for transfers between devices: 209 us -> 67.6 us
  starting transfers between devices: 4.1 us -> 59.4 us
  Pallas kernels: 0 us -> 22.4 us
  matrix products: 24.1 us -> 3.38 us
  blocking collectives: 18.1 us -> 0 us
  between operations: 13.2 us -> 0.64 us
  local copies, waits for them, and re-layouts: 4.86 us -> 0.45 us
    all_gather x2 -> x0, waiting for transfers between devices: 119 us -> none  [the longest x1 105 us: on_device(): piece = lax.all_gather(full_rows, 'dp', axis=0, tiled=True)]
    reduce_scatter x1 -> x0, waiting for transfers between devices: 83.8 us -> none  [on_device(): lax.psum_scatter(jnp.dot(hidden, down_local, preferred_element_type=jnp.f...]
    ppermute x0 -> x41, waiting for transfers between devices: none -> 67.6 us  [the longest x32 50 us: shift(): return lax.ppermute(a, ('dp', 'et'), plane_perm(first, step))]
    ppermute x0 -> x41, starting transfers between devices: none -> 59.4 us  [the longest x32 44 us: shift(): return lax.ppermute(a, ('dp', 'et'), plane_perm(first, step))]
    pallas_call x0 -> x2, Pallas kernels: none -> 22.4 us  [ffn(): pl.pallas_call(ffn_body, in_specs=[pl.BlockSpec(memory_space=pltpu.SMEM)]...]
    dot_general x4 -> x8, matrix products: 24.1 us -> 3.38 us  [the longest x4 2.49 us: on_device(): jnp.dot(pick, v, preferred_element_type=F32).astype(BF)]
    all_to_all x1 -> x0, blocking collectives: 14 us -> none  [on_device(): lax.all_to_all(outgoing, 'expert', split_axis=0, concat_axis=0, tiled=True)]
    all_to_all x1 -> x0, waiting for transfers between devices: 6.42 us -> none  [on_device(): lax.all_to_all(summed, 'expert', split_axis=0, concat_axis=0, tiled=True)]
  transfers between devices with their start and end apart: 4 -> 41, of which waited for: 4 -> 16; matrix products, arithmetic and copies ran while one was open for 0% -> 4% of each run, Pallas kernels for 0% -> 14%
where the time goes in v1:
time: 158 us
  waiting for transfers between devices  67.6 us (43%)
  starting transfers between devices  59.4 us (38%)
  Pallas kernels  22.4 us (14%)
  other arithmetic  3.83 us (2%)
  matrix products  3.38 us (2%)
    ppermute x32, waiting for transfers between devices, shift(): return lax.ppermute(a, ('dp', 'et'), plane_perm(first, step))  50 us
    ppermute x32, starting transfers between devices, shift(): return lax.ppermute(a, ('dp', 'et'), plane_perm(first, step))  44 us
    pallas_call x2, Pallas kernels, ffn(): pl.pallas_call(ffn_body, in_specs=[pl.BlockSpec(memory_space=pltpu.SMEM)]...  22.4 us
    ppermute x2, waiting for transfers between devices, on_device(): arrived.append(lax.ppermute(out, ('expert', 'et'), pairs))  9.48 us
    ppermute x2, waiting for transfers between devices, on_device(): back = lax.ppermute(done, ('expert', 'et'), [(b, a_) for a_, b in pairs])  7.01 us
    ppermute x2, starting transfers between devices, on_device(): arrived.append(lax.ppermute(out, ('expert', 'et'), pairs))  5.95 us
    ppermute x5, starting transfers between devices, swap(): return lax.ppermute(a, 'et', [(0, 1), (1, 0)])  5.59 us
    ppermute x2, starting transfers between devices, on_device(): back = lax.ppermute(done, ('expert', 'et'), [(b, a_) for a_, b in pairs])  3.9 us
  transfers between devices with their start and end apart: 41, of which 16 were waited for; matrix products, arithmetic and copies ran while one was open for 4% of the time, Pallas kernels for 14%

profile of v1, /device:TPU:1, one launch (start us, length us, event | category | flops | bytes accessed | tf_op | source)
XLA Modules:
  0.0 157.7 jit_solution(15568782543891879828)
XLA Ops:
  3.6 5.9 %collective-permute-start.1 = (bf16[40,3072]{1,0:T(8,128)(2,1)S(1)}, bf16[40,3072]{1,0:T(8,128)(2,1)S(1)}, u32[]{:S(2)}, u32[]{:S(2)}) collective-permute-start(bf16[40,3072]{1,0:T(8,128)(2,1)S(1)} %pad_maximum_fusion.4), channel_id=1, source_target_pairs={{0,0},{2,2},{4,4},{6,6},{1,7},{3,1},{5,3},{7,5},{8,8},{10,10},{12,... | collective-permute-start | bytes 737288 | tf_op jit(solution)/shard_map/ppermute | solution.py:170
  9.5 3.1 %collective-permute-done.1 = bf16[40,3072]{1,0:T(8,128)(2,1)S(1)} collective-permute-done((bf16[40,3072]{1,0:T(8,128)(2,1)S(1)}, bf16[40,3072]{1,0:T(8,128)(2,1)S(1)}, u32[]{:S(2)}, u32[]{:S(2)}) %collective-permute-start.1) | collective-permute-done | bytes 245792 | tf_op jit(solution)/shard_map/ppermute | solution.py:170
  16.5 2.4 %collective-permute-done.2 = bf16[40,3072]{1,0:T(8,128)(2,1)S(1)} collective-permute-done((bf16[40,3072]{1,0:T(8,128)(2,1)S(1)}, bf16[40,3072]{1,0:T(8,128)(2,1)S(1)}, u32[]{:S(2)}, u32[]{:S(2)}) %collective-permute-start.2) | collective-permute-done | bytes 245792 | tf_op jit(solution)/shard_map/ppermute | solution.py:25
  19.1 2.6 %collective-permute-start.5 = (bf16[40,1536]{1,0:T(8,128)(2,1)S(1)}, bf16[40,1536]{1,0:T(8,128)(2,1)S(1)}, u32[]{:S(2)}, u32[]{:S(2)}) collective-permute-start(bf16[40,1536]{1,0:T(8,128)(2,1)S(1)} %slice.148), channel_id=1, source_target_pairs={{0,24},{1,97},{8,0},{9,105},{16,8},{17,113},{24,16},{25,121},{32,5... | collective-permute-start | bytes 368648 | tf_op jit(solution)/shard_map/ppermute | solution.py:25
  21.9 3.6 %collective-permute-done.4 = bf16[40,1536]{1,0:T(8,128)(2,1)S(1)} collective-permute-done((bf16[40,1536]{1,0:T(8,128)(2,1)S(1)}, bf16[40,1536]{1,0:T(8,128)(2,1)S(1)}, u32[]{:S(2)}, u32[]{:S(2)}) %collective-permute-start.4) | collective-permute-done | bytes 122912 | tf_op jit(solution)/shard_map/ppermute | solution.py:25
  28.5 6.4 %collective-permute-done.22 = bf16[40,3072]{1,0:T(8,128)(2,1)S(1)} collective-permute-done((bf16[40,3072]{1,0:T(8,128)(2,1)S(1)}, bf16[40,3072]{1,0:T(8,128)(2,1)S(1)}, u32[]{:S(2)}, u32[]{:S(2)}) %collective-permute-start.22) | collective-permute-done | bytes 245792 | tf_op jit(solution)/shard_map/ppermute | solution.py:170
  34.8 3.0 %collective-permute-start.24 = (bf16[40,3072]{1,0:T(8,128)(2,1)S(1)}, bf16[40,3072]{1,0:T(8,128)(2,1)S(1)}, u32[]{:S(2)}, u32[]{:S(2)}) collective-permute-start(bf16[40,3072]{1,0:T(8,128)(2,1)S(1)} %collective-permute-done.22), channel_id=1, source_target_pairs={{0,24},{1,97},{8,0},{9,105},{16,8},{17,113},{24,16},{25,121},{32,5... | collective-permute-start | bytes 737288 | tf_op jit(solution)/shard_map/ppermute | solution.py:25
  37.8 3.6 %collective-permute-done.23 = bf16[40,3072]{1,0:T(8,128)(2,1)S(1)} collective-permute-done((bf16[40,3072]{1,0:T(8,128)(2,1)S(1)}, bf16[40,3072]{1,0:T(8,128)(2,1)S(1)}, u32[]{:S(2)}, u32[]{:S(2)}) %collective-permute-start.23) | collective-permute-done | bytes 245792 | tf_op jit(solution)/shard_map/ppermute | solution.py:25
  41.5 2.7 %collective-permute-start.26 = (bf16[40,1536]{1,0:T(8,128)(2,1)S(1)}, bf16[40,1536]{1,0:T(8,128)(2,1)S(1)}, u32[]{:S(2)}, u32[]{:S(2)}) collective-permute-start(bf16[40,1536]{1,0:T(8,128)(2,1)S(1)} %slice.159), channel_id=1, source_target_pairs={{0,24},{1,97},{8,0},{9,105},{16,8},{17,113},{24,16},{25,121},{32,5... | collective-permute-start | bytes 368648 | tf_op jit(solution)/shard_map/ppermute | solution.py:25
  47.9 3.0 %collective-permute-start.28 = (bf16[160,3072]{1,0:T(8,128)(2,1)S(1)}, bf16[160,3072]{1,0:T(8,128)(2,1)S(1)}, u32[]{:S(2)}, u32[]{:S(2)}) collective-permute-start(bf16[160,3072]{1,0:T(8,128)(2,1)S(1)} %maximum_maximum_fusion.1.own), channel_id=1, source_target_pairs={{0,96},{1,25},{8,104},{9,1},{16,112},{17,9},{24,120},{25,17},{32,0... | collective-permute-start | bytes 2949128 | tf_op jit(solution)/shard_map/ppermute | solution.py:25
  51.0 11.6 %collective-permute-done.27.left = bf16[160,3072]{1,0:T(8,128)(2,1)S(1)} collective-permute-done((bf16[160,3072]{1,0:T(8,128)(2,1)S(1)}, bf16[160,3072]{1,0:T(8,128)(2,1)S(1)}, u32[]{:S(2)}, u32[]{:S(2)}) %collective-permute-start.27) | collective-permute-done | bytes 983072 | tf_op jit(solution)/shard_map/ppermute | solution.py:25
  62.6 2.8 %collective-permute-start.9 = (bf16[160,1536]{1,0:T(8,128)(2,1)S(1)}, bf16[160,1536]{1,0:T(8,128)(2,1)S(1)}, u32[]{:S(2)}, u32[]{:S(2)}) collective-permute-start(bf16[160,1536]{1,0:T(8,128)(2,1)S(1)} %slice.150), channel_id=1, source_target_pairs={{0,96},{1,25},{8,104},{9,1},{16,112},{17,9},{24,120},{25,17},{32,0... | collective-permute-start | bytes 1474568 | tf_op jit(solution)/shard_map/ppermute | solution.py:25
  65.6 2.6 %collective-permute-start.30 = (bf16[160,1536]{1,0:T(8,128)(2,1)S(1)}, bf16[160,1536]{1,0:T(8,128)(2,1)S(1)}, u32[]{:S(2)}, u32[]{:S(2)}) collective-permute-start(bf16[160,1536]{1,0:T(8,128)(2,1)S(1)} %slice.161), channel_id=1, source_target_pairs={{0,96},{1,25},{8,104},{9,1},{16,112},{17,9},{24,120},{25,17},{32,0... | collective-permute-start | bytes 1474568 | tf_op jit(solution)/shard_map/ppermute | solution.py:25
  68.2 3.5 %collective-permute-done.8.far_a = bf16[160,1536]{1,0:T(8,128)(2,1)S(1)} collective-permute-done((bf16[160,1536]{1,0:T(8,128)(2,1)S(1)}, bf16[160,1536]{1,0:T(8,128)(2,1)S(1)}, u32[]{:S(2)}, u32[]{:S(2)}) %collective-permute-start.8) | collective-permute-done | bytes 491552 | tf_op jit(solution)/shard_map/ppermute | solution.py:25
  71.8 11.2 %ffn.2 = (bf16[160,3072]{1,0:T(8,128)(2,1)S(1)}, bf16[160,3072]{1,0:T(8,128)(2,1)S(1)}, bf16[160,3072]{1,0:T(8,128)(2,1)S(1)}, bf16[160,1536]{1,0:T(8,128)(2,1)S(1)}, bf16[160,1536]{1,0:T(8,128)(2,1)S(1)}) custom-call(s32[1]{0:T(128)} %bitcast.2.core, bf16[160,3072]{1,0:T(8,128)(2,1)S(1)} %maximum_maximum_fusion.own, bf16[160,3072]{1,0:T(8,128)(2,1)} %copy-done, ...), custom_call_target="tpu_custom_call" | custom-call | flops 6039797760 | bytes 17301504 | tf_op jit(solution)/shard_map/ffn/pallas_call | solution.py:119
  83.1 2.8 %collective-permute-start.15 = (bf16[160,1536]{1,0:T(8,128)(2,1)S(1)}, bf16[160,1536]{1,0:T(8,128)(2,1)S(1)}, u32[]{:S(2)}, u32[]{:S(2)}) collective-permute-start(bf16[160,1536]{1,0:T(8,128)(2,1)S(1)} %get-tuple-element.19), channel_id=1, source_target_pairs={{0,96},{1,25},{8,104},{9,1},{16,112},{17,9},{24,120},{25,17},{32,0... | collective-permute-start | bytes 1474568 | tf_op jit(solution)/shard_map/ppermute | solution.py:25
  86.0 11.2 %ffn.3 = (bf16[160,3072]{1,0:T(8,128)(2,1)S(1)}, bf16[160,3072]{1,0:T(8,128)(2,1)S(1)}, bf16[160,3072]{1,0:T(8,128)(2,1)S(1)}, bf16[160,1536]{1,0:T(8,128)(2,1)S(1)}, bf16[160,1536]{1,0:T(8,128)(2,1)S(1)}) custom-call(s32[1]{0:T(128)} %bitcast.2.core, bf16[160,3072]{1,0:T(8,128)(2,1)S(1)} %maximum_maximum_fusion.1.own, bf16[160,3072]{1,0:T(8,128)(2,1)} %copy-done.2, ...), custom_call_target="tpu_custom_call" | custom-call | flops 6039797760 | bytes 17301504 | tf_op jit(solution)/shard_map/ffn/pallas_call | solution.py:119
  97.3 2.7 %collective-permute-start.33 = (bf16[160,1536]{1,0:T(8,128)(2,1)S(1)}, bf16[160,1536]{1,0:T(8,128)(2,1)S(1)}, u32[]{:S(2)}, u32[]{:S(2)}) collective-permute-start(bf16[160,1536]{1,0:T(8,128)(2,1)S(1)} %get-tuple-element.24), channel_id=1, source_target_pairs={{0,96},{1,25},{8,104},{9,1},{16,112},{17,9},{24,120},{25,17},{32,0... | collective-permute-start | bytes 1474568 | tf_op jit(solution)/shard_map/ppermute | solution.py:25
  100.6 2.7 %collective-permute-start.16 = (bf16[160,3072]{1,0:T(8,128)(2,1)S(1)}, bf16[160,3072]{1,0:T(8,128)(2,1)S(1)}, u32[]{:S(2)}, u32[]{:S(2)}) collective-permute-start(bf16[160,3072]{1,0:T(8,128)(2,1)S(1)} %pad_maximum_fusion.1), channel_id=1, source_target_pairs={{0,96},{1,25},{8,104},{9,1},{16,112},{17,9},{24,120},{25,17},{32,0... | collective-permute-start | bytes 2949128 | tf_op jit(solution)/shard_map/ppermute | solution.py:25
  103.4 3.1 %collective-permute-done.31 = bf16[160,1536]{1,0:T(8,128)(2,1)S(1)} collective-permute-done((bf16[160,1536]{1,0:T(8,128)(2,1)S(1)}, bf16[160,1536]{1,0:T(8,128)(2,1)S(1)}, u32[]{:S(2)}, u32[]{:S(2)}) %collective-permute-start.31) | collective-permute-done | bytes 491552 | tf_op jit(solution)/shard_map/ppermute | solution.py:25
  107.0 2.7 %collective-permute-start.34 = (bf16[160,3072]{1,0:T(8,128)(2,1)S(1)}, bf16[160,3072]{1,0:T(8,128)(2,1)S(1)}, u32[]{:S(2)}, u32[]{:S(2)}) collective-permute-start(bf16[160,3072]{1,0:T(8,128)(2,1)S(1)} %pad_maximum_fusion.3), channel_id=1, source_target_pairs={{0,96},{1,25},{8,104},{9,1},{16,112},{17,9},{24,120},{25,17},{32,0... | collective-permute-start | bytes 2949128 | tf_op jit(solution)/shard_map/ppermute | solution.py:25
  109.7 7.3 %collective-permute-done.14 = bf16[160,3072]{1,0:T(8,128)(2,1)S(1)} collective-permute-done((bf16[160,3072]{1,0:T(8,128)(2,1)S(1)}, bf16[160,3072]{1,0:T(8,128)(2,1)S(1)}, u32[]{:S(2)}, u32[]{:S(2)}) %collective-permute-start.14) | collective-permute-done | bytes 983072 | tf_op jit(solution)/shard_map/ppermute | solution.py:25
  117.8 2.7 %collective-permute-start.19 = (bf16[40,1536]{1,0:T(8,128)(2,1)S(1)}, bf16[40,1536]{1,0:T(8,128)(2,1)S(1)}, u32[]{:S(2)}, u32[]{:S(2)}) collective-permute-start(bf16[40,1536]{1,0:T(8,128)(2,1)S(1)} %get-tuple-element.32), channel_id=1, source_target_pairs={{0,24},{1,97},{8,0},{9,105},{16,8},{17,113},{24,16},{25,121},{32,5... | collective-permute-start | bytes 368648 | tf_op jit(solution)/shard_map/ppermute | solution.py:25
  120.5 8.4 %collective-permute-done.32 = bf16[160,3072]{1,0:T(8,128)(2,1)S(1)} collective-permute-done((bf16[160,3072]{1,0:T(8,128)(2,1)S(1)}, bf16[160,3072]{1,0:T(8,128)(2,1)S(1)}, u32[]{:S(2)}, u32[]{:S(2)}) %collective-permute-start.32) | collective-permute-done | bytes 983072 | tf_op jit(solution)/shard_map/ppermute | solution.py:25
  129.4 2.7 %collective-permute-start.37 = (bf16[40,1536]{1,0:T(8,128)(2,1)S(1)}, bf16[40,1536]{1,0:T(8,128)(2,1)S(1)}, u32[]{:S(2)}, u32[]{:S(2)}) collective-permute-start(bf16[40,1536]{1,0:T(8,128)(2,1)S(1)} %get-tuple-element.38), channel_id=1, source_target_pairs={{0,24},{1,97},{8,0},{9,105},{16,8},{17,113},{24,16},{25,121},{32,5... | collective-permute-start | bytes 368648 | tf_op jit(solution)/shard_map/ppermute | solution.py:25
  132.3 2.1 %collective-permute-done.35 = bf16[40,1536]{1,0:T(8,128)(2,1)S(1)} collective-permute-done((bf16[40,1536]{1,0:T(8,128)(2,1)S(1)}, bf16[40,1536]{1,0:T(8,128)(2,1)S(1)}, u32[]{:S(2)}, u32[]{:S(2)}) %collective-permute-start.35) | collective-permute-done | bytes 122912 | tf_op jit(solution)/shard_map/ppermute | solution.py:25
  134.6 2.7 %collective-permute-start.38 = (bf16[40,3072]{1,0:T(8,128)(2,1)S(1)}, bf16[40,3072]{1,0:T(8,128)(2,1)S(1)}, u32[]{:S(2)}, u32[]{:S(2)}) collective-permute-start(bf16[40,3072]{1,0:T(8,128)(2,1)S(1)} %pad_maximum_fusion.9), channel_id=1, source_target_pairs={{0,24},{1,97},{8,0},{9,105},{16,8},{17,113},{24,16},{25,121},{32,5... | collective-permute-start | bytes 737288 | tf_op jit(solution)/shard_map/ppermute | solution.py:25
  138.8 2.6 %collective-permute-done.36 = bf16[40,3072]{1,0:T(8,128)(2,1)S(1)} collective-permute-done((bf16[40,3072]{1,0:T(8,128)(2,1)S(1)}, bf16[40,3072]{1,0:T(8,128)(2,1)S(1)}, u32[]{:S(2)}, u32[]{:S(2)}) %collective-permute-start.36) | collective-permute-done | bytes 245792 | tf_op jit(solution)/shard_map/ppermute | solution.py:25
  141.6 2.0 %collective-permute-start.39 = (bf16[40,3072]{1,0:T(8,128)(2,1)S(1)}, bf16[40,3072]{1,0:T(8,128)(2,1)S(1)}, u32[]{:S(2)}, u32[]{:S(2)}) collective-permute-start(bf16[40,3072]{1,0:T(8,128)(2,1)S(1)} %add_convert_fusion.6), channel_id=1, source_target_pairs={{4,0},{6,2},{0,4},{2,6},{3,1},{5,3},{7,5},{1,7},{12,8},{14,10},{8,... | collective-permute-start | bytes 737288 | tf_op jit(solution)/shard_map/ppermute | solution.py:179
  143.6 1.9 %collective-permute-start.21 = (bf16[40,3072]{1,0:T(8,128)(2,1)S(1)}, bf16[40,3072]{1,0:T(8,128)(2,1)S(1)}, u32[]{:S(2)}, u32[]{:S(2)}) collective-permute-start(bf16[40,3072]{1,0:T(8,128)(2,1)S(1)} %add_convert_fusion.7), channel_id=1, source_target_pairs={{0,0},{2,2},{4,4},{6,6},{7,1},{1,3},{3,5},{5,7},{8,8},{10,10},{12,... | collective-permute-start | bytes 737288 | tf_op jit(solution)/shard_map/ppermute | solution.py:179
  147.3 5.6 %collective-permute-done.21 = bf16[40,3072]{1,0:T(8,128)(2,1)S(1)} collective-permute-done((bf16[40,3072]{1,0:T(8,128)(2,1)S(1)}, bf16[40,3072]{1,0:T(8,128)(2,1)S(1)}, u32[]{:S(2)}, u32[]{:S(2)}) %collective-permute-start.21) | collective-permute-done | bytes 245792 | tf_op jit(solution)/shard_map/ppermute | solution.py:179
  153.3 2.6 %collective-permute-start.40 = (bf16[64,1536]{1,0:T(8,128)(2,1)S(1)}, bf16[64,1536]{1,0:T(8,128)(2,1)S(1)}, u32[]{:S(2)}, u32[]{:S(2)}) collective-permute-start(bf16[64,1536]{1,0:T(8,128)(2,1)S(1)} %slice.189), channel_id=1, source_target_pairs={{0,1},{1,0},{2,3},{3,2},{4,5},{5,4},{6,7},{7,6},{8,9},{9,8},{10,11... | collective-permute-start | bytes 589832 | tf_op jit(solution)/shard_map/ppermute | solution.py:29
  (124 shorter events, 23.4 us)
Async XLA Ops:
  3.6 9.0 %collective-permute-start.1 = (bf16[40,3072]{1,0:T(8,128)(2,1)S(1)}, bf16[40,3072]{1,0:T(8,128)(2,1)S(1)}, u32[]{:S(2)}, u32[]{:S(2)}) collective-permute-start(bf16[40,3072]{1,0:T(8,128)(2,1)S(1)} %pad_maximum_fusion.4), channel_id=1, source_target_pairs={{0,0},{2,2},{4,4},{6,6},{1,7},{3,1},{5,3},{7,5},{8,8},{10,10},{12,... | collective-permute-start | bytes 737288 | tf_op jit(solution)/shard_map/ppermute | solution.py:170
  12.6 6.3 %collective-permute-start.2 = (bf16[40,3072]{1,0:T(8,128)(2,1)S(1)}, bf16[40,3072]{1,0:T(8,128)(2,1)S(1)}, u32[]{:S(2)}, u32[]{:S(2)}) collective-permute-start(bf16[40,3072]{1,0:T(8,128)(2,1)S(1)} %collective-permute-done.1), channel_id=1, source_target_pairs={{0,8},{1,33},{8,16},{9,41},{16,24},{17,49},{24,0},{25,57},{32,40},... | collective-permute-start | bytes 737288 | tf_op jit(solution)/shard_map/ppermute | solution.py:25
  18.9 6.6 %collective-permute-start.4 = (bf16[40,1536]{1,0:T(8,128)(2,1)S(1)}, bf16[40,1536]{1,0:T(8,128)(2,1)S(1)}, u32[]{:S(2)}, u32[]{:S(2)}) collective-permute-start(bf16[40,1536]{1,0:T(8,128)(2,1)S(1)} %slice.147), channel_id=1, source_target_pairs={{0,8},{1,33},{8,16},{9,41},{16,24},{17,49},{24,0},{25,57},{32,40},... | collective-permute-start | bytes 368648 | tf_op jit(solution)/shard_map/ppermute | solution.py:25
  19.1 6.4 %collective-permute-start.5 = (bf16[40,1536]{1,0:T(8,128)(2,1)S(1)}, bf16[40,1536]{1,0:T(8,128)(2,1)S(1)}, u32[]{:S(2)}, u32[]{:S(2)}) collective-permute-start(bf16[40,1536]{1,0:T(8,128)(2,1)S(1)} %slice.148), channel_id=1, source_target_pairs={{0,24},{1,97},{8,0},{9,105},{16,8},{17,113},{24,16},{25,121},{32,5... | collective-permute-start | bytes 368648 | tf_op jit(solution)/shard_map/ppermute | solution.py:25
  25.6 22.2 %collective-permute-start.6 = (bf16[160,3072]{1,0:T(8,128)(2,1)S(1)}, bf16[160,3072]{1,0:T(8,128)(2,1)S(1)}, u32[]{:S(2)}, u32[]{:S(2)}) collective-permute-start(bf16[160,3072]{1,0:T(8,128)(2,1)S(1)} %maximum_maximum_fusion.own), channel_id=1, source_target_pairs={{0,32},{1,9},{8,40},{9,17},{16,48},{17,25},{24,56},{25,1},{32,64},... | collective-permute-start | bytes 2949128 | tf_op jit(solution)/shard_map/ppermute | solution.py:25
  26.9 21.0 %collective-permute-start.7 = (bf16[160,3072]{1,0:T(8,128)(2,1)S(1)}, bf16[160,3072]{1,0:T(8,128)(2,1)S(1)}, u32[]{:S(2)}, u32[]{:S(2)}) collective-permute-start(bf16[160,3072]{1,0:T(8,128)(2,1)S(1)} %maximum_maximum_fusion.own), channel_id=1, source_target_pairs={{0,96},{1,25},{8,104},{9,1},{16,112},{17,9},{24,120},{25,17},{32,0... | collective-permute-start | bytes 2949128 | tf_op jit(solution)/shard_map/ppermute | solution.py:25
  28.4 6.4 %collective-permute-start.22 = (bf16[40,3072]{1,0:T(8,128)(2,1)S(1)}, bf16[40,3072]{1,0:T(8,128)(2,1)S(1)}, u32[]{:S(2)}, u32[]{:S(2)}) collective-permute-start(bf16[40,3072]{1,0:T(8,128)(2,1)S(1)} %pad_maximum_fusion.7), channel_id=1, source_target_pairs={{0,4},{2,6},{4,0},{6,2},{1,3},{3,5},{5,7},{7,1},{8,12},{10,14},{12... | collective-permute-start | bytes 737288 | tf_op jit(solution)/shard_map/ppermute | solution.py:170
  34.8 6.5 %collective-permute-start.23 = (bf16[40,3072]{1,0:T(8,128)(2,1)S(1)}, bf16[40,3072]{1,0:T(8,128)(2,1)S(1)}, u32[]{:S(2)}, u32[]{:S(2)}) collective-permute-start(bf16[40,3072]{1,0:T(8,128)(2,1)S(1)} %collective-permute-done.22), channel_id=1, source_target_pairs={{0,8},{1,33},{8,16},{9,41},{16,24},{17,49},{24,0},{25,57},{32,40},... | collective-permute-start | bytes 737288 | tf_op jit(solution)/shard_map/ppermute | solution.py:25
  34.8 6.6 %collective-permute-start.24 = (bf16[40,3072]{1,0:T(8,128)(2,1)S(1)}, bf16[40,3072]{1,0:T(8,128)(2,1)S(1)}, u32[]{:S(2)}, u32[]{:S(2)}) collective-permute-start(bf16[40,3072]{1,0:T(8,128)(2,1)S(1)} %collective-permute-done.22), channel_id=1, source_target_pairs={{0,24},{1,97},{8,0},{9,105},{16,8},{17,113},{24,16},{25,121},{32,5... | collective-permute-start | bytes 737288 | tf_op jit(solution)/shard_map/ppermute | solution.py:25
  44.2 21.2 %collective-permute-start.10 = (bf16[3072,256]{1,0:T(8,128)(2,1)S(1)}, bf16[3072,256]{1,0:T(8,128)(2,1)}, u32[]{:S(2)}, u32[]{:S(2)}) collective-permute-start(bf16[3072,256]{1,0:T(8,128)(2,1)S(1)} %bitcast.38), channel_id=1, source_target_pairs={{0,1},{1,0},{2,3},{3,2},{4,5},{5,4},{6,7},{7,6},{8,9},{9,8},{10,11... | collective-permute-start | bytes 4718600 | tf_op jit(solution)/shard_map/ppermute | solution.py:29
  46.7 18.9 %collective-permute-start.11 = (bf16[3072,256]{1,0:T(8,128)(2,1)S(1)}, bf16[3072,256]{1,0:T(8,128)(2,1)S(1)}, u32[]{:S(2)}, u32[]{:S(2)}) collective-permute-start(bf16[3072,256]{1,0:T(8,128)(2,1)S(1)} %bitcast.41), channel_id=1, source_target_pairs={{0,1},{1,0},{2,3},{3,2},{4,5},{5,4},{6,7},{7,6},{8,9},{9,8},{10,11... | collective-permute-start | bytes 4718600 | tf_op jit(solution)/shard_map/ppermute | solution.py:29
  47.6 20.7 %collective-permute-start.12 = (bf16[512,1536]{1,0:T(8,128)(2,1)S(1)}, bf16[512,1536]{1,0:T(8,128)(2,1)S(1)}, u32[]{:S(2)}, u32[]{:S(2)}) collective-permute-start(bf16[512,1536]{1,0:T(8,128)(2,1)S(1)} %bitcast.44), channel_id=1, source_target_pairs={{0,1},{1,0},{2,3},{3,2},{4,5},{5,4},{6,7},{7,6},{8,9},{9,8},{10,11... | collective-permute-start | bytes 4718600 | tf_op jit(solution)/shard_map/ppermute | solution.py:29
  47.8 14.8 %collective-permute-start.27 = (bf16[160,3072]{1,0:T(8,128)(2,1)S(1)}, bf16[160,3072]{1,0:T(8,128)(2,1)S(1)}, u32[]{:S(2)}, u32[]{:S(2)}) collective-permute-start(bf16[160,3072]{1,0:T(8,128)(2,1)S(1)} %maximum_maximum_fusion.1.own), channel_id=1, source_target_pairs={{0,32},{1,9},{8,40},{9,17},{16,48},{17,25},{24,56},{25,1},{32,64},... | collective-permute-start | bytes 2949128 | tf_op jit(solution)/shard_map/ppermute | solution.py:25
  47.9 14.7 %collective-permute-start.28 = (bf16[160,3072]{1,0:T(8,128)(2,1)S(1)}, bf16[160,3072]{1,0:T(8,128)(2,1)S(1)}, u32[]{:S(2)}, u32[]{:S(2)}) collective-permute-start(bf16[160,3072]{1,0:T(8,128)(2,1)S(1)} %maximum_maximum_fusion.1.own), channel_id=1, source_target_pairs={{0,96},{1,25},{8,104},{9,1},{16,112},{17,9},{24,120},{25,17},{32,0... | collective-permute-start | bytes 2949128 | tf_op jit(solution)/shard_map/ppermute | solution.py:25
  62.6 9.2 %collective-permute-start.8 = (bf16[160,1536]{1,0:T(8,128)(2,1)S(1)}, bf16[160,1536]{1,0:T(8,128)(2,1)S(1)}, u32[]{:S(2)}, u32[]{:S(2)}) collective-permute-start(bf16[160,1536]{1,0:T(8,128)(2,1)S(1)} %slice.149), channel_id=1, source_target_pairs={{0,32},{1,9},{8,40},{9,17},{16,48},{17,25},{24,56},{25,1},{32,64},... | collective-permute-start | bytes 1474568 | tf_op jit(solution)/shard_map/ppermute | solution.py:25
  62.6 9.2 %collective-permute-start.9 = (bf16[160,1536]{1,0:T(8,128)(2,1)S(1)}, bf16[160,1536]{1,0:T(8,128)(2,1)S(1)}, u32[]{:S(2)}, u32[]{:S(2)}) collective-permute-start(bf16[160,1536]{1,0:T(8,128)(2,1)S(1)} %slice.150), channel_id=1, source_target_pairs={{0,96},{1,25},{8,104},{9,1},{16,112},{17,9},{24,120},{25,17},{32,0... | collective-permute-start | bytes 1474568 | tf_op jit(solution)/shard_map/ppermute | solution.py:25
  65.5 20.5 %collective-permute-start.29 = (bf16[160,1536]{1,0:T(8,128)(2,1)S(1)}, bf16[160,1536]{1,0:T(8,128)(2,1)S(1)}, u32[]{:S(2)}, u32[]{:S(2)}) collective-permute-start(bf16[160,1536]{1,0:T(8,128)(2,1)S(1)} %slice.160), channel_id=1, source_target_pairs={{0,32},{1,9},{8,40},{9,17},{16,48},{17,25},{24,56},{25,1},{32,64},... | collective-permute-start | bytes 1474568 | tf_op jit(solution)/shard_map/ppermute | solution.py:25
  65.6 20.4 %collective-permute-start.30 = (bf16[160,1536]{1,0:T(8,128)(2,1)S(1)}, bf16[160,1536]{1,0:T(8,128)(2,1)S(1)}, u32[]{:S(2)}, u32[]{:S(2)}) collective-permute-start(bf16[160,1536]{1,0:T(8,128)(2,1)S(1)} %slice.161), channel_id=1, source_target_pairs={{0,96},{1,25},{8,104},{9,1},{16,112},{17,9},{24,120},{25,17},{32,0... | collective-permute-start | bytes 1474568 | tf_op jit(solution)/shard_map/ppermute | solution.py:25
  83.0 17.1 %collective-permute-start.13 = (bf16[160,1536]{1,0:T(8,128)(2,1)S(1)}, bf16[160,1536]{1,0:T(8,128)(2,1)S(1)}, u32[]{:S(2)}, u32[]{:S(2)}) collective-permute-start(bf16[160,1536]{1,0:T(8,128)(2,1)S(1)} %get-tuple-element.17), channel_id=1, source_target_pairs={{0,32},{1,9},{8,40},{9,17},{16,48},{17,25},{24,56},{25,1},{32,64},... | collective-permute-start | bytes 1474568 | tf_op jit(solution)/shard_map/ppermute | solution.py:25
  83.1 17.3 %collective-permute-start.15 = (bf16[160,1536]{1,0:T(8,128)(2,1)S(1)}, bf16[160,1536]{1,0:T(8,128)(2,1)S(1)}, u32[]{:S(2)}, u32[]{:S(2)}) collective-permute-start(bf16[160,1536]{1,0:T(8,128)(2,1)S(1)} %get-tuple-element.19), channel_id=1, source_target_pairs={{0,96},{1,25},{8,104},{9,1},{16,112},{17,9},{24,120},{25,17},{32,0... | collective-permute-start | bytes 1474568 | tf_op jit(solution)/shard_map/ppermute | solution.py:25
  97.2 9.3 %collective-permute-start.31 = (bf16[160,1536]{1,0:T(8,128)(2,1)S(1)}, bf16[160,1536]{1,0:T(8,128)(2,1)S(1)}, u32[]{:S(2)}, u32[]{:S(2)}) collective-permute-start(bf16[160,1536]{1,0:T(8,128)(2,1)S(1)} %get-tuple-element.22), channel_id=1, source_target_pairs={{0,32},{1,9},{8,40},{9,17},{16,48},{17,25},{24,56},{25,1},{32,64},... | collective-permute-start | bytes 1474568 | tf_op jit(solution)/shard_map/ppermute | solution.py:25
  97.3 9.4 %collective-permute-start.33 = (bf16[160,1536]{1,0:T(8,128)(2,1)S(1)}, bf16[160,1536]{1,0:T(8,128)(2,1)S(1)}, u32[]{:S(2)}, u32[]{:S(2)}) collective-permute-start(bf16[160,1536]{1,0:T(8,128)(2,1)S(1)} %get-tuple-element.24), channel_id=1, source_target_pairs={{0,96},{1,25},{8,104},{9,1},{16,112},{17,9},{24,120},{25,17},{32,0... | collective-permute-start | bytes 1474568 | tf_op jit(solution)/shard_map/ppermute | solution.py:25
  100.3 16.7 %collective-permute-start.14 = (bf16[160,3072]{1,0:T(8,128)(2,1)S(1)}, bf16[160,3072]{1,0:T(8,128)(2,1)S(1)}, u32[]{:S(2)}, u32[]{:S(2)}) collective-permute-start(bf16[160,3072]{1,0:T(8,128)(2,1)S(1)} %pad_maximum_fusion), channel_id=1, source_target_pairs={{0,32},{1,9},{8,40},{9,17},{16,48},{17,25},{24,56},{25,1},{32,64},... | collective-permute-start | bytes 2949128 | tf_op jit(solution)/shard_map/ppermute | solution.py:25
  100.6 16.3 %collective-permute-start.16 = (bf16[160,3072]{1,0:T(8,128)(2,1)S(1)}, bf16[160,3072]{1,0:T(8,128)(2,1)S(1)}, u32[]{:S(2)}, u32[]{:S(2)}) collective-permute-start(bf16[160,3072]{1,0:T(8,128)(2,1)S(1)} %pad_maximum_fusion.1), channel_id=1, source_target_pairs={{0,96},{1,25},{8,104},{9,1},{16,112},{17,9},{24,120},{25,17},{32,0... | collective-permute-start | bytes 2949128 | tf_op jit(solution)/shard_map/ppermute | solution.py:25
  106.7 22.2 %collective-permute-start.32 = (bf16[160,3072]{1,0:T(8,128)(2,1)S(1)}, bf16[160,3072]{1,0:T(8,128)(2,1)S(1)}, u32[]{:S(2)}, u32[]{:S(2)}) collective-permute-start(bf16[160,3072]{1,0:T(8,128)(2,1)S(1)} %pad_maximum_fusion.2), channel_id=1, source_target_pairs={{0,32},{1,9},{8,40},{9,17},{16,48},{17,25},{24,56},{25,1},{32,64},... | collective-permute-start | bytes 2949128 | tf_op jit(solution)/shard_map/ppermute | solution.py:25
  107.0 21.8 %collective-permute-start.34 = (bf16[160,3072]{1,0:T(8,128)(2,1)S(1)}, bf16[160,3072]{1,0:T(8,128)(2,1)S(1)}, u32[]{:S(2)}, u32[]{:S(2)}) collective-permute-start(bf16[160,3072]{1,0:T(8,128)(2,1)S(1)} %pad_maximum_fusion.3), channel_id=1, source_target_pairs={{0,96},{1,25},{8,104},{9,1},{16,112},{17,9},{24,120},{25,17},{32,0... | collective-permute-start | bytes 2949128 | tf_op jit(solution)/shard_map/ppermute | solution.py:25
  117.5 14.6 %collective-permute-start.17 = (bf16[40,1536]{1,0:T(8,128)(2,1)S(1)}, bf16[40,1536]{1,0:T(8,128)(2,1)S(1)}, u32[]{:S(2)}, u32[]{:S(2)}) collective-permute-start(bf16[40,1536]{1,0:T(8,128)(2,1)S(1)} %get-tuple-element.31), channel_id=1, source_target_pairs={{0,8},{1,33},{8,16},{9,41},{16,24},{17,49},{24,0},{25,57},{32,40},... | collective-permute-start | bytes 368648 | tf_op jit(solution)/shard_map/ppermute | solution.py:25
  117.8 14.3 %collective-permute-start.19 = (bf16[40,1536]{1,0:T(8,128)(2,1)S(1)}, bf16[40,1536]{1,0:T(8,128)(2,1)S(1)}, u32[]{:S(2)}, u32[]{:S(2)}) collective-permute-start(bf16[40,1536]{1,0:T(8,128)(2,1)S(1)} %get-tuple-element.32), channel_id=1, source_target_pairs={{0,24},{1,97},{8,0},{9,105},{16,8},{17,113},{24,16},{25,121},{32,5... | collective-permute-start | bytes 368648 | tf_op jit(solution)/shard_map/ppermute | solution.py:25
  132.2 11.3 %collective-permute-start.18 = (bf16[40,3072]{1,0:T(8,128)(2,1)S(1)}, bf16[40,3072]{1,0:T(8,128)(2,1)S(1)}, u32[]{:S(2)}, u32[]{:S(2)}) collective-permute-start(bf16[40,3072]{1,0:T(8,128)(2,1)S(1)} %pad_maximum_fusion.5), channel_id=1, source_target_pairs={{0,8},{1,33},{8,16},{9,41},{16,24},{17,49},{24,0},{25,57},{32,40},... | collective-permute-start | bytes 737288 | tf_op jit(solution)/shard_map/ppermute | solution.py:25
  134.5 7.0 %collective-permute-start.36 = (bf16[40,3072]{1,0:T(8,128)(2,1)S(1)}, bf16[40,3072]{1,0:T(8,128)(2,1)S(1)}, u32[]{:S(2)}, u32[]{:S(2)}) collective-permute-start(bf16[40,3072]{1,0:T(8,128)(2,1)S(1)} %pad_maximum_fusion.8), channel_id=1, source_target_pairs={{0,8},{1,33},{8,16},{9,41},{16,24},{17,49},{24,0},{25,57},{32,40},... | collective-permute-start | bytes 737288 | tf_op jit(solution)/shard_map/ppermute | solution.py:25
  134.6 6.9 %collective-permute-start.38 = (bf16[40,3072]{1,0:T(8,128)(2,1)S(1)}, bf16[40,3072]{1,0:T(8,128)(2,1)S(1)}, u32[]{:S(2)}, u32[]{:S(2)}) collective-permute-start(bf16[40,3072]{1,0:T(8,128)(2,1)S(1)} %pad_maximum_fusion.9), channel_id=1, source_target_pairs={{0,24},{1,97},{8,0},{9,105},{16,8},{17,113},{24,16},{25,121},{32,5... | collective-permute-start | bytes 737288 | tf_op jit(solution)/shard_map/ppermute | solution.py:25
  143.6 9.3 %collective-permute-start.21 = (bf16[40,3072]{1,0:T(8,128)(2,1)S(1)}, bf16[40,3072]{1,0:T(8,128)(2,1)S(1)}, u32[]{:S(2)}, u32[]{:S(2)}) collective-permute-start(bf16[40,3072]{1,0:T(8,128)(2,1)S(1)} %add_convert_fusion.7), channel_id=1, source_target_pairs={{0,0},{2,2},{4,4},{6,6},{7,1},{1,3},{3,5},{5,7},{8,8},{10,10},{12,... | collective-permute-start | bytes 737288 | tf_op jit(solution)/shard_map/ppermute | solution.py:179
  (20 other events, 263.4 us)

commit v2 on v1

v2 whole, which is shorter than its diff:
```python
import jax
import jax.numpy as jnp
from jax import lax
from jax.experimental import pallas as pl
from jax.experimental.pallas import tpu as pltpu
from jax.sharding import PartitionSpec as P

SIDE = 4
BF = jnp.bfloat16
F32 = jnp.float32
VMEM_MB = 16


def plane_perm(first, step):
    pairs = []
    for y in range(SIDE):
        for x in range(SIDE):
            for c in range(2):
                along_x = (c == 0) == first
                ty, tx = (y, (x + step) % SIDE) if along_x else ((y + step) % SIDE, x)
                pairs.append(((y * SIDE + x) * 2 + c, (ty * SIDE + tx) * 2 + c))
    return pairs


def shift(a, first, step):
    return lax.ppermute(a, ("dp", "et"), plane_perm(first, step))


def swap(a):
    return lax.ppermute(a, "et", [(0, 1), (1, 0)])


def tie(value, *after):
    return lax.optimization_barrier((value, *after))[0]


def both(plus, minus, first):
    return shift(plus, first, 1), shift(minus, first, -1)


def add(*terms):
    total = terms[0].astype(F32)
    for t in terms[1:]:
        total = total + t.astype(F32)
    return total.astype(BF)


def ffn_body(core, *refs):
    c = core[0]
    wg0, wg1, wu0, wu1, wd0, wd1 = refs[:6]
    hidden = refs[-1]
    n_arrays = (len(refs) - 7) // 2
    ins, outs = refs[6:6 + n_arrays], refs[6 + n_arrays:-1]
    d = 2 * wd0.shape[1]
    half = d // 2
    hid = wg0.shape[1]
    mine = pl.multiple_of(c * half, half)
    other = pl.multiple_of((1 - c) * half, half)
    mine_h = pl.multiple_of(c * hid, hid)
    other_h = pl.multiple_of((1 - c) * hid, hid)
    lo, hi = pl.ds(0, half), pl.ds(half, half)
    at = 0
    while at < n_arrays:
        if ins[at].shape[1] == d:
            a, b = ins[at][:, lo], ins[at][:, hi]
            halves = [(outs[at], lo), (outs[at], hi)]
            at += 1
        else:
            a, b = ins[at][...], ins[at + 1][...]
            halves = [(outs[at], lo), (outs[at + 1], lo)]
            at += 2
        for k, (wg, wu) in enumerate(((wg0, wu0), (wg1, wu1))):
            def proj(w):
                return jnp.dot(a, w[pl.ds(mine, half), :], preferred_element_type=F32) + jnp.dot(
                    b, w[pl.ds(other, half), :], preferred_element_type=F32
                )

            g = proj(wg)
            u = proj(wu)
            hidden[:, pl.ds(k * hid, hid)] = (g / (1.0 + jnp.exp(-g)) * u).astype(BF)
        h0, h1 = hidden[:, pl.ds(0, hid)], hidden[:, pl.ds(hid, hid)]
        for (out, cols), w, first, second in zip(halves, (wd0, wd1), (mine_h, 0), (other_h, hid)):
            p = jnp.dot(h0, w[pl.ds(first, hid), :], preferred_element_type=F32) + jnp.dot(
                h1, w[pl.ds(second, hid), :], preferred_element_type=F32
            )
            out[:, cols] = p.astype(BF)


def ffn(core, weights, arrays):
    n = arrays[0].shape[0]
    half = weights[4].shape[1]
    hid = weights[0].shape[1]
    rows = sum(a.size for a in arrays) // (2 * half)
    whole = pl.BlockSpec(memory_space=pltpu.VMEM)
    return pl.pallas_call(
        ffn_body,
        in_specs=[pl.BlockSpec(memory_space=pltpu.SMEM)] + [whole] * (6 + len(arrays)),
        out_specs=[whole] * len(arrays),
        out_shape=[jax.ShapeDtypeStruct(a.shape, BF) for a in arrays],
        scratch_shapes=[pltpu.VMEM((n, 2 * hid), BF)],
        compiler_params=pltpu.CompilerParams(vmem_limit_bytes=VMEM_MB * 1024 * 1024),
        cost_estimate=pl.CostEstimate(
            flops=2 * rows * half * 2 * hid * 6, bytes_accessed=8 * rows * half + 24 * half * hid,
            transcendentals=2 * rows * hid,
        ),
        name="ffn",
    )(core, *weights, *arrays)


def on_device(tokens, expert_ids, gate_scores, w_gate, w_up, w_down):
    tok_rows, half = tokens.shape
    n_expert = lax.axis_size("expert")
    capacity = max(2, 5 * tok_rows // (2 * n_expert))
    z = lax.axis_index("expert")
    c = lax.axis_index("et")
    core = c.astype(jnp.int32).reshape(1)

    other_tokens = swap(tokens)
    t = jnp.arange(tok_rows, dtype=jnp.int32)
    slots = jnp.arange(capacity, dtype=jnp.int32)
    before = (t[:, None] < t[None, :]).astype(F32)

    def choose(e):
        named = expert_ids == e
        mask = jnp.any(named, axis=1)
        rank = jnp.dot(mask.astype(F32)[None, :], before, preferred_element_type=F32)[0].astype(jnp.int32)
        pick = (slots[:, None] == rank[None, :]) & mask[None, :]
        return pick.astype(BF), jnp.sum(jnp.where(named, gate_scores, 0.0), axis=1)

    send = [
        [(s * 2, s * 2) for s in range(n_expert)] + [(s * 2 + 1, (s - 1) % n_expert * 2 + 1) for s in range(n_expert)],
        [(s * 2, (s + 2) % n_expert * 2) for s in range(n_expert)]
        + [(s * 2 + 1, (s + 1) % n_expert * 2 + 1) for s in range(n_expert)],
    ]
    picks = [choose((z - c) % n_expert), choose((z + 2 - c) % n_expert)]

    pick_all = jnp.concatenate([pick for pick, _ in picks], axis=0)
    outgoing = jnp.concatenate(
        [jnp.dot(pick_all, v, preferred_element_type=F32).astype(BF) for v in (tokens, other_tokens)], axis=1
    )

    def dispatch(k):
        return lax.ppermute(outgoing[k * capacity:(k + 1) * capacity], ("expert", "et"), send[k])

    def far_pair(left, right, first):
        return both(left[:, :half], right[:, half:], first)

    def fold(left, right, got_a, got_b):
        return (
            jnp.concatenate([left[:, :half], add(left[:, half:], got_b)], axis=1),
            jnp.concatenate([add(right[:, :half], got_a), right[:, half:]], axis=1),
        )

    weights = []
    for w in (w_down[0], w_up[0], w_gate[0]):
        weights = [w, swap(w)] + weights
    hid = w_gate.shape[2]
    down = weights[5]
    weights[5] = jnp.where(c == 0, down, jnp.concatenate([down[hid:], down[:hid]], axis=0))
    z0 = dispatch(0)
    z1 = dispatch(1)

    def spread(own):
        left, right, far = shift(own, True, 1), shift(own, True, -1), shift(own, True, 2)
        return jnp.concatenate([own, left, right, far], axis=0)

    def collect(sums):
        own, left, right, far = sums.reshape(SIDE, capacity, 2 * half)
        return add(own, shift(left, True, -1), shift(right, True, 1), shift(far, True, 2))

    line0 = spread(tie(z0, z1, *weights))
    line1 = spread(tie(z1, line0))
    left0, right0 = both(line0, line0, False)
    (p_own0,) = ffn(core, weights, (line0,))
    line1 = tie(line1, p_own0)
    left1, right1 = both(line1, line1, False)
    far_a0, far_b0 = far_pair(left0, right0, False)
    p_left0, p_right0 = ffn(core, weights, (left0, right0))
    (p_own1,) = ffn(core, weights, (tie(line1, p_left0),))
    far_a1, far_b1 = far_pair(tie(left1, p_own1), right1, False)
    p_left1, p_right1 = ffn(core, weights, (left1, right1))
    pf_a0, pf_b0 = ffn(core, weights, (tie(far_a0, p_left1), far_b0))
    got_a0, got_b0 = both(pf_a0, pf_b0, False)
    pf_a1, pf_b1 = ffn(core, weights, (tie(far_a1, pf_a0), far_b1))
    got_a1, got_b1 = both(pf_a1, pf_b1, False)
    sl0, sr0 = fold(p_left0, p_right0, got_a0, got_b0)
    from_l0, from_r0 = both(sr0, sl0, False)
    sl1, sr1 = fold(p_left1, p_right1, got_a1, got_b1)
    from_l1, from_r1 = both(sr1, sl1, False)
    done0 = collect(add(p_own0, from_l0, from_r0))
    done1 = collect(add(p_own1, from_l1, from_r1))
    back0 = lax.ppermute(done0, ("expert", "et"), [(b, a) for a, b in send[0]])
    back1 = lax.ppermute(tie(done1, back0), ("expert", "et"), [(b, a) for a, b in send[1]])

    total = jnp.zeros((tok_rows, 2 * half), F32)
    for back, (pick, score) in zip((back0, back1), picks):
        rows = lax.dot_general(pick, back, (((0,), (0,)), ((), ())), preferred_element_type=F32)
        total = total + rows * score[:, None]
    theirs = swap(total[:, half:].astype(BF))
    return (total[:, :half] + theirs.astype(F32)).astype(BF)


def solution(mesh):
    placed = (
        P(("dp", "expert"), "et"),
        P(("dp", "expert"), None),
        P(("dp", "expert"), None),
        P("expert", None, ("dp", "et")),
        P("expert", None, ("dp", "et")),
        P("expert", "dp", "et"),
    )
    return jax.shard_map(
        on_device, mesh=mesh, in_specs=placed, out_specs=P(("dp", "expert"), "et"), check_vma=False
    )
```

time: 158 us -> 138 us (0.87)
  starting transfers between devices: 59.4 us -> 50.4 us
  Pallas kernels: 22.4 us -> 14.3 us
  waiting for transfers between devices: 67.6 us -> 64.9 us
    pallas_call x2 -> x6, Pallas kernels: 22.4 us -> 14.3 us  [ffn(): pl.pallas_call(ffn_body, in_specs=[pl.BlockSpec(memory_space=pltpu.SMEM)]...]
    ppermute x32 -> x28, waiting for transfers between devices: 50 us -> 43.1 us  [shift(): return lax.ppermute(a, ('dp', 'et'), plane_perm(first, step))]
    ppermute x32 -> x28, starting transfers between devices: 44 us -> 38.1 us  [shift(): return lax.ppermute(a, ('dp', 'et'), plane_perm(first, step))]
    ppermute x5, waiting for transfers between devices: 1.08 us -> 6.84 us  [swap(): return lax.ppermute(a, 'et', [(0, 1), (1, 0)])]
    ppermute x5, starting transfers between devices: 5.59 us -> 2.02 us  [swap(): return lax.ppermute(a, 'et', [(0, 1), (1, 0)])]
  transfers between devices with their start and end apart: 41 -> 37, of which waited for: 16 -> 22; matrix products, arithmetic and copies ran while one was open for 4% -> 5% of each run, Pallas kernels for 14% -> 10%
where the time goes in v2:
time: 138 us
  waiting for transfers between devices  64.9 us (47%)
  starting transfers between devices  50.4 us (37%)
  Pallas kernels  14.3 us (10%)
  other arithmetic  4.02 us (3%)
  matrix products  2.21 us (2%)
  local copies, waits for them, and re-layouts  1.96 us (1%)
    ppermute x28, waiting for transfers between devices, shift(): return lax.ppermute(a, ('dp', 'et'), plane_perm(first, step))  43.1 us
    ppermute x28, starting transfers between devices, shift(): return lax.ppermute(a, ('dp', 'et'), plane_perm(first, step))  38.1 us
    pallas_call x6, Pallas kernels, ffn(): pl.pallas_call(ffn_body, in_specs=[pl.BlockSpec(memory_space=pltpu.SMEM)]...  14.3 us
    ppermute x5, waiting for transfers between devices, swap(): return lax.ppermute(a, 'et', [(0, 1), (1, 0)])  6.84 us
    ppermute x2, starting transfers between devices, dispatch(): lax.ppermute(outgoing[k * capacity:(k + 1) * capacity], ('expert', 'et'),...  5.83 us
    ppermute x1, waiting for transfers between devices, on_device(): lax.ppermute(tie(done1, back0), ('expert', 'et'), [(b, a) for a, b in sen...  5.75 us
    ppermute x1, waiting for transfers between devices, on_device(): back0 = lax.ppermute(done0, ('expert', 'et'), [(b, a) for a, b in send[0]])  5.5 us
    ppermute x2, waiting for transfers between devices, dispatch(): lax.ppermute(outgoing[k * capacity:(k + 1) * capacity], ('expert', 'et'),...  3.75 us
  transfers between devices with their start and end apart: 37, of which 22 were waited for; matrix products, arithmetic and copies ran while one was open for 5% of the time, Pallas kernels for 10%

profile of v2, /device:TPU:1, one launch (start us, length us, event | category | flops | bytes accessed | tf_op | source)
XLA Modules:
  0.0 138.3 jit_solution(9916977267773738918)
XLA Ops:
  4.1 5.4 %collective-permute-done.3 = bf16[64,1536]{1,0:T(8,128)(2,1)S(1)} collective-permute-done((bf16[64,1536]{1,0:T(8,128)(2,1)}, bf16[64,1536]{1,0:T(8,128)(2,1)S(1)}, u32[]{:S(2)}, u32[]{:S(2)}) %collective-permute-start.3) | collective-permute-done | bytes 196640 | tf_op jit(solution)/shard_map/ppermute | solution.py:30
  11.5 4.0 %collective-permute-start.4 = (bf16[40,3072]{1,0:T(8,128)(2,1)S(1)}, bf16[40,3072]{1,0:T(8,128)(2,1)S(1)}, u32[]{:S(2)}, u32[]{:S(2)}) collective-permute-start(bf16[40,3072]{1,0:T(8,128)(2,1)S(1)} %get-tuple-element.49), channel_id=1, source_target_pairs={{0,0},{2,2},{4,4},{6,6},{1,7},{3,1},{5,3},{7,5},{8,8},{10,10},{12,... | collective-permute-start | bytes 737288 | tf_op jit(solution)/shard_map/ppermute | solution.py:143
  17.5 2.4 %collective-permute-done.5 = bf16[40,3072]{1,0:T(8,128)(2,1)S(1)} collective-permute-done((bf16[40,3072]{1,0:T(8,128)(2,1)S(1)}, bf16[40,3072]{1,0:T(8,128)(2,1)S(1)}, u32[]{:S(2)}, u32[]{:S(2)}) %collective-permute-start.5) | collective-permute-done | bytes 245792 | tf_op jit(solution)/shard_map/ppermute | solution.py:143
  25.6 1.9 %collective-permute-done.6 = bf16[40,3072]{1,0:T(8,128)(2,1)S(1)} collective-permute-done((bf16[40,3072]{1,0:T(8,128)(2,1)S(1)}, bf16[40,3072]{1,0:T(8,128)(2,1)S(1)}, u32[]{:S(2)}, u32[]{:S(2)}) %collective-permute-start.6) | collective-permute-done | bytes 245792 | tf_op jit(solution)/shard_map/ppermute | solution.py:26
  27.6 2.2 %collective-permute-done.7 = bf16[40,3072]{1,0:T(8,128)(2,1)S(1)} collective-permute-done((bf16[40,3072]{1,0:T(8,128)(2,1)S(1)}, bf16[40,3072]{1,0:T(8,128)(2,1)S(1)}, u32[]{:S(2)}, u32[]{:S(2)}) %collective-permute-start.7) | collective-permute-done | bytes 245792 | tf_op jit(solution)/shard_map/ppermute | solution.py:26
  32.6 2.2 %collective-permute-start.13 = (bf16[40,3072]{1,0:T(8,128)(2,1)S(1)}, bf16[40,3072]{1,0:T(8,128)(2,1)S(1)}, u32[]{:S(2)}, u32[]{:S(2)}) collective-permute-start(bf16[40,3072]{1,0:T(8,128)(2,1)S(1)} %collective-permute-done.5), channel_id=1, source_target_pairs={{0,24},{1,97},{8,0},{9,105},{16,8},{17,113},{24,16},{25,121},{32,5... | collective-permute-start | bytes 737288 | tf_op jit(solution)/shard_map/ppermute | solution.py:26
  40.7 2.0 %collective-permute-done.12 = bf16[40,3072]{1,0:T(8,128)(2,1)S(1)} collective-permute-done((bf16[40,3072]{1,0:T(8,128)(2,1)S(1)}, bf16[40,3072]{1,0:T(8,128)(2,1)S(1)}, u32[]{:S(2)}, u32[]{:S(2)}) %collective-permute-start.12) | collective-permute-done | bytes 245792 | tf_op jit(solution)/shard_map/ppermute | solution.py:26
  45.5 6.3 %collective-permute-done.9.refs_6_ = bf16[160,3072]{1,0:T(8,128)(2,1)S(1)} collective-permute-done((bf16[160,3072]{1,0:T(8,128)(2,1)S(1)}, bf16[160,3072]{1,0:T(8,128)(2,1)S(1)}, u32[]{:S(2)}, u32[]{:S(2)}) %collective-permute-start.9) | collective-permute-done | bytes 983072 | tf_op jit(solution)/shard_map/ppermute | solution.py:26
  52.0 2.9 %collective-permute-start.17 = (bf16[160,1536]{1,0:T(8,128)(2,1)S(1)}, bf16[160,1536]{1,0:T(8,128)(2,1)S(1)}, u32[]{:S(2)}, u32[]{:S(2)}) collective-permute-start(bf16[160,1536]{1,0:T(8,128)(2,1)S(1)} %slice.86), channel_id=1, source_target_pairs={{0,96},{1,25},{8,104},{9,1},{16,112},{17,9},{24,120},{25,17},{32,0... | collective-permute-start | bytes 1474568 | tf_op jit(solution)/shard_map/ppermute | solution.py:26
  54.9 3.5 %ffn.7 = (bf16[160,3072]{1,0:T(8,128)(2,1)S(1)}, bf16[160,3072]{1,0:T(8,128)(2,1)S(1)}) custom-call(s32[1]{0:T(128)} %bitcast.2.core, bf16[3072,256]{1,0:T(8,128)(2,1)S(1)} %bitcast.24, bf16[3072,256]{1,0:T(8,128)(2,1)S(1)} %collective-permute-done.refs_1_, bf16[3072,256]{1,0:T(8,128)(2,1)S(1)} %bitcast.31, ...), custom_call_target="tpu_custom_call" | custom-call | flops 3019898880 | bytes 13369344 | tf_op jit(solution)/shard_map/ffn/pallas_call | solution.py:95
  58.4 1.9 %ffn.10 = bf16[160,3072]{1,0:T(8,128)(2,1)S(1)} custom-call(s32[1]{0:T(128)} %bitcast.2.core, bf16[3072,256]{1,0:T(8,128)(2,1)S(1)} %bitcast.25, bf16[3072,256]{1,0:T(8,128)(2,1)S(1)} %collective-permute-done.refs_1_, bf16[3072,256]{1,0:T(8,128)(2,1)S(1)} %bitcast.32, bf16[3072,256]{1,0:T(8,128)(2,1)S(1)} %collective-permute-done.1.refs_3_, ...), custom_call_target="tpu_custom_call" | custom-call | flops 1509949440 | bytes 11403264 | tf_op jit(solution)/shard_map/ffn/pallas_call | solution.py:95
  60.3 2.1 %collective-permute-done.15.refs_6_ = bf16[160,3072]{1,0:T(8,128)(2,1)S(1)} collective-permute-done((bf16[160,3072]{1,0:T(8,128)(2,1)S(1)}, bf16[160,3072]{1,0:T(8,128)(2,1)S(1)}, u32[]{:S(2)}, u32[]{:S(2)}) %collective-permute-start.15) | collective-permute-done | bytes 983072 | tf_op jit(solution)/shard_map/ppermute | solution.py:26
  62.5 2.7 %collective-permute-start.27 = (bf16[160,1536]{1,0:T(8,128)(2,1)S(1)}, bf16[160,1536]{1,0:T(8,128)(2,1)S(1)}, u32[]{:S(2)}, u32[]{:S(2)}) collective-permute-start(bf16[160,1536]{1,0:T(8,128)(2,1)S(1)} %slice.87), channel_id=1, source_target_pairs={{0,96},{1,25},{8,104},{9,1},{16,112},{17,9},{24,120},{25,17},{32,0... | collective-permute-start | bytes 1474568 | tf_op jit(solution)/shard_map/ppermute | solution.py:26
  65.3 3.5 %ffn.8 = (bf16[160,3072]{1,0:T(8,128)(2,1)S(1)}, bf16[160,3072]{1,0:T(8,128)(2,1)S(1)}) custom-call(s32[1]{0:T(128)} %bitcast.2.core, bf16[3072,256]{1,0:T(8,128)(2,1)S(1)} %bitcast.26, bf16[3072,256]{1,0:T(8,128)(2,1)S(1)} %collective-permute-done.refs_1_, bf16[3072,256]{1,0:T(8,128)(2,1)S(1)} %bitcast.33, ...), custom_call_target="tpu_custom_call" | custom-call | flops 3019898880 | bytes 13369344 | tf_op jit(solution)/shard_map/ffn/pallas_call | solution.py:95
  68.8 1.8 %ffn.9 = (bf16[160,1536]{1,0:T(8,128)(2,1)S(1)}, bf16[160,1536]{1,0:T(8,128)(2,1)S(1)}) custom-call(s32[1]{0:T(128)} %bitcast.2.core, bf16[3072,256]{1,0:T(8,128)(2,1)S(1)} %bitcast.27, bf16[3072,256]{1,0:T(8,128)(2,1)S(1)} %collective-permute-done.refs_1_, bf16[3072,256]{1,0:T(8,128)(2,1)S(1)} %bitcast.34, ...), custom_call_target="tpu_custom_call" | custom-call | flops 1509949440 | bytes 11403264 | tf_op jit(solution)/shard_map/ffn/pallas_call | solution.py:95
  72.9 1.8 %ffn.11 = (bf16[160,1536]{1,0:T(8,128)(2,1)S(1)}, bf16[160,1536]{1,0:T(8,128)(2,1)S(1)}) custom-call(s32[1]{0:T(128)} %bitcast.2.core, bf16[3072,256]{1,0:T(8,128)(2,1)S(1)} %bitcast.28, bf16[3072,256]{1,0:T(8,128)(2,1)S(1)} %collective-permute-done.refs_1_, bf16[3072,256]{1,0:T(8,128)(2,1)S(1)} %bitcast.35, ...), custom_call_target="tpu_custom_call" | custom-call | flops 1509949440 | bytes 11403264 | tf_op jit(solution)/shard_map/ffn/pallas_call | solution.py:95
  74.7 2.1 %collective-permute-start.30 = (bf16[160,1536]{1,0:T(8,128)(2,1)S(1)}, bf16[160,1536]{1,0:T(8,128)(2,1)S(1)}, u32[]{:S(2)}, u32[]{:S(2)}) collective-permute-start(bf16[160,1536]{1,0:T(8,128)(2,1)S(1)} %get-tuple-element.35), channel_id=1, source_target_pairs={{0,96},{1,25},{8,104},{9,1},{16,112},{17,9},{24,120},{25,17},{32,0... | collective-permute-start | bytes 1474568 | tf_op jit(solution)/shard_map/ppermute | solution.py:26
  76.8 1.8 %collective-permute-done.20 = bf16[160,1536]{1,0:T(8,128)(2,1)S(1)} collective-permute-done((bf16[160,1536]{1,0:T(8,128)(2,1)S(1)}, bf16[160,1536]{1,0:T(8,128)(2,1)S(1)}, u32[]{:S(2)}, u32[]{:S(2)}) %collective-permute-start.20) | collective-permute-done | bytes 491552 | tf_op jit(solution)/shard_map/ppermute | solution.py:26
  78.9 2.1 %collective-permute-start.21 = (bf16[160,3072]{1,0:T(8,128)(2,1)S(1)}, bf16[160,3072]{1,0:T(8,128)(2,1)S(1)}, u32[]{:S(2)}, u32[]{:S(2)}) collective-permute-start(bf16[160,3072]{1,0:T(8,128)(2,1)S(1)} %pad_maximum_fusion.2), channel_id=1, source_target_pairs={{0,96},{1,25},{8,104},{9,1},{16,112},{17,9},{24,120},{25,17},{32,0... | collective-permute-start | bytes 2949128 | tf_op jit(solution)/shard_map/ppermute | solution.py:26
  81.3 2.6 %collective-permute-done.30 = bf16[160,1536]{1,0:T(8,128)(2,1)S(1)} collective-permute-done((bf16[160,1536]{1,0:T(8,128)(2,1)S(1)}, bf16[160,1536]{1,0:T(8,128)(2,1)S(1)}, u32[]{:S(2)}, u32[]{:S(2)}) %collective-permute-start.30) | collective-permute-done | bytes 491552 | tf_op jit(solution)/shard_map/ppermute | solution.py:26
  84.2 2.1 %collective-permute-start.31 = (bf16[160,3072]{1,0:T(8,128)(2,1)S(1)}, bf16[160,3072]{1,0:T(8,128)(2,1)S(1)}, u32[]{:S(2)}, u32[]{:S(2)}) collective-permute-start(bf16[160,3072]{1,0:T(8,128)(2,1)S(1)} %pad_maximum_fusion.4), channel_id=1, source_target_pairs={{0,96},{1,25},{8,104},{9,1},{16,112},{17,9},{24,120},{25,17},{32,0... | collective-permute-start | bytes 2949128 | tf_op jit(solution)/shard_map/ppermute | solution.py:26
  86.6 7.8 %collective-permute-done.21 = bf16[160,3072]{1,0:T(8,128)(2,1)S(1)} collective-permute-done((bf16[160,3072]{1,0:T(8,128)(2,1)S(1)}, bf16[160,3072]{1,0:T(8,128)(2,1)S(1)}, u32[]{:S(2)}, u32[]{:S(2)}) %collective-permute-start.21) | collective-permute-done | bytes 983072 | tf_op jit(solution)/shard_map/ppermute | solution.py:26
  94.5 2.3 %collective-permute-done.19 = bf16[160,3072]{1,0:T(8,128)(2,1)S(1)} collective-permute-done((bf16[160,3072]{1,0:T(8,128)(2,1)S(1)}, bf16[160,3072]{1,0:T(8,128)(2,1)S(1)}, u32[]{:S(2)}, u32[]{:S(2)}) %collective-permute-start.19) | collective-permute-done | bytes 983072 | tf_op jit(solution)/shard_map/ppermute | solution.py:26
  97.3 2.5 %collective-permute-start.24 = (bf16[40,3072]{1,0:T(8,128)(2,1)S(1)}, bf16[40,3072]{1,0:T(8,128)(2,1)S(1)}, u32[]{:S(2)}, u32[]{:S(2)}) collective-permute-start(bf16[40,3072]{1,0:T(8,128)(2,1)S(1)} %get-tuple-element.44), channel_id=1, source_target_pairs={{0,16},{1,65},{8,24},{9,73},{16,0},{17,81},{24,8},{25,89},{32,48},... | collective-permute-start | bytes 737288 | tf_op jit(solution)/shard_map/ppermute | solution.py:26
  100.5 2.0 %collective-permute-start.22 = (bf16[40,3072]{1,0:T(8,128)(2,1)S(1)}, bf16[40,3072]{1,0:T(8,128)(2,1)S(1)}, u32[]{:S(2)}, u32[]{:S(2)}) collective-permute-start(bf16[40,3072]{1,0:T(8,128)(2,1)S(1)} %get-tuple-element.43), channel_id=1, source_target_pairs={{0,24},{1,97},{8,0},{9,105},{16,8},{17,113},{24,16},{25,121},{32,5... | collective-permute-start | bytes 737288 | tf_op jit(solution)/shard_map/ppermute | solution.py:26
  102.5 3.3 %collective-permute-done.31 = bf16[160,3072]{1,0:T(8,128)(2,1)S(1)} collective-permute-done((bf16[160,3072]{1,0:T(8,128)(2,1)S(1)}, bf16[160,3072]{1,0:T(8,128)(2,1)S(1)}, u32[]{:S(2)}, u32[]{:S(2)}) %collective-permute-start.31) | collective-permute-done | bytes 983072 | tf_op jit(solution)/shard_map/ppermute | solution.py:26
  105.8 6.1 %collective-permute-done.29 = bf16[160,3072]{1,0:T(8,128)(2,1)S(1)} collective-permute-done((bf16[160,3072]{1,0:T(8,128)(2,1)S(1)}, bf16[160,3072]{1,0:T(8,128)(2,1)S(1)}, u32[]{:S(2)}, u32[]{:S(2)}) %collective-permute-start.29) | collective-permute-done | bytes 983072 | tf_op jit(solution)/shard_map/ppermute | solution.py:26
  112.5 3.2 %collective-permute-start.34 = (bf16[40,3072]{1,0:T(8,128)(2,1)S(1)}, bf16[40,3072]{1,0:T(8,128)(2,1)S(1)}, u32[]{:S(2)}, u32[]{:S(2)}) collective-permute-start(bf16[40,3072]{1,0:T(8,128)(2,1)S(1)} %get-tuple-element.47), channel_id=1, source_target_pairs={{0,16},{1,65},{8,24},{9,73},{16,0},{17,81},{24,8},{25,89},{32,48},... | collective-permute-start | bytes 737288 | tf_op jit(solution)/shard_map/ppermute | solution.py:26
  116.0 2.3 %collective-permute-start.32 = (bf16[40,3072]{1,0:T(8,128)(2,1)S(1)}, bf16[40,3072]{1,0:T(8,128)(2,1)S(1)}, u32[]{:S(2)}, u32[]{:S(2)}) collective-permute-start(bf16[40,3072]{1,0:T(8,128)(2,1)S(1)} %get-tuple-element.46), channel_id=1, source_target_pairs={{0,24},{1,97},{8,0},{9,105},{16,8},{17,113},{24,16},{25,121},{32,5... | collective-permute-start | bytes 737288 | tf_op jit(solution)/shard_map/ppermute | solution.py:26
  118.5 3.0 %collective-permute-start.25 = (bf16[40,3072]{1,0:T(8,128)(2,1)S(1)}, bf16[40,3072]{1,0:T(8,128)(2,1)S(1)}, u32[]{:S(2)}, u32[]{:S(2)}) collective-permute-start(bf16[40,3072]{1,0:T(8,128)(2,1)S(1)} %add_convert_fusion.7), channel_id=1, source_target_pairs={{0,0},{2,2},{4,4},{6,6},{7,1},{1,3},{3,5},{5,7},{8,8},{10,10},{12,... | collective-permute-start | bytes 737288 | tf_op jit(solution)/shard_map/ppermute | solution.py:192
  122.6 5.5 %collective-permute-done.25 = bf16[40,3072]{1,0:T(8,128)(2,1)S(1)} collective-permute-done((bf16[40,3072]{1,0:T(8,128)(2,1)S(1)}, bf16[40,3072]{1,0:T(8,128)(2,1)S(1)}, u32[]{:S(2)}, u32[]{:S(2)}) %collective-permute-start.25) | collective-permute-done | bytes 245792 | tf_op jit(solution)/shard_map/ppermute | solution.py:192
  129.6 5.7 %collective-permute-done.35 = bf16[40,3072]{1,0:T(8,128)(2,1)S(1)} collective-permute-done((bf16[40,3072]{1,0:T(8,128)(2,1)S(1)}, bf16[40,3072]{1,0:T(8,128)(2,1)S(1)}, u32[]{:S(2)}, u32[]{:S(2)}) %collective-permute-start.35) | collective-permute-done | bytes 245792 | tf_op jit(solution)/shard_map/ppermute | solution.py:193
  (99 shorter events, 36.5 us)
Async XLA Ops:
  0.0 21.2 %collective-permute-start = (bf16[3072,256]{1,0:T(8,128)(2,1)}, bf16[3072,256]{1,0:T(8,128)(2,1)S(1)}, u32[]{:S(2)}, u32[]{:S(2)}) collective-permute-start(bf16[3072,256]{1,0:T(8,128)(2,1)} %bitcast.22), channel_id=1, source_target_pairs={{0,1},{1,0},{2,3},{3,2},{4,5},{5,4},{6,7},{7,6},{8,9},{9,8},{10,11... | collective-permute-start | bytes 4718600 | tf_op jit(solution)/shard_map/ppermute | solution.py:30
  1.4 19.8 %collective-permute-start.1 = (bf16[3072,256]{1,0:T(8,128)(2,1)}, bf16[3072,256]{1,0:T(8,128)(2,1)S(1)}, u32[]{:S(2)}, u32[]{:S(2)}) collective-permute-start(bf16[3072,256]{1,0:T(8,128)(2,1)} %bitcast.29), channel_id=1, source_target_pairs={{0,1},{1,0},{2,3},{3,2},{4,5},{5,4},{6,7},{7,6},{8,9},{9,8},{10,11... | collective-permute-start | bytes 4718600 | tf_op jit(solution)/shard_map/ppermute | solution.py:30
  1.4 14.1 %collective-permute-start.2 = (bf16[512,1536]{1,0:T(8,128)(2,1)}, bf16[512,1536]{1,0:T(8,128)(2,1)}, u32[]{:S(2)}, u32[]{:S(2)}) collective-permute-start(bf16[512,1536]{1,0:T(8,128)(2,1)} %bitcast.36), channel_id=1, source_target_pairs={{0,1},{1,0},{2,3},{3,2},{4,5},{5,4},{6,7},{7,6},{8,9},{9,8},{10,11... | collective-permute-start | bytes 4718600 | tf_op jit(solution)/shard_map/ppermute | solution.py:30
  1.9 7.5 %collective-permute-start.3 = (bf16[64,1536]{1,0:T(8,128)(2,1)}, bf16[64,1536]{1,0:T(8,128)(2,1)S(1)}, u32[]{:S(2)}, u32[]{:S(2)}) collective-permute-start(bf16[64,1536]{1,0:T(8,128)(2,1)} %param.6), channel_id=1, source_target_pairs={{0,1},{1,0},{2,3},{3,2},{4,5},{5,4},{6,7},{7,6},{8,9},{9,8},{10,11... | collective-permute-start | bytes 589832 | tf_op jit(solution)/shard_map/ppermute | solution.py:30
  9.7 10.1 %collective-permute-start.5 = (bf16[40,3072]{1,0:T(8,128)(2,1)S(1)}, bf16[40,3072]{1,0:T(8,128)(2,1)S(1)}, u32[]{:S(2)}, u32[]{:S(2)}) collective-permute-start(bf16[40,3072]{1,0:T(8,128)(2,1)S(1)} %get-tuple-element.50), channel_id=1, source_target_pairs={{0,4},{2,6},{4,0},{6,2},{1,3},{3,5},{5,7},{7,1},{8,12},{10,14},{12... | collective-permute-start | bytes 737288 | tf_op jit(solution)/shard_map/ppermute | solution.py:143
  11.5 9.7 %collective-permute-start.4 = (bf16[40,3072]{1,0:T(8,128)(2,1)S(1)}, bf16[40,3072]{1,0:T(8,128)(2,1)S(1)}, u32[]{:S(2)}, u32[]{:S(2)}) collective-permute-start(bf16[40,3072]{1,0:T(8,128)(2,1)S(1)} %get-tuple-element.49), channel_id=1, source_target_pairs={{0,0},{2,2},{4,4},{6,6},{1,7},{3,1},{5,3},{7,5},{8,8},{10,10},{12,... | collective-permute-start | bytes 737288 | tf_op jit(solution)/shard_map/ppermute | solution.py:143
  22.5 7.3 %collective-permute-start.7 = (bf16[40,3072]{1,0:T(8,128)(2,1)S(1)}, bf16[40,3072]{1,0:T(8,128)(2,1)S(1)}, u32[]{:S(2)}, u32[]{:S(2)}) collective-permute-start(bf16[40,3072]{1,0:T(8,128)(2,1)S(1)} %collective-permute-done.4), channel_id=1, source_target_pairs={{0,24},{1,97},{8,0},{9,105},{16,8},{17,113},{24,16},{25,121},{32,5... | collective-permute-start | bytes 737288 | tf_op jit(solution)/shard_map/ppermute | solution.py:26
  24.0 7.3 %collective-permute-start.8 = (bf16[40,3072]{1,0:T(8,128)(2,1)S(1)}, bf16[40,3072]{1,0:T(8,128)(2,1)S(1)}, u32[]{:S(2)}, u32[]{:S(2)}) collective-permute-start(bf16[40,3072]{1,0:T(8,128)(2,1)S(1)} %collective-permute-done.4), channel_id=1, source_target_pairs={{0,16},{1,65},{8,24},{9,73},{16,0},{17,81},{24,8},{25,89},{32,48},... | collective-permute-start | bytes 737288 | tf_op jit(solution)/shard_map/ppermute | solution.py:26
  31.4 7.9 %collective-permute-start.14 = (bf16[40,3072]{1,0:T(8,128)(2,1)S(1)}, bf16[40,3072]{1,0:T(8,128)(2,1)S(1)}, u32[]{:S(2)}, u32[]{:S(2)}) collective-permute-start(bf16[40,3072]{1,0:T(8,128)(2,1)S(1)} %collective-permute-done.5), channel_id=1, source_target_pairs={{0,16},{1,65},{8,24},{9,73},{16,0},{17,81},{24,8},{25,89},{32,48},... | collective-permute-start | bytes 737288 | tf_op jit(solution)/shard_map/ppermute | solution.py:26
  32.6 8.1 %collective-permute-start.13 = (bf16[40,3072]{1,0:T(8,128)(2,1)S(1)}, bf16[40,3072]{1,0:T(8,128)(2,1)S(1)}, u32[]{:S(2)}, u32[]{:S(2)}) collective-permute-start(bf16[40,3072]{1,0:T(8,128)(2,1)S(1)} %collective-permute-done.5), channel_id=1, source_target_pairs={{0,24},{1,97},{8,0},{9,105},{16,8},{17,113},{24,16},{25,121},{32,5... | collective-permute-start | bytes 737288 | tf_op jit(solution)/shard_map/ppermute | solution.py:26
  34.7 8.0 %collective-permute-start.12 = (bf16[40,3072]{1,0:T(8,128)(2,1)S(1)}, bf16[40,3072]{1,0:T(8,128)(2,1)S(1)}, u32[]{:S(2)}, u32[]{:S(2)}) collective-permute-start(bf16[40,3072]{1,0:T(8,128)(2,1)S(1)} %collective-permute-done.5), channel_id=1, source_target_pairs={{0,8},{1,33},{8,16},{9,41},{16,24},{17,49},{24,0},{25,57},{32,40},... | collective-permute-start | bytes 737288 | tf_op jit(solution)/shard_map/ppermute | solution.py:26
  34.7 17.1 %collective-permute-start.9 = (bf16[160,3072]{1,0:T(8,128)(2,1)S(1)}, bf16[160,3072]{1,0:T(8,128)(2,1)S(1)}, u32[]{:S(2)}, u32[]{:S(2)}) collective-permute-start(bf16[160,3072]{1,0:T(8,128)(2,1)S(1)} %constant_dynamic-update-slice_fusion.refs_6_), channel_id=1, source_target_pairs={{0,32},{1,9},{8,40},{9,17},{16,48},{17,25},{24,56},{25,1},{32,64},... | collective-permute-start | bytes 2949128 | tf_op jit(solution)/shard_map/ppermute | solution.py:26
  35.9 16.0 %collective-permute-start.10 = (bf16[160,3072]{1,0:T(8,128)(2,1)S(1)}, bf16[160,3072]{1,0:T(8,128)(2,1)S(1)}, u32[]{:S(2)}, u32[]{:S(2)}) collective-permute-start(bf16[160,3072]{1,0:T(8,128)(2,1)S(1)} %constant_dynamic-update-slice_fusion.refs_6_), channel_id=1, source_target_pairs={{0,96},{1,25},{8,104},{9,1},{16,112},{17,9},{24,120},{25,17},{32,0... | collective-permute-start | bytes 2949128 | tf_op jit(solution)/shard_map/ppermute | solution.py:26
  42.8 19.6 %collective-permute-start.15 = (bf16[160,3072]{1,0:T(8,128)(2,1)S(1)}, bf16[160,3072]{1,0:T(8,128)(2,1)S(1)}, u32[]{:S(2)}, u32[]{:S(2)}) collective-permute-start(bf16[160,3072]{1,0:T(8,128)(2,1)S(1)} %pad_maximum_fusion.refs_6_), channel_id=1, source_target_pairs={{0,32},{1,9},{8,40},{9,17},{16,48},{17,25},{24,56},{25,1},{32,64},... | collective-permute-start | bytes 2949128 | tf_op jit(solution)/shard_map/ppermute | solution.py:26
  44.5 18.0 %collective-permute-start.16 = (bf16[160,3072]{1,0:T(8,128)(2,1)S(1)}, bf16[160,3072]{1,0:T(8,128)(2,1)S(1)}, u32[]{:S(2)}, u32[]{:S(2)}) collective-permute-start(bf16[160,3072]{1,0:T(8,128)(2,1)S(1)} %pad_maximum_fusion.refs_6_), channel_id=1, source_target_pairs={{0,96},{1,25},{8,104},{9,1},{16,112},{17,9},{24,120},{25,17},{32,0... | collective-permute-start | bytes 2949128 | tf_op jit(solution)/shard_map/ppermute | solution.py:26
  51.9 16.9 %collective-permute-start.11 = (bf16[160,1536]{1,0:T(8,128)(2,1)S(1)}, bf16[160,1536]{1,0:T(8,128)(2,1)S(1)}, u32[]{:S(2)}, u32[]{:S(2)}) collective-permute-start(bf16[160,1536]{1,0:T(8,128)(2,1)S(1)} %slice.85), channel_id=1, source_target_pairs={{0,32},{1,9},{8,40},{9,17},{16,48},{17,25},{24,56},{25,1},{32,64},... | collective-permute-start | bytes 1474568 | tf_op jit(solution)/shard_map/ppermute | solution.py:26
  52.0 16.8 %collective-permute-start.17 = (bf16[160,1536]{1,0:T(8,128)(2,1)S(1)}, bf16[160,1536]{1,0:T(8,128)(2,1)S(1)}, u32[]{:S(2)}, u32[]{:S(2)}) collective-permute-start(bf16[160,1536]{1,0:T(8,128)(2,1)S(1)} %slice.86), channel_id=1, source_target_pairs={{0,96},{1,25},{8,104},{9,1},{16,112},{17,9},{24,120},{25,17},{32,0... | collective-permute-start | bytes 1474568 | tf_op jit(solution)/shard_map/ppermute | solution.py:26
  62.4 10.5 %collective-permute-start.26 = (bf16[160,1536]{1,0:T(8,128)(2,1)S(1)}, bf16[160,1536]{1,0:T(8,128)(2,1)S(1)}, u32[]{:S(2)}, u32[]{:S(2)}) collective-permute-start(bf16[160,1536]{1,0:T(8,128)(2,1)S(1)} %slice.74), channel_id=1, source_target_pairs={{0,32},{1,9},{8,40},{9,17},{16,48},{17,25},{24,56},{25,1},{32,64},... | collective-permute-start | bytes 1474568 | tf_op jit(solution)/shard_map/ppermute | solution.py:26
  62.5 10.3 %collective-permute-start.27 = (bf16[160,1536]{1,0:T(8,128)(2,1)S(1)}, bf16[160,1536]{1,0:T(8,128)(2,1)S(1)}, u32[]{:S(2)}, u32[]{:S(2)}) collective-permute-start(bf16[160,1536]{1,0:T(8,128)(2,1)S(1)} %slice.87), channel_id=1, source_target_pairs={{0,96},{1,25},{8,104},{9,1},{16,112},{17,9},{24,120},{25,17},{32,0... | collective-permute-start | bytes 1474568 | tf_op jit(solution)/shard_map/ppermute | solution.py:26
  70.6 8.0 %collective-permute-start.20 = (bf16[160,1536]{1,0:T(8,128)(2,1)S(1)}, bf16[160,1536]{1,0:T(8,128)(2,1)S(1)}, u32[]{:S(2)}, u32[]{:S(2)}) collective-permute-start(bf16[160,1536]{1,0:T(8,128)(2,1)S(1)} %get-tuple-element.29), channel_id=1, source_target_pairs={{0,96},{1,25},{8,104},{9,1},{16,112},{17,9},{24,120},{25,17},{32,0... | collective-permute-start | bytes 1474568 | tf_op jit(solution)/shard_map/ppermute | solution.py:26
  71.7 9.3 %collective-permute-start.18 = (bf16[160,1536]{1,0:T(8,128)(2,1)S(1)}, bf16[160,1536]{1,0:T(8,128)(2,1)S(1)}, u32[]{:S(2)}, u32[]{:S(2)}) collective-permute-start(bf16[160,1536]{1,0:T(8,128)(2,1)S(1)} %get-tuple-element.27), channel_id=1, source_target_pairs={{0,32},{1,9},{8,40},{9,17},{16,48},{17,25},{24,56},{25,1},{32,64},... | collective-permute-start | bytes 1474568 | tf_op jit(solution)/shard_map/ppermute | solution.py:26
  74.7 9.2 %collective-permute-start.30 = (bf16[160,1536]{1,0:T(8,128)(2,1)S(1)}, bf16[160,1536]{1,0:T(8,128)(2,1)S(1)}, u32[]{:S(2)}, u32[]{:S(2)}) collective-permute-start(bf16[160,1536]{1,0:T(8,128)(2,1)S(1)} %get-tuple-element.35), channel_id=1, source_target_pairs={{0,96},{1,25},{8,104},{9,1},{16,112},{17,9},{24,120},{25,17},{32,0... | collective-permute-start | bytes 1474568 | tf_op jit(solution)/shard_map/ppermute | solution.py:26
  76.8 9.5 %collective-permute-start.28 = (bf16[160,1536]{1,0:T(8,128)(2,1)S(1)}, bf16[160,1536]{1,0:T(8,128)(2,1)S(1)}, u32[]{:S(2)}, u32[]{:S(2)}) collective-permute-start(bf16[160,1536]{1,0:T(8,128)(2,1)S(1)} %get-tuple-element.34), channel_id=1, source_target_pairs={{0,32},{1,9},{8,40},{9,17},{16,48},{17,25},{24,56},{25,1},{32,64},... | collective-permute-start | bytes 1474568 | tf_op jit(solution)/shard_map/ppermute | solution.py:26
  78.9 15.6 %collective-permute-start.21 = (bf16[160,3072]{1,0:T(8,128)(2,1)S(1)}, bf16[160,3072]{1,0:T(8,128)(2,1)S(1)}, u32[]{:S(2)}, u32[]{:S(2)}) collective-permute-start(bf16[160,3072]{1,0:T(8,128)(2,1)S(1)} %pad_maximum_fusion.2), channel_id=1, source_target_pairs={{0,96},{1,25},{8,104},{9,1},{16,112},{17,9},{24,120},{25,17},{32,0... | collective-permute-start | bytes 2949128 | tf_op jit(solution)/shard_map/ppermute | solution.py:26
  81.2 15.5 %collective-permute-start.19 = (bf16[160,3072]{1,0:T(8,128)(2,1)S(1)}, bf16[160,3072]{1,0:T(8,128)(2,1)S(1)}, u32[]{:S(2)}, u32[]{:S(2)}) collective-permute-start(bf16[160,3072]{1,0:T(8,128)(2,1)S(1)} %pad_maximum_fusion.1), channel_id=1, source_target_pairs={{0,32},{1,9},{8,40},{9,17},{16,48},{17,25},{24,56},{25,1},{32,64},... | collective-permute-start | bytes 2949128 | tf_op jit(solution)/shard_map/ppermute | solution.py:26
  84.2 21.7 %collective-permute-start.31 = (bf16[160,3072]{1,0:T(8,128)(2,1)S(1)}, bf16[160,3072]{1,0:T(8,128)(2,1)S(1)}, u32[]{:S(2)}, u32[]{:S(2)}) collective-permute-start(bf16[160,3072]{1,0:T(8,128)(2,1)S(1)} %pad_maximum_fusion.4), channel_id=1, source_target_pairs={{0,96},{1,25},{8,104},{9,1},{16,112},{17,9},{24,120},{25,17},{32,0... | collective-permute-start | bytes 2949128 | tf_op jit(solution)/shard_map/ppermute | solution.py:26
  86.5 25.4 %collective-permute-start.29 = (bf16[160,3072]{1,0:T(8,128)(2,1)S(1)}, bf16[160,3072]{1,0:T(8,128)(2,1)S(1)}, u32[]{:S(2)}, u32[]{:S(2)}) collective-permute-start(bf16[160,3072]{1,0:T(8,128)(2,1)S(1)} %pad_maximum_fusion.3), channel_id=1, source_target_pairs={{0,32},{1,9},{8,40},{9,17},{16,48},{17,25},{24,56},{25,1},{32,64},... | collective-permute-start | bytes 2949128 | tf_op jit(solution)/shard_map/ppermute | solution.py:26
  97.3 18.7 %collective-permute-start.24 = (bf16[40,3072]{1,0:T(8,128)(2,1)S(1)}, bf16[40,3072]{1,0:T(8,128)(2,1)S(1)}, u32[]{:S(2)}, u32[]{:S(2)}) collective-permute-start(bf16[40,3072]{1,0:T(8,128)(2,1)S(1)} %get-tuple-element.44), channel_id=1, source_target_pairs={{0,16},{1,65},{8,24},{9,73},{16,0},{17,81},{24,8},{25,89},{32,48},... | collective-permute-start | bytes 737288 | tf_op jit(solution)/shard_map/ppermute | solution.py:26
  99.8 18.5 %collective-permute-start.23 = (bf16[40,3072]{1,0:T(8,128)(2,1)S(1)}, bf16[40,3072]{1,0:T(8,128)(2,1)S(1)}, u32[]{:S(2)}, u32[]{:S(2)}) collective-permute-start(bf16[40,3072]{1,0:T(8,128)(2,1)S(1)} %get-tuple-element.45), channel_id=1, source_target_pairs={{0,8},{1,33},{8,16},{9,41},{16,24},{17,49},{24,0},{25,57},{32,40},... | collective-permute-start | bytes 737288 | tf_op jit(solution)/shard_map/ppermute | solution.py:26
  100.5 17.9 %collective-permute-start.22 = (bf16[40,3072]{1,0:T(8,128)(2,1)S(1)}, bf16[40,3072]{1,0:T(8,128)(2,1)S(1)}, u32[]{:S(2)}, u32[]{:S(2)}) collective-permute-start(bf16[40,3072]{1,0:T(8,128)(2,1)S(1)} %get-tuple-element.43), channel_id=1, source_target_pairs={{0,24},{1,97},{8,0},{9,105},{16,8},{17,113},{24,16},{25,121},{32,5... | collective-permute-start | bytes 737288 | tf_op jit(solution)/shard_map/ppermute | solution.py:26
  112.5 9.0 %collective-permute-start.34 = (bf16[40,3072]{1,0:T(8,128)(2,1)S(1)}, bf16[40,3072]{1,0:T(8,128)(2,1)S(1)}, u32[]{:S(2)}, u32[]{:S(2)}) collective-permute-start(bf16[40,3072]{1,0:T(8,128)(2,1)S(1)} %get-tuple-element.47), channel_id=1, source_target_pairs={{0,16},{1,65},{8,24},{9,73},{16,0},{17,81},{24,8},{25,89},{32,48},... | collective-permute-start | bytes 737288 | tf_op jit(solution)/shard_map/ppermute | solution.py:26
  118.5 9.7 %collective-permute-start.25 = (bf16[40,3072]{1,0:T(8,128)(2,1)S(1)}, bf16[40,3072]{1,0:T(8,128)(2,1)S(1)}, u32[]{:S(2)}, u32[]{:S(2)}) collective-permute-start(bf16[40,3072]{1,0:T(8,128)(2,1)S(1)} %add_convert_fusion.7), channel_id=1, source_target_pairs={{0,0},{2,2},{4,4},{6,6},{7,1},{1,3},{3,5},{5,7},{8,8},{10,10},{12,... | collective-permute-start | bytes 737288 | tf_op jit(solution)/shard_map/ppermute | solution.py:192
  (10 other events, 123.1 us)

commit v3 on v2

--- a/solution.py
+++ b/solution.py
@@ -139,8 +139,9 @@
         [jnp.dot(pick_all, v, preferred_element_type=F32).astype(BF) for v in (tokens, other_tokens)], axis=1
     )
 
-    def dispatch(k):
-        return lax.ppermute(outgoing[k * capacity:(k + 1) * capacity], ("expert", "et"), send[k])
+    def dispatch(k, *after):
+        rows = outgoing[k * capacity:(k + 1) * capacity]
+        return lax.ppermute(tie(rows, *after) if after else rows, ("expert", "et"), send[k])
 
     def far_pair(left, right, first):
         return both(left[:, :half], right[:, half:], first)
@@ -151,33 +152,33 @@
             jnp.concatenate([add(right[:, :half], got_a), right[:, half:]], axis=1),
         )
 
-    weights = []
-    for w in (w_down[0], w_up[0], w_gate[0]):
-        weights = [w, swap(w)] + weights
-    hid = w_gate.shape[2]
-    down = weights[5]
-    weights[5] = jnp.where(c == 0, down, jnp.concatenate([down[hid:], down[:hid]], axis=0))
     z0 = dispatch(0)
     z1 = dispatch(1)
-
-    def spread(own):
-        left, right, far = shift(own, True, 1), shift(own, True, -1), shift(own, True, 2)
-        return jnp.concatenate([own, left, right, far], axis=0)
-
-    def collect(sums):
+    weights = []
+    for w in (w_gate[0], w_up[0], w_down[0]):
+        weights += [w, swap(tie(w, other_tokens))]
+
+    def collect(sums, *after):
         own, left, right, far = sums.reshape(SIDE, capacity, 2 * half)
+        own = tie(own, *after) if after else own
         return add(own, shift(left, True, -1), shift(right, True, 1), shift(far, True, 2))
 
-    line0 = spread(tie(z0, z1, *weights))
-    line1 = spread(tie(z1, line0))
+    own = tie(jnp.concatenate([z0, z1], axis=0), *weights)
+    ring = (own, shift(own, True, 1), shift(own, True, -1), shift(own, True, 2))
+    line0, line1 = [
+        jnp.concatenate([p[k * capacity:(k + 1) * capacity] for p in ring], axis=0) for k in range(2)
+    ]
+    hid = w_gate.shape[2]
+    down = tie(weights[5], own)
+    weights[5] = jnp.where(c == 0, down, jnp.concatenate([down[hid:], down[:hid]], axis=0))
     left0, right0 = both(line0, line0, False)
+    left1, right1 = both(line1, line1, False)
     (p_own0,) = ffn(core, weights, (line0,))
-    line1 = tie(line1, p_own0)
-    left1, right1 = both(line1, line1, False)
+    (p_own1,) = ffn(core, weights, (line1,))
+    left0, right0 = tie(left0, p_own0, p_own1), tie(right0, p_own0, p_own1)
     far_a0, far_b0 = far_pair(left0, right0, False)
     p_left0, p_right0 = ffn(core, weights, (left0, right0))
-    (p_own1,) = ffn(core, weights, (tie(line1, p_left0),))
-    far_a1, far_b1 = far_pair(tie(left1, p_own1), right1, False)
+    far_a1, far_b1 = far_pair(tie(left1, p_left0), tie(right1, p_left0), False)
     p_left1, p_right1 = ffn(core, weights, (left1, right1))
     pf_a0, pf_b0 = ffn(core, weights, (tie(far_a0, p_left1), far_b0))
     got_a0, got_b0 = both(pf_a0, pf_b0, False)
@@ -188,16 +189,19 @@
     sl1, sr1 = fold(p_left1, p_right1, got_a1, got_b1)
     from_l1, from_r1 = both(sr1, sl1, False)
     done0 = collect(add(p_own0, from_l0, from_r0))
-    done1 = collect(add(p_own1, from_l1, from_r1))
     back0 = lax.ppermute(done0, ("expert", "et"), [(b, a) for a, b in send[0]])
-    back1 = lax.ppermute(tie(done1, back0), ("expert", "et"), [(b, a) for a, b in send[1]])
-
-    total = jnp.zeros((tok_rows, 2 * half), F32)
-    for back, (pick, score) in zip((back0, back1), picks):
-        rows = lax.dot_general(pick, back, (((0,), (0,)), ((), ())), preferred_element_type=F32)
-        total = total + rows * score[:, None]
-    theirs = swap(total[:, half:].astype(BF))
-    return (total[:, :half] + theirs.astype(F32)).astype(BF)
+    done1 = collect(tie(add(p_own1, from_l1, from_r1), done0), back0)
+    back1 = lax.ppermute(done1, ("expert", "et"), [(b, a) for a, b in send[1]])
+
+    def combine(cols):
+        total = jnp.zeros((tok_rows, half), F32)
+        for back, (pick, score) in zip((back0, back1), picks):
+            rows = lax.dot_general(pick, back[:, cols], (((0,), (0,)), ((), ())), preferred_element_type=F32)
+            total = total + rows * score[:, None]
+        return total
+
+    theirs = swap(combine(slice(half, 2 * half)).astype(BF))
+    return (combine(slice(0, half)) + theirs.astype(F32)).astype(BF)
 
 
 def solution(mesh):

time: 138 us -> 134 us (0.971)
  waiting for transfers between devices: 64.9 us -> 53.9 us
  starting transfers between devices: 50.4 us -> 52.7 us
  local copies, waits for them, and re-layouts: 1.96 us -> 3.95 us
    ppermute x5, waiting for transfers between devices: 6.84 us -> 1.14 us  [swap(): return lax.ppermute(a, 'et', [(0, 1), (1, 0)])]
    ppermute x1, waiting for transfers between devices: 5.5 us -> 0.71 us  [on_device(): back0 = lax.ppermute(done0, ('expert', 'et'), [(b, a) for a, b in send[0]])]
    ppermute x5, starting transfers between devices: 2.02 us -> 5.57 us  [swap(): return lax.ppermute(a, 'et', [(0, 1), (1, 0)])]
    unnamed x13 -> x10, local copies, waits for them, and re-layouts: 0.08 us -> 1.96 us
    ppermute x28 -> x25, starting transfers between devices: 38.1 us -> 36.6 us  [shift(): return lax.ppermute(a, ('dp', 'et'), plane_perm(first, step))]
    ppermute x28 -> x25, waiting for transfers between devices: 43.1 us -> 43.2 us  [shift(): return lax.ppermute(a, ('dp', 'et'), plane_perm(first, step))]
  transfers between devices with their start and end apart: 37 -> 34, of which waited for: 22 -> 20; matrix products, arithmetic and copies ran while one was open for 5% -> 6% of each run, Pallas kernels for 10% -> 11%
where the time goes in v3:
time: 134 us
  waiting for transfers between devices  53.9 us (40%)
  starting transfers between devices  52.7 us (39%)
  Pallas kernels  14.3 us (11%)
  other arithmetic  5.14 us (4%)
  local copies, waits for them, and re-layouts  3.95 us (3%)
  matrix products  3.29 us (2%)
    ppermute x25, waiting for transfers between devices, shift(): return lax.ppermute(a, ('dp', 'et'), plane_perm(first, step))  43.2 us
    ppermute x25, starting transfers between devices, shift(): return lax.ppermute(a, ('dp', 'et'), plane_perm(first, step))  36.6 us
    pallas_call x6, Pallas kernels, ffn(): pl.pallas_call(ffn_body, in_specs=[pl.BlockSpec(memory_space=pltpu.SMEM)]...  14.3 us
    ppermute x2, waiting for transfers between devices, dispatch(): lax.ppermute(tie(rows, *after) if after else rows, ('expert', 'et'), send...  5.79 us
    ppermute x2, starting transfers between devices, dispatch(): lax.ppermute(tie(rows, *after) if after else rows, ('expert', 'et'), send...  5.74 us
    ppermute x5, starting transfers between devices, swap(): return lax.ppermute(a, 'et', [(0, 1), (1, 0)])  5.57 us
    ppermute x1, waiting for transfers between devices, on_device(): back1 = lax.ppermute(done1, ('expert', 'et'), [(b, a) for a, b in send[1]])  3.12 us
    ppermute x1, starting transfers between devices, on_device(): back1 = lax.ppermute(done1, ('expert', 'et'), [(b, a) for a, b in send[1]])  2.83 us
  transfers between devices with their start and end apart: 34, of which 20 were waited for; matrix products, arithmetic and copies ran while one was open for 6% of the time, Pallas kernels for 11%

profile of v3, /device:TPU:1, one launch (start us, length us, event | category | flops | bytes accessed | tf_op | source)
XLA Modules:
  0.0 133.7 jit_solution(366186293137117184)
XLA Ops:
  5.7 1.7 %collective-permute-start.5 = (bf16[40,3072]{1,0:T(8,128)(2,1)}, bf16[40,3072]{1,0:T(8,128)(2,1)}, u32[]{:S(2)}, u32[]{:S(2)}) collective-permute-start(bf16[40,3072]{1,0:T(8,128)(2,1)} %get-tuple-element.69), channel_id=1, source_target_pairs={{0,4},{2,6},{4,0},{6,2},{1,3},{3,5},{5,7},{7,1},{8,12},{10,14},{12... | collective-permute-start | bytes 737288 | tf_op jit(solution)/shard_map/ppermute | solution.py:144
  7.4 4.0 %collective-permute-start.4 = (bf16[40,3072]{1,0:T(8,128)(2,1)S(1)}, bf16[40,3072]{1,0:T(8,128)(2,1)}, u32[]{:S(2)}, u32[]{:S(2)}) collective-permute-start(bf16[40,3072]{1,0:T(8,128)(2,1)S(1)} %get-tuple-element.68), channel_id=1, source_target_pairs={{0,0},{2,2},{4,4},{6,6},{1,7},{3,1},{5,3},{7,5},{8,8},{10,10},{12,... | collective-permute-start | bytes 737288 | tf_op jit(solution)/shard_map/ppermute | solution.py:144
  11.4 4.6 %collective-permute-done.5 = bf16[40,3072]{1,0:T(8,128)(2,1)} collective-permute-done((bf16[40,3072]{1,0:T(8,128)(2,1)}, bf16[40,3072]{1,0:T(8,128)(2,1)}, u32[]{:S(2)}, u32[]{:S(2)}) %collective-permute-start.5) | collective-permute-done | bytes 245792 | tf_op jit(solution)/shard_map/ppermute | solution.py:144
  18.4 3.0 %collective-permute-start.8 = (bf16[80,3072]{1,0:T(8,128)(2,1)S(1)}, bf16[80,3072]{1,0:T(8,128)(2,1)S(1)}, u32[]{:S(2)}, u32[]{:S(2)}) collective-permute-start(bf16[80,3072]{1,0:T(8,128)(2,1)S(1)} %pad_maximum_fusion.6), channel_id=1, source_target_pairs={{0,16},{1,65},{8,24},{9,73},{16,0},{17,81},{24,8},{25,89},{32,48},... | collective-permute-start | bytes 1474568 | tf_op jit(solution)/shard_map/ppermute | solution.py:26
  24.3 3.4 %collective-permute-done.8 = bf16[80,3072]{1,0:T(8,128)(2,1)S(1)} collective-permute-done((bf16[80,3072]{1,0:T(8,128)(2,1)S(1)}, bf16[80,3072]{1,0:T(8,128)(2,1)S(1)}, u32[]{:S(2)}, u32[]{:S(2)}) %collective-permute-start.8) | collective-permute-done | bytes 491552 | tf_op jit(solution)/shard_map/ppermute | solution.py:26
  27.8 5.5 %collective-permute-done.7 = bf16[80,3072]{1,0:T(8,128)(2,1)S(1)} collective-permute-done((bf16[80,3072]{1,0:T(8,128)(2,1)S(1)}, bf16[80,3072]{1,0:T(8,128)(2,1)S(1)}, u32[]{:S(2)}, u32[]{:S(2)}) %collective-permute-start.7) | collective-permute-done | bytes 491552 | tf_op jit(solution)/shard_map/ppermute | solution.py:26
  36.3 2.7 %collective-permute-start.13 = (bf16[160,3072]{1,0:T(8,128)(2,1)S(1)}, bf16[160,3072]{1,0:T(8,128)(2,1)S(1)}, u32[]{:S(2)}, u32[]{:S(2)}) collective-permute-start(bf16[160,3072]{1,0:T(8,128)(2,1)S(1)} %pad_maximum_fusion.1.refs_6_), channel_id=1, source_target_pairs={{0,96},{1,25},{8,104},{9,1},{16,112},{17,9},{24,120},{25,17},{32,0... | collective-permute-start | bytes 2949128 | tf_op jit(solution)/shard_map/ppermute | solution.py:26
  41.4 1.8 %ffn.6 = bf16[160,3072]{1,0:T(8,128)(2,1)S(1)} custom-call(s32[1]{0:T(128)} %bitcast.2.core, bf16[3072,256]{1,0:T(8,128)(2,1)S(1)} %bitcast.21, bf16[3072,256]{1,0:T(8,128)(2,1)S(1)} %collective-permute-done.1.refs_1_, bf16[3072,256]{1,0:T(8,128)(2,1)S(1)} %bitcast.28, bf16[3072,256]{1,0:T(8,128)(2,1)S(1)} %collective-permute-done.2.refs_3_, ...), custom_call_target="tpu_custom_call" | custom-call | flops 1509949440 | bytes 11403264 | tf_op jit(solution)/shard_map/ffn/pallas_call | solution.py:95
  43.2 1.8 %ffn.7 = bf16[160,3072]{1,0:T(8,128)(2,1)S(1)} custom-call(s32[1]{0:T(128)} %bitcast.2.core, bf16[3072,256]{1,0:T(8,128)(2,1)S(1)} %bitcast.22, bf16[3072,256]{1,0:T(8,128)(2,1)S(1)} %collective-permute-done.1.refs_1_, bf16[3072,256]{1,0:T(8,128)(2,1)S(1)} %bitcast.29, bf16[3072,256]{1,0:T(8,128)(2,1)S(1)} %collective-permute-done.2.refs_3_, ...), custom_call_target="tpu_custom_call" | custom-call | flops 1509949440 | bytes 11403264 | tf_op jit(solution)/shard_map/ffn/pallas_call | solution.py:95
  45.0 2.9 %collective-permute-done.9.refs_6_ = bf16[160,3072]{1,0:T(8,128)(2,1)S(1)} collective-permute-done((bf16[160,3072]{1,0:T(8,128)(2,1)S(1)}, bf16[160,3072]{1,0:T(8,128)(2,1)S(1)}, u32[]{:S(2)}, u32[]{:S(2)}) %collective-permute-start.9) | collective-permute-done | bytes 983072 | tf_op jit(solution)/shard_map/ppermute | solution.py:26
  49.3 1.7 %collective-permute-start.14 = (bf16[160,1536]{1,0:T(8,128)(2,1)S(1)}, bf16[160,1536]{1,0:T(8,128)(2,1)S(1)}, u32[]{:S(2)}, u32[]{:S(2)}) collective-permute-start(bf16[160,1536]{1,0:T(8,128)(2,1)S(1)} %slice.106), channel_id=1, source_target_pairs={{0,96},{1,25},{8,104},{9,1},{16,112},{17,9},{24,120},{25,17},{32,0... | collective-permute-start | bytes 1474568 | tf_op jit(solution)/shard_map/ppermute | solution.py:26
  51.0 3.5 %ffn.8 = (bf16[160,3072]{1,0:T(8,128)(2,1)S(1)}, bf16[160,3072]{1,0:T(8,128)(2,1)S(1)}) custom-call(s32[1]{0:T(128)} %bitcast.2.core, bf16[3072,256]{1,0:T(8,128)(2,1)S(1)} %bitcast.23, bf16[3072,256]{1,0:T(8,128)(2,1)S(1)} %collective-permute-done.1.refs_1_, bf16[3072,256]{1,0:T(8,128)(2,1)S(1)} %bitcast.30, ...), custom_call_target="tpu_custom_call" | custom-call | flops 3019898880 | bytes 13369344 | tf_op jit(solution)/shard_map/ffn/pallas_call | solution.py:95
  54.5 4.0 %collective-permute-done.12.refs_6_ = bf16[160,3072]{1,0:T(8,128)(2,1)S(1)} collective-permute-done((bf16[160,3072]{1,0:T(8,128)(2,1)S(1)}, bf16[160,3072]{1,0:T(8,128)(2,1)S(1)}, u32[]{:S(2)}, u32[]{:S(2)}) %collective-permute-start.12) | collective-permute-done | bytes 983072 | tf_op jit(solution)/shard_map/ppermute | solution.py:26
  58.7 2.7 %collective-permute-start.24 = (bf16[160,1536]{1,0:T(8,128)(2,1)S(1)}, bf16[160,1536]{1,0:T(8,128)(2,1)S(1)}, u32[]{:S(2)}, u32[]{:S(2)}) collective-permute-start(bf16[160,1536]{1,0:T(8,128)(2,1)S(1)} %slice.113), channel_id=1, source_target_pairs={{0,96},{1,25},{8,104},{9,1},{16,112},{17,9},{24,120},{25,17},{32,0... | collective-permute-start | bytes 1474568 | tf_op jit(solution)/shard_map/ppermute | solution.py:26
  61.4 3.5 %ffn.9 = (bf16[160,3072]{1,0:T(8,128)(2,1)S(1)}, bf16[160,3072]{1,0:T(8,128)(2,1)S(1)}) custom-call(s32[1]{0:T(128)} %bitcast.2.core, bf16[3072,256]{1,0:T(8,128)(2,1)S(1)} %bitcast.24, bf16[3072,256]{1,0:T(8,128)(2,1)S(1)} %collective-permute-done.1.refs_1_, bf16[3072,256]{1,0:T(8,128)(2,1)S(1)} %bitcast.31, ...), custom_call_target="tpu_custom_call" | custom-call | flops 3019898880 | bytes 13369344 | tf_op jit(solution)/shard_map/ffn/pallas_call | solution.py:95
  64.9 1.8 %ffn.10 = (bf16[160,1536]{1,0:T(8,128)(2,1)S(1)}, bf16[160,1536]{1,0:T(8,128)(2,1)S(1)}) custom-call(s32[1]{0:T(128)} %bitcast.2.core, bf16[3072,256]{1,0:T(8,128)(2,1)S(1)} %bitcast.25, bf16[3072,256]{1,0:T(8,128)(2,1)S(1)} %collective-permute-done.1.refs_1_, bf16[3072,256]{1,0:T(8,128)(2,1)S(1)} %bitcast.32, ...), custom_call_target="tpu_custom_call" | custom-call | flops 1509949440 | bytes 11403264 | tf_op jit(solution)/shard_map/ffn/pallas_call | solution.py:95
  69.0 1.8 %ffn.11 = (bf16[160,1536]{1,0:T(8,128)(2,1)S(1)}, bf16[160,1536]{1,0:T(8,128)(2,1)S(1)}) custom-call(s32[1]{0:T(128)} %bitcast.2.core, bf16[3072,256]{1,0:T(8,128)(2,1)S(1)} %bitcast.26, bf16[3072,256]{1,0:T(8,128)(2,1)S(1)} %collective-permute-done.1.refs_1_, bf16[3072,256]{1,0:T(8,128)(2,1)S(1)} %bitcast.33, ...), custom_call_target="tpu_custom_call" | custom-call | flops 1509949440 | bytes 11403264 | tf_op jit(solution)/shard_map/ffn/pallas_call | solution.py:95
  70.9 2.5 %collective-permute-start.27 = (bf16[160,1536]{1,0:T(8,128)(2,1)S(1)}, bf16[160,1536]{1,0:T(8,128)(2,1)S(1)}, u32[]{:S(2)}, u32[]{:S(2)}) collective-permute-start(bf16[160,1536]{1,0:T(8,128)(2,1)S(1)} %get-tuple-element.44), channel_id=1, source_target_pairs={{0,96},{1,25},{8,104},{9,1},{16,112},{17,9},{24,120},{25,17},{32,0... | collective-permute-start | bytes 1474568 | tf_op jit(solution)/shard_map/ppermute | solution.py:26
  75.0 2.8 %collective-permute-start.18 = (bf16[160,3072]{1,0:T(8,128)(2,1)S(1)}, bf16[160,3072]{1,0:T(8,128)(2,1)S(1)}, u32[]{:S(2)}, u32[]{:S(2)}) collective-permute-start(bf16[160,3072]{1,0:T(8,128)(2,1)S(1)} %pad_maximum_fusion.3), channel_id=1, source_target_pairs={{0,96},{1,25},{8,104},{9,1},{16,112},{17,9},{24,120},{25,17},{32,0... | collective-permute-start | bytes 2949128 | tf_op jit(solution)/shard_map/ppermute | solution.py:26
  80.3 2.8 %collective-permute-start.28 = (bf16[160,3072]{1,0:T(8,128)(2,1)S(1)}, bf16[160,3072]{1,0:T(8,128)(2,1)S(1)}, u32[]{:S(2)}, u32[]{:S(2)}) collective-permute-start(bf16[160,3072]{1,0:T(8,128)(2,1)S(1)} %pad_maximum_fusion.5), channel_id=1, source_target_pairs={{0,96},{1,25},{8,104},{9,1},{16,112},{17,9},{24,120},{25,17},{32,0... | collective-permute-start | bytes 2949128 | tf_op jit(solution)/shard_map/ppermute | solution.py:26
  83.4 7.2 %collective-permute-done.18 = bf16[160,3072]{1,0:T(8,128)(2,1)S(1)} collective-permute-done((bf16[160,3072]{1,0:T(8,128)(2,1)S(1)}, bf16[160,3072]{1,0:T(8,128)(2,1)S(1)}, u32[]{:S(2)}, u32[]{:S(2)}) %collective-permute-start.18) | collective-permute-done | bytes 983072 | tf_op jit(solution)/shard_map/ppermute | solution.py:26
  90.6 3.0 %collective-permute-done.16 = bf16[160,3072]{1,0:T(8,128)(2,1)S(1)} collective-permute-done((bf16[160,3072]{1,0:T(8,128)(2,1)S(1)}, bf16[160,3072]{1,0:T(8,128)(2,1)S(1)}, u32[]{:S(2)}, u32[]{:S(2)}) %collective-permute-start.16) | collective-permute-done | bytes 983072 | tf_op jit(solution)/shard_map/ppermute | solution.py:26
  94.1 2.0 %collective-permute-start.21 = (bf16[40,3072]{1,0:T(8,128)(2,1)S(1)}, bf16[40,3072]{1,0:T(8,128)(2,1)S(1)}, u32[]{:S(2)}, u32[]{:S(2)}) collective-permute-start(bf16[40,3072]{1,0:T(8,128)(2,1)S(1)} %get-tuple-element.58), channel_id=1, source_target_pairs={{0,16},{1,65},{8,24},{9,73},{16,0},{17,81},{24,8},{25,89},{32,48},... | collective-permute-start | bytes 737288 | tf_op jit(solution)/shard_map/ppermute | solution.py:26
  98.7 4.3 %collective-permute-done.28 = bf16[160,3072]{1,0:T(8,128)(2,1)S(1)} collective-permute-done((bf16[160,3072]{1,0:T(8,128)(2,1)S(1)}, bf16[160,3072]{1,0:T(8,128)(2,1)S(1)}, u32[]{:S(2)}, u32[]{:S(2)}) %collective-permute-start.28) | collective-permute-done | bytes 983072 | tf_op jit(solution)/shard_map/ppermute | solution.py:26
  103.1 5.4 %collective-permute-done.26 = bf16[160,3072]{1,0:T(8,128)(2,1)S(1)} collective-permute-done((bf16[160,3072]{1,0:T(8,128)(2,1)S(1)}, bf16[160,3072]{1,0:T(8,128)(2,1)S(1)}, u32[]{:S(2)}, u32[]{:S(2)}) %collective-permute-start.26) | collective-permute-done | bytes 983072 | tf_op jit(solution)/shard_map/ppermute | solution.py:26
  109.2 1.9 %collective-permute-start.22 = (bf16[40,3072]{1,0:T(8,128)(2,1)S(1)}, bf16[40,3072]{1,0:T(8,128)(2,1)S(1)}, u32[]{:S(2)}, u32[]{:S(2)}) collective-permute-start(bf16[40,3072]{1,0:T(8,128)(2,1)S(1)} %add_convert_fusion.7), channel_id=1, source_target_pairs={{0,0},{2,2},{4,4},{6,6},{7,1},{1,3},{3,5},{5,7},{8,8},{10,10},{12,... | collective-permute-start | bytes 737288 | tf_op jit(solution)/shard_map/ppermute | solution.py:192
  111.2 3.3 %collective-permute-start.31 = (bf16[40,3072]{1,0:T(8,128)(2,1)S(1)}, bf16[40,3072]{1,0:T(8,128)(2,1)S(1)}, u32[]{:S(2)}, u32[]{:S(2)}) collective-permute-start(bf16[40,3072]{1,0:T(8,128)(2,1)S(1)} %get-tuple-element.54), channel_id=1, source_target_pairs={{0,16},{1,65},{8,24},{9,73},{16,0},{17,81},{24,8},{25,89},{32,48},... | collective-permute-start | bytes 737288 | tf_op jit(solution)/shard_map/ppermute | solution.py:26
  115.3 1.9 %collective-permute-start.29 = (bf16[40,3072]{1,0:T(8,128)(2,1)S(1)}, bf16[40,3072]{1,0:T(8,128)(2,1)S(1)}, u32[]{:S(2)}, u32[]{:S(2)}) collective-permute-start(bf16[40,3072]{1,0:T(8,128)(2,1)S(1)} %get-tuple-element.56), channel_id=1, source_target_pairs={{0,24},{1,97},{8,0},{9,105},{16,8},{17,113},{24,16},{25,121},{32,5... | collective-permute-start | bytes 737288 | tf_op jit(solution)/shard_map/ppermute | solution.py:26
  118.4 2.7 %collective-permute-done.30 = bf16[40,3072]{1,0:T(8,128)(2,1)S(1)} collective-permute-done((bf16[40,3072]{1,0:T(8,128)(2,1)S(1)}, bf16[40,3072]{1,0:T(8,128)(2,1)S(1)}, u32[]{:S(2)}, u32[]{:S(2)}) %collective-permute-start.30) | collective-permute-done | bytes 245792 | tf_op jit(solution)/shard_map/ppermute | solution.py:26
  121.9 2.8 %collective-permute-start.32 = (bf16[40,3072]{1,0:T(8,128)(2,1)S(1)}, bf16[40,3072]{1,0:T(8,128)(2,1)S(1)}, u32[]{:S(2)}, u32[]{:S(2)}) collective-permute-start(bf16[40,3072]{1,0:T(8,128)(2,1)S(1)} %add_convert_fusion.6), channel_id=1, source_target_pairs={{4,0},{6,2},{0,4},{2,6},{3,1},{5,3},{7,5},{1,7},{12,8},{14,10},{8,... | collective-permute-start | bytes 737288 | tf_op jit(solution)/shard_map/ppermute | solution.py:194
  124.8 3.1 %collective-permute-done.32 = bf16[40,3072]{1,0:T(8,128)(2,1)S(1)} collective-permute-done((bf16[40,3072]{1,0:T(8,128)(2,1)S(1)}, bf16[40,3072]{1,0:T(8,128)(2,1)S(1)}, u32[]{:S(2)}, u32[]{:S(2)}) %collective-permute-start.32) | collective-permute-done | bytes 245792 | tf_op jit(solution)/shard_map/ppermute | solution.py:194
  128.4 3.3 %collective-permute-start.33 = (bf16[64,1536]{1,0:T(8,128)(2,1)S(1)}, bf16[64,1536]{1,0:T(8,128)(2,1)S(1)}, u32[]{:S(2)}, u32[]{:S(2)}) collective-permute-start(bf16[64,1536]{1,0:T(8,128)(2,1)S(1)} %fusion.3), channel_id=1, source_target_pairs={{0,1},{1,0},{2,3},{3,2},{4,5},{5,4},{6,7},{7,6},{8,9},{9,8},{10,11... | collective-permute-start | bytes 589832 | tf_op jit(solution)/shard_map/ppermute | solution.py:30
  (95 shorter events, 33.6 us)
Async XLA Ops:
  2.7 15.6 %collective-permute-start.1 = (bf16[3072,256]{1,0:T(8,128)(2,1)}, bf16[3072,256]{1,0:T(8,128)(2,1)S(1)}, u32[]{:S(2)}, u32[]{:S(2)}) collective-permute-start(bf16[3072,256]{1,0:T(8,128)(2,1)} %bitcast.20), channel_id=1, source_target_pairs={{0,1},{1,0},{2,3},{3,2},{4,5},{5,4},{6,7},{7,6},{8,9},{9,8},{10,11... | collective-permute-start | bytes 4718600 | tf_op jit(solution)/shard_map/ppermute | solution.py:30
  3.1 15.3 %collective-permute-start.2 = (bf16[3072,256]{1,0:T(8,128)(2,1)}, bf16[3072,256]{1,0:T(8,128)(2,1)S(1)}, u32[]{:S(2)}, u32[]{:S(2)}) collective-permute-start(bf16[3072,256]{1,0:T(8,128)(2,1)} %bitcast.27), channel_id=1, source_target_pairs={{0,1},{1,0},{2,3},{3,2},{4,5},{5,4},{6,7},{7,6},{8,9},{9,8},{10,11... | collective-permute-start | bytes 4718600 | tf_op jit(solution)/shard_map/ppermute | solution.py:30
  3.2 15.1 %collective-permute-start.3 = (bf16[512,1536]{1,0:T(8,128)(2,1)}, bf16[512,1536]{1,0:T(8,128)(2,1)}, u32[]{:S(2)}, u32[]{:S(2)}) collective-permute-start(bf16[512,1536]{1,0:T(8,128)(2,1)} %bitcast.34), channel_id=1, source_target_pairs={{0,1},{1,0},{2,3},{3,2},{4,5},{5,4},{6,7},{7,6},{8,9},{9,8},{10,11... | collective-permute-start | bytes 4718600 | tf_op jit(solution)/shard_map/ppermute | solution.py:30
  5.7 10.4 %collective-permute-start.5 = (bf16[40,3072]{1,0:T(8,128)(2,1)}, bf16[40,3072]{1,0:T(8,128)(2,1)}, u32[]{:S(2)}, u32[]{:S(2)}) collective-permute-start(bf16[40,3072]{1,0:T(8,128)(2,1)} %get-tuple-element.69), channel_id=1, source_target_pairs={{0,4},{2,6},{4,0},{6,2},{1,3},{3,5},{5,7},{7,1},{8,12},{10,14},{12... | collective-permute-start | bytes 737288 | tf_op jit(solution)/shard_map/ppermute | solution.py:144
  7.4 9.8 %collective-permute-start.4 = (bf16[40,3072]{1,0:T(8,128)(2,1)S(1)}, bf16[40,3072]{1,0:T(8,128)(2,1)}, u32[]{:S(2)}, u32[]{:S(2)}) collective-permute-start(bf16[40,3072]{1,0:T(8,128)(2,1)S(1)} %get-tuple-element.68), channel_id=1, source_target_pairs={{0,0},{2,2},{4,4},{6,6},{1,7},{3,1},{5,3},{7,5},{8,8},{10,10},{12,... | collective-permute-start | bytes 737288 | tf_op jit(solution)/shard_map/ppermute | solution.py:144
  18.4 9.4 %collective-permute-start.8 = (bf16[80,3072]{1,0:T(8,128)(2,1)S(1)}, bf16[80,3072]{1,0:T(8,128)(2,1)S(1)}, u32[]{:S(2)}, u32[]{:S(2)}) collective-permute-start(bf16[80,3072]{1,0:T(8,128)(2,1)S(1)} %pad_maximum_fusion.6), channel_id=1, source_target_pairs={{0,16},{1,65},{8,24},{9,73},{16,0},{17,81},{24,8},{25,89},{32,48},... | collective-permute-start | bytes 1474568 | tf_op jit(solution)/shard_map/ppermute | solution.py:26
  21.3 11.9 %collective-permute-start.7 = (bf16[80,3072]{1,0:T(8,128)(2,1)S(1)}, bf16[80,3072]{1,0:T(8,128)(2,1)S(1)}, u32[]{:S(2)}, u32[]{:S(2)}) collective-permute-start(bf16[80,3072]{1,0:T(8,128)(2,1)S(1)} %pad_maximum_fusion.6), channel_id=1, source_target_pairs={{0,24},{1,97},{8,0},{9,105},{16,8},{17,113},{24,16},{25,121},{32,5... | collective-permute-start | bytes 1474568 | tf_op jit(solution)/shard_map/ppermute | solution.py:26
  22.1 11.2 %collective-permute-start.6 = (bf16[80,3072]{1,0:T(8,128)(2,1)S(1)}, bf16[80,3072]{1,0:T(8,128)(2,1)S(1)}, u32[]{:S(2)}, u32[]{:S(2)}) collective-permute-start(bf16[80,3072]{1,0:T(8,128)(2,1)S(1)} %pad_maximum_fusion.6), channel_id=1, source_target_pairs={{0,8},{1,33},{8,16},{9,41},{16,24},{17,49},{24,0},{25,57},{32,40},... | collective-permute-start | bytes 1474568 | tf_op jit(solution)/shard_map/ppermute | solution.py:26
  33.4 14.5 %collective-permute-start.9 = (bf16[160,3072]{1,0:T(8,128)(2,1)S(1)}, bf16[160,3072]{1,0:T(8,128)(2,1)S(1)}, u32[]{:S(2)}, u32[]{:S(2)}) collective-permute-start(bf16[160,3072]{1,0:T(8,128)(2,1)S(1)} %pad_maximum_fusion.refs_6_), channel_id=1, source_target_pairs={{0,32},{1,9},{8,40},{9,17},{16,48},{17,25},{24,56},{25,1},{32,64},... | collective-permute-start | bytes 2949128 | tf_op jit(solution)/shard_map/ppermute | solution.py:26
  34.7 13.2 %collective-permute-start.10 = (bf16[160,3072]{1,0:T(8,128)(2,1)S(1)}, bf16[160,3072]{1,0:T(8,128)(2,1)S(1)}, u32[]{:S(2)}, u32[]{:S(2)}) collective-permute-start(bf16[160,3072]{1,0:T(8,128)(2,1)S(1)} %pad_maximum_fusion.refs_6_), channel_id=1, source_target_pairs={{0,96},{1,25},{8,104},{9,1},{16,112},{17,9},{24,120},{25,17},{32,0... | collective-permute-start | bytes 2949128 | tf_op jit(solution)/shard_map/ppermute | solution.py:26
  36.2 22.2 %collective-permute-start.12 = (bf16[160,3072]{1,0:T(8,128)(2,1)S(1)}, bf16[160,3072]{1,0:T(8,128)(2,1)S(1)}, u32[]{:S(2)}, u32[]{:S(2)}) collective-permute-start(bf16[160,3072]{1,0:T(8,128)(2,1)S(1)} %pad_maximum_fusion.1.refs_6_), channel_id=1, source_target_pairs={{0,32},{1,9},{8,40},{9,17},{16,48},{17,25},{24,56},{25,1},{32,64},... | collective-permute-start | bytes 2949128 | tf_op jit(solution)/shard_map/ppermute | solution.py:26
  36.3 22.3 %collective-permute-start.13 = (bf16[160,3072]{1,0:T(8,128)(2,1)S(1)}, bf16[160,3072]{1,0:T(8,128)(2,1)S(1)}, u32[]{:S(2)}, u32[]{:S(2)}) collective-permute-start(bf16[160,3072]{1,0:T(8,128)(2,1)S(1)} %pad_maximum_fusion.1.refs_6_), channel_id=1, source_target_pairs={{0,96},{1,25},{8,104},{9,1},{16,112},{17,9},{24,120},{25,17},{32,0... | collective-permute-start | bytes 2949128 | tf_op jit(solution)/shard_map/ppermute | solution.py:26
  48.0 16.9 %collective-permute-start.11 = (bf16[160,1536]{1,0:T(8,128)(2,1)S(1)}, bf16[160,1536]{1,0:T(8,128)(2,1)S(1)}, u32[]{:S(2)}, u32[]{:S(2)}) collective-permute-start(bf16[160,1536]{1,0:T(8,128)(2,1)S(1)} %slice.105), channel_id=1, source_target_pairs={{0,32},{1,9},{8,40},{9,17},{16,48},{17,25},{24,56},{25,1},{32,64},... | collective-permute-start | bytes 1474568 | tf_op jit(solution)/shard_map/ppermute | solution.py:26
  49.3 15.6 %collective-permute-start.14 = (bf16[160,1536]{1,0:T(8,128)(2,1)S(1)}, bf16[160,1536]{1,0:T(8,128)(2,1)S(1)}, u32[]{:S(2)}, u32[]{:S(2)}) collective-permute-start(bf16[160,1536]{1,0:T(8,128)(2,1)S(1)} %slice.106), channel_id=1, source_target_pairs={{0,96},{1,25},{8,104},{9,1},{16,112},{17,9},{24,120},{25,17},{32,0... | collective-permute-start | bytes 1474568 | tf_op jit(solution)/shard_map/ppermute | solution.py:26
  58.5 10.5 %collective-permute-start.23 = (bf16[160,1536]{1,0:T(8,128)(2,1)S(1)}, bf16[160,1536]{1,0:T(8,128)(2,1)S(1)}, u32[]{:S(2)}, u32[]{:S(2)}) collective-permute-start(bf16[160,1536]{1,0:T(8,128)(2,1)S(1)} %slice.112), channel_id=1, source_target_pairs={{0,32},{1,9},{8,40},{9,17},{16,48},{17,25},{24,56},{25,1},{32,64},... | collective-permute-start | bytes 1474568 | tf_op jit(solution)/shard_map/ppermute | solution.py:26
  58.7 10.4 %collective-permute-start.24 = (bf16[160,1536]{1,0:T(8,128)(2,1)S(1)}, bf16[160,1536]{1,0:T(8,128)(2,1)S(1)}, u32[]{:S(2)}, u32[]{:S(2)}) collective-permute-start(bf16[160,1536]{1,0:T(8,128)(2,1)S(1)} %slice.113), channel_id=1, source_target_pairs={{0,96},{1,25},{8,104},{9,1},{16,112},{17,9},{24,120},{25,17},{32,0... | collective-permute-start | bytes 1474568 | tf_op jit(solution)/shard_map/ppermute | solution.py:26
  66.7 8.0 %collective-permute-start.17 = (bf16[160,1536]{1,0:T(8,128)(2,1)S(1)}, bf16[160,1536]{1,0:T(8,128)(2,1)S(1)}, u32[]{:S(2)}, u32[]{:S(2)}) collective-permute-start(bf16[160,1536]{1,0:T(8,128)(2,1)S(1)} %get-tuple-element.38), channel_id=1, source_target_pairs={{0,96},{1,25},{8,104},{9,1},{16,112},{17,9},{24,120},{25,17},{32,0... | collective-permute-start | bytes 1474568 | tf_op jit(solution)/shard_map/ppermute | solution.py:26
  68.5 9.3 %collective-permute-start.15 = (bf16[160,1536]{1,0:T(8,128)(2,1)S(1)}, bf16[160,1536]{1,0:T(8,128)(2,1)S(1)}, u32[]{:S(2)}, u32[]{:S(2)}) collective-permute-start(bf16[160,1536]{1,0:T(8,128)(2,1)S(1)} %get-tuple-element.36), channel_id=1, source_target_pairs={{0,32},{1,9},{8,40},{9,17},{16,48},{17,25},{24,56},{25,1},{32,64},... | collective-permute-start | bytes 1474568 | tf_op jit(solution)/shard_map/ppermute | solution.py:26
  70.9 9.2 %collective-permute-start.27 = (bf16[160,1536]{1,0:T(8,128)(2,1)S(1)}, bf16[160,1536]{1,0:T(8,128)(2,1)S(1)}, u32[]{:S(2)}, u32[]{:S(2)}) collective-permute-start(bf16[160,1536]{1,0:T(8,128)(2,1)S(1)} %get-tuple-element.44), channel_id=1, source_target_pairs={{0,96},{1,25},{8,104},{9,1},{16,112},{17,9},{24,120},{25,17},{32,0... | collective-permute-start | bytes 1474568 | tf_op jit(solution)/shard_map/ppermute | solution.py:26
  73.4 9.7 %collective-permute-start.25 = (bf16[160,1536]{1,0:T(8,128)(2,1)S(1)}, bf16[160,1536]{1,0:T(8,128)(2,1)S(1)}, u32[]{:S(2)}, u32[]{:S(2)}) collective-permute-start(bf16[160,1536]{1,0:T(8,128)(2,1)S(1)} %get-tuple-element.43), channel_id=1, source_target_pairs={{0,32},{1,9},{8,40},{9,17},{16,48},{17,25},{24,56},{25,1},{32,64},... | collective-permute-start | bytes 1474568 | tf_op jit(solution)/shard_map/ppermute | solution.py:26
  75.0 15.6 %collective-permute-start.18 = (bf16[160,3072]{1,0:T(8,128)(2,1)S(1)}, bf16[160,3072]{1,0:T(8,128)(2,1)S(1)}, u32[]{:S(2)}, u32[]{:S(2)}) collective-permute-start(bf16[160,3072]{1,0:T(8,128)(2,1)S(1)} %pad_maximum_fusion.3), channel_id=1, source_target_pairs={{0,96},{1,25},{8,104},{9,1},{16,112},{17,9},{24,120},{25,17},{32,0... | collective-permute-start | bytes 2949128 | tf_op jit(solution)/shard_map/ppermute | solution.py:26
  78.0 15.5 %collective-permute-start.16 = (bf16[160,3072]{1,0:T(8,128)(2,1)S(1)}, bf16[160,3072]{1,0:T(8,128)(2,1)S(1)}, u32[]{:S(2)}, u32[]{:S(2)}) collective-permute-start(bf16[160,3072]{1,0:T(8,128)(2,1)S(1)} %pad_maximum_fusion.2), channel_id=1, source_target_pairs={{0,32},{1,9},{8,40},{9,17},{16,48},{17,25},{24,56},{25,1},{32,64},... | collective-permute-start | bytes 2949128 | tf_op jit(solution)/shard_map/ppermute | solution.py:26
  80.3 22.8 %collective-permute-start.28 = (bf16[160,3072]{1,0:T(8,128)(2,1)S(1)}, bf16[160,3072]{1,0:T(8,128)(2,1)S(1)}, u32[]{:S(2)}, u32[]{:S(2)}) collective-permute-start(bf16[160,3072]{1,0:T(8,128)(2,1)S(1)} %pad_maximum_fusion.5), channel_id=1, source_target_pairs={{0,96},{1,25},{8,104},{9,1},{16,112},{17,9},{24,120},{25,17},{32,0... | collective-permute-start | bytes 2949128 | tf_op jit(solution)/shard_map/ppermute | solution.py:26
  83.3 25.2 %collective-permute-start.26 = (bf16[160,3072]{1,0:T(8,128)(2,1)S(1)}, bf16[160,3072]{1,0:T(8,128)(2,1)S(1)}, u32[]{:S(2)}, u32[]{:S(2)}) collective-permute-start(bf16[160,3072]{1,0:T(8,128)(2,1)S(1)} %pad_maximum_fusion.4), channel_id=1, source_target_pairs={{0,32},{1,9},{8,40},{9,17},{16,48},{17,25},{24,56},{25,1},{32,64},... | collective-permute-start | bytes 2949128 | tf_op jit(solution)/shard_map/ppermute | solution.py:26
  94.1 14.9 %collective-permute-start.21 = (bf16[40,3072]{1,0:T(8,128)(2,1)S(1)}, bf16[40,3072]{1,0:T(8,128)(2,1)S(1)}, u32[]{:S(2)}, u32[]{:S(2)}) collective-permute-start(bf16[40,3072]{1,0:T(8,128)(2,1)S(1)} %get-tuple-element.58), channel_id=1, source_target_pairs={{0,16},{1,65},{8,24},{9,73},{16,0},{17,81},{24,8},{25,89},{32,48},... | collective-permute-start | bytes 737288 | tf_op jit(solution)/shard_map/ppermute | solution.py:26
  96.1 13.0 %collective-permute-start.20 = (bf16[40,3072]{1,0:T(8,128)(2,1)S(1)}, bf16[40,3072]{1,0:T(8,128)(2,1)S(1)}, u32[]{:S(2)}, u32[]{:S(2)}) collective-permute-start(bf16[40,3072]{1,0:T(8,128)(2,1)S(1)} %get-tuple-element.59), channel_id=1, source_target_pairs={{0,8},{1,33},{8,16},{9,41},{16,24},{17,49},{24,0},{25,57},{32,40},... | collective-permute-start | bytes 737288 | tf_op jit(solution)/shard_map/ppermute | solution.py:26
  97.1 11.9 %collective-permute-start.19 = (bf16[40,3072]{1,0:T(8,128)(2,1)S(1)}, bf16[40,3072]{1,0:T(8,128)(2,1)S(1)}, u32[]{:S(2)}, u32[]{:S(2)}) collective-permute-start(bf16[40,3072]{1,0:T(8,128)(2,1)S(1)} %get-tuple-element.57), channel_id=1, source_target_pairs={{0,24},{1,97},{8,0},{9,105},{16,8},{17,113},{24,16},{25,121},{32,5... | collective-permute-start | bytes 737288 | tf_op jit(solution)/shard_map/ppermute | solution.py:26
  109.2 8.7 %collective-permute-start.22 = (bf16[40,3072]{1,0:T(8,128)(2,1)S(1)}, bf16[40,3072]{1,0:T(8,128)(2,1)S(1)}, u32[]{:S(2)}, u32[]{:S(2)}) collective-permute-start(bf16[40,3072]{1,0:T(8,128)(2,1)S(1)} %add_convert_fusion.7), channel_id=1, source_target_pairs={{0,0},{2,2},{4,4},{6,6},{7,1},{1,3},{3,5},{5,7},{8,8},{10,10},{12,... | collective-permute-start | bytes 737288 | tf_op jit(solution)/shard_map/ppermute | solution.py:192
  111.2 7.2 %collective-permute-start.31 = (bf16[40,3072]{1,0:T(8,128)(2,1)S(1)}, bf16[40,3072]{1,0:T(8,128)(2,1)S(1)}, u32[]{:S(2)}, u32[]{:S(2)}) collective-permute-start(bf16[40,3072]{1,0:T(8,128)(2,1)S(1)} %get-tuple-element.54), channel_id=1, source_target_pairs={{0,16},{1,65},{8,24},{9,73},{16,0},{17,81},{24,8},{25,89},{32,48},... | collective-permute-start | bytes 737288 | tf_op jit(solution)/shard_map/ppermute | solution.py:26
  114.5 6.6 %collective-permute-start.30 = (bf16[40,3072]{1,0:T(8,128)(2,1)S(1)}, bf16[40,3072]{1,0:T(8,128)(2,1)S(1)}, u32[]{:S(2)}, u32[]{:S(2)}) collective-permute-start(bf16[40,3072]{1,0:T(8,128)(2,1)S(1)} %get-tuple-element.55), channel_id=1, source_target_pairs={{0,8},{1,33},{8,16},{9,41},{16,24},{17,49},{24,0},{25,57},{32,40},... | collective-permute-start | bytes 737288 | tf_op jit(solution)/shard_map/ppermute | solution.py:26
  115.3 6.5 %collective-permute-start.29 = (bf16[40,3072]{1,0:T(8,128)(2,1)S(1)}, bf16[40,3072]{1,0:T(8,128)(2,1)S(1)}, u32[]{:S(2)}, u32[]{:S(2)}) collective-permute-start(bf16[40,3072]{1,0:T(8,128)(2,1)S(1)} %get-tuple-element.56), channel_id=1, source_target_pairs={{0,24},{1,97},{8,0},{9,105},{16,8},{17,113},{24,16},{25,121},{32,5... | collective-permute-start | bytes 737288 | tf_op jit(solution)/shard_map/ppermute | solution.py:26
  121.9 6.0 %collective-permute-start.32 = (bf16[40,3072]{1,0:T(8,128)(2,1)S(1)}, bf16[40,3072]{1,0:T(8,128)(2,1)S(1)}, u32[]{:S(2)}, u32[]{:S(2)}) collective-permute-start(bf16[40,3072]{1,0:T(8,128)(2,1)S(1)} %add_convert_fusion.6), channel_id=1, source_target_pairs={{4,0},{6,2},{0,4},{2,6},{3,1},{5,3},{7,5},{1,7},{12,8},{14,10},{8,... | collective-permute-start | bytes 737288 | tf_op jit(solution)/shard_map/ppermute | solution.py:194
  (7 other events, 43.9 us)

commit v4 on v3

--- a/solution.py
+++ b/solution.py
@@ -128,11 +128,11 @@
         return pick.astype(BF), jnp.sum(jnp.where(named, gate_scores, 0.0), axis=1)
 
     send = [
-        [(s * 2, s * 2) for s in range(n_expert)] + [(s * 2 + 1, (s - 1) % n_expert * 2 + 1) for s in range(n_expert)],
         [(s * 2, (s + 2) % n_expert * 2) for s in range(n_expert)]
         + [(s * 2 + 1, (s + 1) % n_expert * 2 + 1) for s in range(n_expert)],
+        [(s * 2, s * 2) for s in range(n_expert)] + [(s * 2 + 1, (s - 1) % n_expert * 2 + 1) for s in range(n_expert)],
     ]
-    picks = [choose((z - c) % n_expert), choose((z + 2 - c) % n_expert)]
+    picks = [choose((z + 2 - c) % n_expert), choose((z - c) % n_expert)]
 
     pick_all = jnp.concatenate([pick for pick, _ in picks], axis=0)
     outgoing = jnp.concatenate(
@@ -152,8 +152,8 @@
             jnp.concatenate([add(right[:, :half], got_a), right[:, half:]], axis=1),
         )
 
+    z1 = dispatch(1)
     z0 = dispatch(0)
-    z1 = dispatch(1)
     weights = []
     for w in (w_gate[0], w_up[0], w_down[0]):
         weights += [w, swap(tie(w, other_tokens))]
@@ -163,10 +163,10 @@
         own = tie(own, *after) if after else own
         return add(own, shift(left, True, -1), shift(right, True, 1), shift(far, True, 2))
 
-    own = tie(jnp.concatenate([z0, z1], axis=0), *weights)
+    own = tie(jnp.concatenate([z1, z0], axis=0), *weights)
     ring = (own, shift(own, True, 1), shift(own, True, -1), shift(own, True, 2))
     line0, line1 = [
-        jnp.concatenate([p[k * capacity:(k + 1) * capacity] for p in ring], axis=0) for k in range(2)
+        jnp.concatenate([p[k * capacity:(k + 1) * capacity] for p in ring], axis=0) for k in (1, 0)
     ]
     hid = w_gate.shape[2]
     down = tie(weights[5], own)

time: 134 us -> 134 us (level)
  waiting for transfers between devices: 53.9 us -> 57.6 us
  starting transfers between devices: 52.7 us -> 49.2 us
    ppermute x5, starting transfers between devices: 5.57 us -> 2.39 us  [swap(): return lax.ppermute(a, 'et', [(0, 1), (1, 0)])]
    ppermute x1, waiting for transfers between devices: 3.12 us -> 6.18 us  [on_device(): back1 = lax.ppermute(done1, ('expert', 'et'), [(b, a) for a, b in send[1]])]
  transfers between devices with their start and end apart: 34 -> 34, of which waited for: 20 -> 19; matrix products, arithmetic and copies ran while one was open for 6% -> 6% of each run, Pallas kernels for 11% -> 11%
where the time goes in v4:
time: 134 us
  waiting for transfers between devices  57.6 us (43%)
  starting transfers between devices  49.2 us (37%)
  Pallas kernels  14.3 us (11%)
  other arithmetic  5.14 us (4%)
  local copies, waits for them, and re-layouts  3.95 us (3%)
  matrix products  3.3 us (2%)
    ppermute x25, waiting for transfers between devices, shift(): return lax.ppermute(a, ('dp', 'et'), plane_perm(first, step))  44.1 us
    ppermute x25, starting transfers between devices, shift(): return lax.ppermute(a, ('dp', 'et'), plane_perm(first, step))  36.1 us
    pallas_call x6, Pallas kernels, ffn(): pl.pallas_call(ffn_body, in_specs=[pl.BlockSpec(memory_space=pltpu.SMEM)]...  14.3 us
    ppermute x1, waiting for transfers between devices, on_device(): back1 = lax.ppermute(done1, ('expert', 'et'), [(b, a) for a, b in send[1]])  6.18 us
    ppermute x2, waiting for transfers between devices, dispatch(): lax.ppermute(tie(rows, *after) if after else rows, ('expert', 'et'), send...  5.79 us
    ppermute x2, starting transfers between devices, dispatch(): lax.ppermute(tie(rows, *after) if after else rows, ('expert', 'et'), send...  5.74 us
    ppermute x1, starting transfers between devices, on_device(): back0 = lax.ppermute(done0, ('expert', 'et'), [(b, a) for a, b in send[0]])  3.03 us
  transfers between devices with their start and end apart: 34, of which 19 were waited for; matrix products, arithmetic and copies ran while one was open for 6% of the time, Pallas kernels for 11%

profile of v4, /device:TPU:1, one launch (start us, length us, event | category | flops | bytes accessed | tf_op | source)
XLA Modules:
  0.0 134.0 jit_solution(3355824192837915610)
XLA Ops:
  5.7 1.7 %collective-permute-start.5 = (bf16[40,3072]{1,0:T(8,128)(2,1)}, bf16[40,3072]{1,0:T(8,128)(2,1)}, u32[]{:S(2)}, u32[]{:S(2)}) collective-permute-start(bf16[40,3072]{1,0:T(8,128)(2,1)} %get-tuple-element.69), channel_id=1, source_target_pairs={{0,4},{2,6},{4,0},{6,2},{1,3},{3,5},{5,7},{7,1},{8,12},{10,14},{12... | collective-permute-start | bytes 737288 | tf_op jit(solution)/shard_map/ppermute | solution.py:144
  7.4 4.0 %collective-permute-start.4 = (bf16[40,3072]{1,0:T(8,128)(2,1)S(1)}, bf16[40,3072]{1,0:T(8,128)(2,1)}, u32[]{:S(2)}, u32[]{:S(2)}) collective-permute-start(bf16[40,3072]{1,0:T(8,128)(2,1)S(1)} %get-tuple-element.68), channel_id=1, source_target_pairs={{0,0},{2,2},{4,4},{6,6},{1,7},{3,1},{5,3},{7,5},{8,8},{10,10},{12,... | collective-permute-start | bytes 737288 | tf_op jit(solution)/shard_map/ppermute | solution.py:144
  11.4 4.6 %collective-permute-done.5 = bf16[40,3072]{1,0:T(8,128)(2,1)} collective-permute-done((bf16[40,3072]{1,0:T(8,128)(2,1)}, bf16[40,3072]{1,0:T(8,128)(2,1)}, u32[]{:S(2)}, u32[]{:S(2)}) %collective-permute-start.5) | collective-permute-done | bytes 245792 | tf_op jit(solution)/shard_map/ppermute | solution.py:144
  18.4 3.0 %collective-permute-start.8 = (bf16[80,3072]{1,0:T(8,128)(2,1)S(1)}, bf16[80,3072]{1,0:T(8,128)(2,1)S(1)}, u32[]{:S(2)}, u32[]{:S(2)}) collective-permute-start(bf16[80,3072]{1,0:T(8,128)(2,1)S(1)} %pad_maximum_fusion.6), channel_id=1, source_target_pairs={{0,16},{1,65},{8,24},{9,73},{16,0},{17,81},{24,8},{25,89},{32,48},... | collective-permute-start | bytes 1474568 | tf_op jit(solution)/shard_map/ppermute | solution.py:26
  24.3 3.4 %collective-permute-done.8 = bf16[80,3072]{1,0:T(8,128)(2,1)S(1)} collective-permute-done((bf16[80,3072]{1,0:T(8,128)(2,1)S(1)}, bf16[80,3072]{1,0:T(8,128)(2,1)S(1)}, u32[]{:S(2)}, u32[]{:S(2)}) %collective-permute-start.8) | collective-permute-done | bytes 491552 | tf_op jit(solution)/shard_map/ppermute | solution.py:26
  27.8 5.5 %collective-permute-done.7 = bf16[80,3072]{1,0:T(8,128)(2,1)S(1)} collective-permute-done((bf16[80,3072]{1,0:T(8,128)(2,1)S(1)}, bf16[80,3072]{1,0:T(8,128)(2,1)S(1)}, u32[]{:S(2)}, u32[]{:S(2)}) %collective-permute-start.7) | collective-permute-done | bytes 491552 | tf_op jit(solution)/shard_map/ppermute | solution.py:26
  36.3 2.7 %collective-permute-start.13 = (bf16[160,3072]{1,0:T(8,128)(2,1)S(1)}, bf16[160,3072]{1,0:T(8,128)(2,1)S(1)}, u32[]{:S(2)}, u32[]{:S(2)}) collective-permute-start(bf16[160,3072]{1,0:T(8,128)(2,1)S(1)} %pad_maximum_fusion.1.refs_6_), channel_id=1, source_target_pairs={{0,96},{1,25},{8,104},{9,1},{16,112},{17,9},{24,120},{25,17},{32,0... | collective-permute-start | bytes 2949128 | tf_op jit(solution)/shard_map/ppermute | solution.py:26
  41.4 1.8 %ffn.6 = bf16[160,3072]{1,0:T(8,128)(2,1)S(1)} custom-call(s32[1]{0:T(128)} %bitcast.2.core, bf16[3072,256]{1,0:T(8,128)(2,1)S(1)} %bitcast.21, bf16[3072,256]{1,0:T(8,128)(2,1)S(1)} %collective-permute-done.1.refs_1_, bf16[3072,256]{1,0:T(8,128)(2,1)S(1)} %bitcast.28, bf16[3072,256]{1,0:T(8,128)(2,1)S(1)} %collective-permute-done.2.refs_3_, ...), custom_call_target="tpu_custom_call" | custom-call | flops 1509949440 | bytes 11403264 | tf_op jit(solution)/shard_map/ffn/pallas_call | solution.py:95
  43.2 1.8 %ffn.7 = bf16[160,3072]{1,0:T(8,128)(2,1)S(1)} custom-call(s32[1]{0:T(128)} %bitcast.2.core, bf16[3072,256]{1,0:T(8,128)(2,1)S(1)} %bitcast.22, bf16[3072,256]{1,0:T(8,128)(2,1)S(1)} %collective-permute-done.1.refs_1_, bf16[3072,256]{1,0:T(8,128)(2,1)S(1)} %bitcast.29, bf16[3072,256]{1,0:T(8,128)(2,1)S(1)} %collective-permute-done.2.refs_3_, ...), custom_call_target="tpu_custom_call" | custom-call | flops 1509949440 | bytes 11403264 | tf_op jit(solution)/shard_map/ffn/pallas_call | solution.py:95
  45.0 2.9 %collective-permute-done.9.refs_6_ = bf16[160,3072]{1,0:T(8,128)(2,1)S(1)} collective-permute-done((bf16[160,3072]{1,0:T(8,128)(2,1)S(1)}, bf16[160,3072]{1,0:T(8,128)(2,1)S(1)}, u32[]{:S(2)}, u32[]{:S(2)}) %collective-permute-start.9) | collective-permute-done | bytes 983072 | tf_op jit(solution)/shard_map/ppermute | solution.py:26
  49.3 1.7 %collective-permute-start.14 = (bf16[160,1536]{1,0:T(8,128)(2,1)S(1)}, bf16[160,1536]{1,0:T(8,128)(2,1)S(1)}, u32[]{:S(2)}, u32[]{:S(2)}) collective-permute-start(bf16[160,1536]{1,0:T(8,128)(2,1)S(1)} %slice.106), channel_id=1, source_target_pairs={{0,96},{1,25},{8,104},{9,1},{16,112},{17,9},{24,120},{25,17},{32,0... | collective-permute-start | bytes 1474568 | tf_op jit(solution)/shard_map/ppermute | solution.py:26
  51.0 3.5 %ffn.8 = (bf16[160,3072]{1,0:T(8,128)(2,1)S(1)}, bf16[160,3072]{1,0:T(8,128)(2,1)S(1)}) custom-call(s32[1]{0:T(128)} %bitcast.2.core, bf16[3072,256]{1,0:T(8,128)(2,1)S(1)} %bitcast.23, bf16[3072,256]{1,0:T(8,128)(2,1)S(1)} %collective-permute-done.1.refs_1_, bf16[3072,256]{1,0:T(8,128)(2,1)S(1)} %bitcast.30, ...), custom_call_target="tpu_custom_call" | custom-call | flops 3019898880 | bytes 13369344 | tf_op jit(solution)/shard_map/ffn/pallas_call | solution.py:95
  54.5 4.0 %collective-permute-done.12.refs_6_ = bf16[160,3072]{1,0:T(8,128)(2,1)S(1)} collective-permute-done((bf16[160,3072]{1,0:T(8,128)(2,1)S(1)}, bf16[160,3072]{1,0:T(8,128)(2,1)S(1)}, u32[]{:S(2)}, u32[]{:S(2)}) %collective-permute-start.12) | collective-permute-done | bytes 983072 | tf_op jit(solution)/shard_map/ppermute | solution.py:26
  58.7 2.7 %collective-permute-start.24 = (bf16[160,1536]{1,0:T(8,128)(2,1)S(1)}, bf16[160,1536]{1,0:T(8,128)(2,1)S(1)}, u32[]{:S(2)}, u32[]{:S(2)}) collective-permute-start(bf16[160,1536]{1,0:T(8,128)(2,1)S(1)} %slice.113), channel_id=1, source_target_pairs={{0,96},{1,25},{8,104},{9,1},{16,112},{17,9},{24,120},{25,17},{32,0... | collective-permute-start | bytes 1474568 | tf_op jit(solution)/shard_map/ppermute | solution.py:26
  61.4 3.5 %ffn.9 = (bf16[160,3072]{1,0:T(8,128)(2,1)S(1)}, bf16[160,3072]{1,0:T(8,128)(2,1)S(1)}) custom-call(s32[1]{0:T(128)} %bitcast.2.core, bf16[3072,256]{1,0:T(8,128)(2,1)S(1)} %bitcast.24, bf16[3072,256]{1,0:T(8,128)(2,1)S(1)} %collective-permute-done.1.refs_1_, bf16[3072,256]{1,0:T(8,128)(2,1)S(1)} %bitcast.31, ...), custom_call_target="tpu_custom_call" | custom-call | flops 3019898880 | bytes 13369344 | tf_op jit(solution)/shard_map/ffn/pallas_call | solution.py:95
  64.9 1.8 %ffn.10 = (bf16[160,1536]{1,0:T(8,128)(2,1)S(1)}, bf16[160,1536]{1,0:T(8,128)(2,1)S(1)}) custom-call(s32[1]{0:T(128)} %bitcast.2.core, bf16[3072,256]{1,0:T(8,128)(2,1)S(1)} %bitcast.25, bf16[3072,256]{1,0:T(8,128)(2,1)S(1)} %collective-permute-done.1.refs_1_, bf16[3072,256]{1,0:T(8,128)(2,1)S(1)} %bitcast.32, ...), custom_call_target="tpu_custom_call" | custom-call | flops 1509949440 | bytes 11403264 | tf_op jit(solution)/shard_map/ffn/pallas_call | solution.py:95
  69.0 1.8 %ffn.11 = (bf16[160,1536]{1,0:T(8,128)(2,1)S(1)}, bf16[160,1536]{1,0:T(8,128)(2,1)S(1)}) custom-call(s32[1]{0:T(128)} %bitcast.2.core, bf16[3072,256]{1,0:T(8,128)(2,1)S(1)} %bitcast.26, bf16[3072,256]{1,0:T(8,128)(2,1)S(1)} %collective-permute-done.1.refs_1_, bf16[3072,256]{1,0:T(8,128)(2,1)S(1)} %bitcast.33, ...), custom_call_target="tpu_custom_call" | custom-call | flops 1509949440 | bytes 11403264 | tf_op jit(solution)/shard_map/ffn/pallas_call | solution.py:95
  70.9 2.5 %collective-permute-start.27 = (bf16[160,1536]{1,0:T(8,128)(2,1)S(1)}, bf16[160,1536]{1,0:T(8,128)(2,1)S(1)}, u32[]{:S(2)}, u32[]{:S(2)}) collective-permute-start(bf16[160,1536]{1,0:T(8,128)(2,1)S(1)} %get-tuple-element.44), channel_id=1, source_target_pairs={{0,96},{1,25},{8,104},{9,1},{16,112},{17,9},{24,120},{25,17},{32,0... | collective-permute-start | bytes 1474568 | tf_op jit(solution)/shard_map/ppermute | solution.py:26
  75.0 2.8 %collective-permute-start.18 = (bf16[160,3072]{1,0:T(8,128)(2,1)S(1)}, bf16[160,3072]{1,0:T(8,128)(2,1)S(1)}, u32[]{:S(2)}, u32[]{:S(2)}) collective-permute-start(bf16[160,3072]{1,0:T(8,128)(2,1)S(1)} %pad_maximum_fusion.3), channel_id=1, source_target_pairs={{0,96},{1,25},{8,104},{9,1},{16,112},{17,9},{24,120},{25,17},{32,0... | collective-permute-start | bytes 2949128 | tf_op jit(solution)/shard_map/ppermute | solution.py:26
  78.3 1.7 %collective-permute-done.27 = bf16[160,1536]{1,0:T(8,128)(2,1)S(1)} collective-permute-done((bf16[160,1536]{1,0:T(8,128)(2,1)S(1)}, bf16[160,1536]{1,0:T(8,128)(2,1)S(1)}, u32[]{:S(2)}, u32[]{:S(2)}) %collective-permute-start.27) | collective-permute-done | bytes 491552 | tf_op jit(solution)/shard_map/ppermute | solution.py:26
  80.3 2.8 %collective-permute-start.28 = (bf16[160,3072]{1,0:T(8,128)(2,1)S(1)}, bf16[160,3072]{1,0:T(8,128)(2,1)S(1)}, u32[]{:S(2)}, u32[]{:S(2)}) collective-permute-start(bf16[160,3072]{1,0:T(8,128)(2,1)S(1)} %pad_maximum_fusion.5), channel_id=1, source_target_pairs={{0,96},{1,25},{8,104},{9,1},{16,112},{17,9},{24,120},{25,17},{32,0... | collective-permute-start | bytes 2949128 | tf_op jit(solution)/shard_map/ppermute | solution.py:26
  83.4 7.2 %collective-permute-done.18 = bf16[160,3072]{1,0:T(8,128)(2,1)S(1)} collective-permute-done((bf16[160,3072]{1,0:T(8,128)(2,1)S(1)}, bf16[160,3072]{1,0:T(8,128)(2,1)S(1)}, u32[]{:S(2)}, u32[]{:S(2)}) %collective-permute-start.18) | collective-permute-done | bytes 983072 | tf_op jit(solution)/shard_map/ppermute | solution.py:26
  90.6 3.0 %collective-permute-done.16 = bf16[160,3072]{1,0:T(8,128)(2,1)S(1)} collective-permute-done((bf16[160,3072]{1,0:T(8,128)(2,1)S(1)}, bf16[160,3072]{1,0:T(8,128)(2,1)S(1)}, u32[]{:S(2)}, u32[]{:S(2)}) %collective-permute-start.16) | collective-permute-done | bytes 983072 | tf_op jit(solution)/shard_map/ppermute | solution.py:26
  94.1 2.0 %collective-permute-start.21 = (bf16[40,3072]{1,0:T(8,128)(2,1)S(1)}, bf16[40,3072]{1,0:T(8,128)(2,1)S(1)}, u32[]{:S(2)}, u32[]{:S(2)}) collective-permute-start(bf16[40,3072]{1,0:T(8,128)(2,1)S(1)} %get-tuple-element.58), channel_id=1, source_target_pairs={{0,16},{1,65},{8,24},{9,73},{16,0},{17,81},{24,8},{25,89},{32,48},... | collective-permute-start | bytes 737288 | tf_op jit(solution)/shard_map/ppermute | solution.py:26
  98.7 4.3 %collective-permute-done.28 = bf16[160,3072]{1,0:T(8,128)(2,1)S(1)} collective-permute-done((bf16[160,3072]{1,0:T(8,128)(2,1)S(1)}, bf16[160,3072]{1,0:T(8,128)(2,1)S(1)}, u32[]{:S(2)}, u32[]{:S(2)}) %collective-permute-start.28) | collective-permute-done | bytes 983072 | tf_op jit(solution)/shard_map/ppermute | solution.py:26
  103.1 5.4 %collective-permute-done.26 = bf16[160,3072]{1,0:T(8,128)(2,1)S(1)} collective-permute-done((bf16[160,3072]{1,0:T(8,128)(2,1)S(1)}, bf16[160,3072]{1,0:T(8,128)(2,1)S(1)}, u32[]{:S(2)}, u32[]{:S(2)}) %collective-permute-start.26) | collective-permute-done | bytes 983072 | tf_op jit(solution)/shard_map/ppermute | solution.py:26
  109.2 3.0 %collective-permute-start.22 = (bf16[40,3072]{1,0:T(8,128)(2,1)S(1)}, bf16[40,3072]{1,0:T(8,128)(2,1)S(1)}, u32[]{:S(2)}, u32[]{:S(2)}) collective-permute-start(bf16[40,3072]{1,0:T(8,128)(2,1)S(1)} %add_convert_fusion.7), channel_id=1, source_target_pairs={{4,0},{6,2},{0,4},{2,6},{3,1},{5,3},{7,5},{1,7},{12,8},{14,10},{8,... | collective-permute-start | bytes 737288 | tf_op jit(solution)/shard_map/ppermute | solution.py:192
  112.3 2.9 %collective-permute-start.31 = (bf16[40,3072]{1,0:T(8,128)(2,1)S(1)}, bf16[40,3072]{1,0:T(8,128)(2,1)S(1)}, u32[]{:S(2)}, u32[]{:S(2)}) collective-permute-start(bf16[40,3072]{1,0:T(8,128)(2,1)S(1)} %get-tuple-element.54), channel_id=1, source_target_pairs={{0,16},{1,65},{8,24},{9,73},{16,0},{17,81},{24,8},{25,89},{32,48},... | collective-permute-start | bytes 737288 | tf_op jit(solution)/shard_map/ppermute | solution.py:26
  116.2 1.7 %collective-permute-start.29 = (bf16[40,3072]{1,0:T(8,128)(2,1)S(1)}, bf16[40,3072]{1,0:T(8,128)(2,1)S(1)}, u32[]{:S(2)}, u32[]{:S(2)}) collective-permute-start(bf16[40,3072]{1,0:T(8,128)(2,1)S(1)} %get-tuple-element.56), channel_id=1, source_target_pairs={{0,24},{1,97},{8,0},{9,105},{16,8},{17,113},{24,16},{25,121},{32,5... | collective-permute-start | bytes 737288 | tf_op jit(solution)/shard_map/ppermute | solution.py:26
  119.2 2.6 %collective-permute-done.30 = bf16[40,3072]{1,0:T(8,128)(2,1)S(1)} collective-permute-done((bf16[40,3072]{1,0:T(8,128)(2,1)S(1)}, bf16[40,3072]{1,0:T(8,128)(2,1)S(1)}, u32[]{:S(2)}, u32[]{:S(2)}) %collective-permute-start.30) | collective-permute-done | bytes 245792 | tf_op jit(solution)/shard_map/ppermute | solution.py:26
  122.8 1.9 %collective-permute-start.32 = (bf16[40,3072]{1,0:T(8,128)(2,1)S(1)}, bf16[40,3072]{1,0:T(8,128)(2,1)S(1)}, u32[]{:S(2)}, u32[]{:S(2)}) collective-permute-start(bf16[40,3072]{1,0:T(8,128)(2,1)S(1)} %add_convert_fusion.6), channel_id=1, source_target_pairs={{0,0},{2,2},{4,4},{6,6},{7,1},{1,3},{3,5},{5,7},{8,8},{10,10},{12,... | collective-permute-start | bytes 737288 | tf_op jit(solution)/shard_map/ppermute | solution.py:194
  124.8 6.2 %collective-permute-done.32 = bf16[40,3072]{1,0:T(8,128)(2,1)S(1)} collective-permute-done((bf16[40,3072]{1,0:T(8,128)(2,1)S(1)}, bf16[40,3072]{1,0:T(8,128)(2,1)S(1)}, u32[]{:S(2)}, u32[]{:S(2)}) %collective-permute-start.32) | collective-permute-done | bytes 245792 | tf_op jit(solution)/shard_map/ppermute | solution.py:194
  (95 shorter events, 32.9 us)
Async XLA Ops:
  2.7 15.6 %collective-permute-start.1 = (bf16[3072,256]{1,0:T(8,128)(2,1)}, bf16[3072,256]{1,0:T(8,128)(2,1)S(1)}, u32[]{:S(2)}, u32[]{:S(2)}) collective-permute-start(bf16[3072,256]{1,0:T(8,128)(2,1)} %bitcast.20), channel_id=1, source_target_pairs={{0,1},{1,0},{2,3},{3,2},{4,5},{5,4},{6,7},{7,6},{8,9},{9,8},{10,11... | collective-permute-start | bytes 4718600 | tf_op jit(solution)/shard_map/ppermute | solution.py:30
  3.1 15.3 %collective-permute-start.2 = (bf16[3072,256]{1,0:T(8,128)(2,1)}, bf16[3072,256]{1,0:T(8,128)(2,1)S(1)}, u32[]{:S(2)}, u32[]{:S(2)}) collective-permute-start(bf16[3072,256]{1,0:T(8,128)(2,1)} %bitcast.27), channel_id=1, source_target_pairs={{0,1},{1,0},{2,3},{3,2},{4,5},{5,4},{6,7},{7,6},{8,9},{9,8},{10,11... | collective-permute-start | bytes 4718600 | tf_op jit(solution)/shard_map/ppermute | solution.py:30
  3.2 15.1 %collective-permute-start.3 = (bf16[512,1536]{1,0:T(8,128)(2,1)}, bf16[512,1536]{1,0:T(8,128)(2,1)}, u32[]{:S(2)}, u32[]{:S(2)}) collective-permute-start(bf16[512,1536]{1,0:T(8,128)(2,1)} %bitcast.34), channel_id=1, source_target_pairs={{0,1},{1,0},{2,3},{3,2},{4,5},{5,4},{6,7},{7,6},{8,9},{9,8},{10,11... | collective-permute-start | bytes 4718600 | tf_op jit(solution)/shard_map/ppermute | solution.py:30
  5.7 10.4 %collective-permute-start.5 = (bf16[40,3072]{1,0:T(8,128)(2,1)}, bf16[40,3072]{1,0:T(8,128)(2,1)}, u32[]{:S(2)}, u32[]{:S(2)}) collective-permute-start(bf16[40,3072]{1,0:T(8,128)(2,1)} %get-tuple-element.69), channel_id=1, source_target_pairs={{0,4},{2,6},{4,0},{6,2},{1,3},{3,5},{5,7},{7,1},{8,12},{10,14},{12... | collective-permute-start | bytes 737288 | tf_op jit(solution)/shard_map/ppermute | solution.py:144
  7.4 9.8 %collective-permute-start.4 = (bf16[40,3072]{1,0:T(8,128)(2,1)S(1)}, bf16[40,3072]{1,0:T(8,128)(2,1)}, u32[]{:S(2)}, u32[]{:S(2)}) collective-permute-start(bf16[40,3072]{1,0:T(8,128)(2,1)S(1)} %get-tuple-element.68), channel_id=1, source_target_pairs={{0,0},{2,2},{4,4},{6,6},{1,7},{3,1},{5,3},{7,5},{8,8},{10,10},{12,... | collective-permute-start | bytes 737288 | tf_op jit(solution)/shard_map/ppermute | solution.py:144
  18.4 9.4 %collective-permute-start.8 = (bf16[80,3072]{1,0:T(8,128)(2,1)S(1)}, bf16[80,3072]{1,0:T(8,128)(2,1)S(1)}, u32[]{:S(2)}, u32[]{:S(2)}) collective-permute-start(bf16[80,3072]{1,0:T(8,128)(2,1)S(1)} %pad_maximum_fusion.6), channel_id=1, source_target_pairs={{0,16},{1,65},{8,24},{9,73},{16,0},{17,81},{24,8},{25,89},{32,48},... | collective-permute-start | bytes 1474568 | tf_op jit(solution)/shard_map/ppermute | solution.py:26
  21.3 11.9 %collective-permute-start.7 = (bf16[80,3072]{1,0:T(8,128)(2,1)S(1)}, bf16[80,3072]{1,0:T(8,128)(2,1)S(1)}, u32[]{:S(2)}, u32[]{:S(2)}) collective-permute-start(bf16[80,3072]{1,0:T(8,128)(2,1)S(1)} %pad_maximum_fusion.6), channel_id=1, source_target_pairs={{0,24},{1,97},{8,0},{9,105},{16,8},{17,113},{24,16},{25,121},{32,5... | collective-permute-start | bytes 1474568 | tf_op jit(solution)/shard_map/ppermute | solution.py:26
  22.1 11.2 %collective-permute-start.6 = (bf16[80,3072]{1,0:T(8,128)(2,1)S(1)}, bf16[80,3072]{1,0:T(8,128)(2,1)S(1)}, u32[]{:S(2)}, u32[]{:S(2)}) collective-permute-start(bf16[80,3072]{1,0:T(8,128)(2,1)S(1)} %pad_maximum_fusion.6), channel_id=1, source_target_pairs={{0,8},{1,33},{8,16},{9,41},{16,24},{17,49},{24,0},{25,57},{32,40},... | collective-permute-start | bytes 1474568 | tf_op jit(solution)/shard_map/ppermute | solution.py:26
  33.4 14.5 %collective-permute-start.9 = (bf16[160,3072]{1,0:T(8,128)(2,1)S(1)}, bf16[160,3072]{1,0:T(8,128)(2,1)S(1)}, u32[]{:S(2)}, u32[]{:S(2)}) collective-permute-start(bf16[160,3072]{1,0:T(8,128)(2,1)S(1)} %pad_maximum_fusion.refs_6_), channel_id=1, source_target_pairs={{0,32},{1,9},{8,40},{9,17},{16,48},{17,25},{24,56},{25,1},{32,64},... | collective-permute-start | bytes 2949128 | tf_op jit(solution)/shard_map/ppermute | solution.py:26
  34.7 13.2 %collective-permute-start.10 = (bf16[160,3072]{1,0:T(8,128)(2,1)S(1)}, bf16[160,3072]{1,0:T(8,128)(2,1)S(1)}, u32[]{:S(2)}, u32[]{:S(2)}) collective-permute-start(bf16[160,3072]{1,0:T(8,128)(2,1)S(1)} %pad_maximum_fusion.refs_6_), channel_id=1, source_target_pairs={{0,96},{1,25},{8,104},{9,1},{16,112},{17,9},{24,120},{25,17},{32,0... | collective-permute-start | bytes 2949128 | tf_op jit(solution)/shard_map/ppermute | solution.py:26
  36.2 22.2 %collective-permute-start.12 = (bf16[160,3072]{1,0:T(8,128)(2,1)S(1)}, bf16[160,3072]{1,0:T(8,128)(2,1)S(1)}, u32[]{:S(2)}, u32[]{:S(2)}) collective-permute-start(bf16[160,3072]{1,0:T(8,128)(2,1)S(1)} %pad_maximum_fusion.1.refs_6_), channel_id=1, source_target_pairs={{0,32},{1,9},{8,40},{9,17},{16,48},{17,25},{24,56},{25,1},{32,64},... | collective-permute-start | bytes 2949128 | tf_op jit(solution)/shard_map/ppermute | solution.py:26
  36.3 22.3 %collective-permute-start.13 = (bf16[160,3072]{1,0:T(8,128)(2,1)S(1)}, bf16[160,3072]{1,0:T(8,128)(2,1)S(1)}, u32[]{:S(2)}, u32[]{:S(2)}) collective-permute-start(bf16[160,3072]{1,0:T(8,128)(2,1)S(1)} %pad_maximum_fusion.1.refs_6_), channel_id=1, source_target_pairs={{0,96},{1,25},{8,104},{9,1},{16,112},{17,9},{24,120},{25,17},{32,0... | collective-permute-start | bytes 2949128 | tf_op jit(solution)/shard_map/ppermute | solution.py:26
  48.0 16.9 %collective-permute-start.11 = (bf16[160,1536]{1,0:T(8,128)(2,1)S(1)}, bf16[160,1536]{1,0:T(8,128)(2,1)S(1)}, u32[]{:S(2)}, u32[]{:S(2)}) collective-permute-start(bf16[160,1536]{1,0:T(8,128)(2,1)S(1)} %slice.105), channel_id=1, source_target_pairs={{0,32},{1,9},{8,40},{9,17},{16,48},{17,25},{24,56},{25,1},{32,64},... | collective-permute-start | bytes 1474568 | tf_op jit(solution)/shard_map/ppermute | solution.py:26
  49.3 15.6 %collective-permute-start.14 = (bf16[160,1536]{1,0:T(8,128)(2,1)S(1)}, bf16[160,1536]{1,0:T(8,128)(2,1)S(1)}, u32[]{:S(2)}, u32[]{:S(2)}) collective-permute-start(bf16[160,1536]{1,0:T(8,128)(2,1)S(1)} %slice.106), channel_id=1, source_target_pairs={{0,96},{1,25},{8,104},{9,1},{16,112},{17,9},{24,120},{25,17},{32,0... | collective-permute-start | bytes 1474568 | tf_op jit(solution)/shard_map/ppermute | solution.py:26
  58.5 10.5 %collective-permute-start.23 = (bf16[160,1536]{1,0:T(8,128)(2,1)S(1)}, bf16[160,1536]{1,0:T(8,128)(2,1)S(1)}, u32[]{:S(2)}, u32[]{:S(2)}) collective-permute-start(bf16[160,1536]{1,0:T(8,128)(2,1)S(1)} %slice.112), channel_id=1, source_target_pairs={{0,32},{1,9},{8,40},{9,17},{16,48},{17,25},{24,56},{25,1},{32,64},... | collective-permute-start | bytes 1474568 | tf_op jit(solution)/shard_map/ppermute | solution.py:26
  58.7 10.4 %collective-permute-start.24 = (bf16[160,1536]{1,0:T(8,128)(2,1)S(1)}, bf16[160,1536]{1,0:T(8,128)(2,1)S(1)}, u32[]{:S(2)}, u32[]{:S(2)}) collective-permute-start(bf16[160,1536]{1,0:T(8,128)(2,1)S(1)} %slice.113), channel_id=1, source_target_pairs={{0,96},{1,25},{8,104},{9,1},{16,112},{17,9},{24,120},{25,17},{32,0... | collective-permute-start | bytes 1474568 | tf_op jit(solution)/shard_map/ppermute | solution.py:26
  66.7 8.0 %collective-permute-start.17 = (bf16[160,1536]{1,0:T(8,128)(2,1)S(1)}, bf16[160,1536]{1,0:T(8,128)(2,1)S(1)}, u32[]{:S(2)}, u32[]{:S(2)}) collective-permute-start(bf16[160,1536]{1,0:T(8,128)(2,1)S(1)} %get-tuple-element.38), channel_id=1, source_target_pairs={{0,96},{1,25},{8,104},{9,1},{16,112},{17,9},{24,120},{25,17},{32,0... | collective-permute-start | bytes 1474568 | tf_op jit(solution)/shard_map/ppermute | solution.py:26
  68.5 9.3 %collective-permute-start.15 = (bf16[160,1536]{1,0:T(8,128)(2,1)S(1)}, bf16[160,1536]{1,0:T(8,128)(2,1)S(1)}, u32[]{:S(2)}, u32[]{:S(2)}) collective-permute-start(bf16[160,1536]{1,0:T(8,128)(2,1)S(1)} %get-tuple-element.36), channel_id=1, source_target_pairs={{0,32},{1,9},{8,40},{9,17},{16,48},{17,25},{24,56},{25,1},{32,64},... | collective-permute-start | bytes 1474568 | tf_op jit(solution)/shard_map/ppermute | solution.py:26
  70.9 9.2 %collective-permute-start.27 = (bf16[160,1536]{1,0:T(8,128)(2,1)S(1)}, bf16[160,1536]{1,0:T(8,128)(2,1)S(1)}, u32[]{:S(2)}, u32[]{:S(2)}) collective-permute-start(bf16[160,1536]{1,0:T(8,128)(2,1)S(1)} %get-tuple-element.44), channel_id=1, source_target_pairs={{0,96},{1,25},{8,104},{9,1},{16,112},{17,9},{24,120},{25,17},{32,0... | collective-permute-start | bytes 1474568 | tf_op jit(solution)/shard_map/ppermute | solution.py:26
  73.4 9.7 %collective-permute-start.25 = (bf16[160,1536]{1,0:T(8,128)(2,1)S(1)}, bf16[160,1536]{1,0:T(8,128)(2,1)S(1)}, u32[]{:S(2)}, u32[]{:S(2)}) collective-permute-start(bf16[160,1536]{1,0:T(8,128)(2,1)S(1)} %get-tuple-element.43), channel_id=1, source_target_pairs={{0,32},{1,9},{8,40},{9,17},{16,48},{17,25},{24,56},{25,1},{32,64},... | collective-permute-start | bytes 1474568 | tf_op jit(solution)/shard_map/ppermute | solution.py:26
  75.0 15.6 %collective-permute-start.18 = (bf16[160,3072]{1,0:T(8,128)(2,1)S(1)}, bf16[160,3072]{1,0:T(8,128)(2,1)S(1)}, u32[]{:S(2)}, u32[]{:S(2)}) collective-permute-start(bf16[160,3072]{1,0:T(8,128)(2,1)S(1)} %pad_maximum_fusion.3), channel_id=1, source_target_pairs={{0,96},{1,25},{8,104},{9,1},{16,112},{17,9},{24,120},{25,17},{32,0... | collective-permute-start | bytes 2949128 | tf_op jit(solution)/shard_map/ppermute | solution.py:26
  78.0 15.5 %collective-permute-start.16 = (bf16[160,3072]{1,0:T(8,128)(2,1)S(1)}, bf16[160,3072]{1,0:T(8,128)(2,1)S(1)}, u32[]{:S(2)}, u32[]{:S(2)}) collective-permute-start(bf16[160,3072]{1,0:T(8,128)(2,1)S(1)} %pad_maximum_fusion.2), channel_id=1, source_target_pairs={{0,32},{1,9},{8,40},{9,17},{16,48},{17,25},{24,56},{25,1},{32,64},... | collective-permute-start | bytes 2949128 | tf_op jit(solution)/shard_map/ppermute | solution.py:26
  80.3 22.8 %collective-permute-start.28 = (bf16[160,3072]{1,0:T(8,128)(2,1)S(1)}, bf16[160,3072]{1,0:T(8,128)(2,1)S(1)}, u32[]{:S(2)}, u32[]{:S(2)}) collective-permute-start(bf16[160,3072]{1,0:T(8,128)(2,1)S(1)} %pad_maximum_fusion.5), channel_id=1, source_target_pairs={{0,96},{1,25},{8,104},{9,1},{16,112},{17,9},{24,120},{25,17},{32,0... | collective-permute-start | bytes 2949128 | tf_op jit(solution)/shard_map/ppermute | solution.py:26
  83.3 25.2 %collective-permute-start.26 = (bf16[160,3072]{1,0:T(8,128)(2,1)S(1)}, bf16[160,3072]{1,0:T(8,128)(2,1)S(1)}, u32[]{:S(2)}, u32[]{:S(2)}) collective-permute-start(bf16[160,3072]{1,0:T(8,128)(2,1)S(1)} %pad_maximum_fusion.4), channel_id=1, source_target_pairs={{0,32},{1,9},{8,40},{9,17},{16,48},{17,25},{24,56},{25,1},{32,64},... | collective-permute-start | bytes 2949128 | tf_op jit(solution)/shard_map/ppermute | solution.py:26
  94.1 14.9 %collective-permute-start.21 = (bf16[40,3072]{1,0:T(8,128)(2,1)S(1)}, bf16[40,3072]{1,0:T(8,128)(2,1)S(1)}, u32[]{:S(2)}, u32[]{:S(2)}) collective-permute-start(bf16[40,3072]{1,0:T(8,128)(2,1)S(1)} %get-tuple-element.58), channel_id=1, source_target_pairs={{0,16},{1,65},{8,24},{9,73},{16,0},{17,81},{24,8},{25,89},{32,48},... | collective-permute-start | bytes 737288 | tf_op jit(solution)/shard_map/ppermute | solution.py:26
  96.1 13.0 %collective-permute-start.20 = (bf16[40,3072]{1,0:T(8,128)(2,1)S(1)}, bf16[40,3072]{1,0:T(8,128)(2,1)S(1)}, u32[]{:S(2)}, u32[]{:S(2)}) collective-permute-start(bf16[40,3072]{1,0:T(8,128)(2,1)S(1)} %get-tuple-element.59), channel_id=1, source_target_pairs={{0,8},{1,33},{8,16},{9,41},{16,24},{17,49},{24,0},{25,57},{32,40},... | collective-permute-start | bytes 737288 | tf_op jit(solution)/shard_map/ppermute | solution.py:26
  97.1 11.9 %collective-permute-start.19 = (bf16[40,3072]{1,0:T(8,128)(2,1)S(1)}, bf16[40,3072]{1,0:T(8,128)(2,1)S(1)}, u32[]{:S(2)}, u32[]{:S(2)}) collective-permute-start(bf16[40,3072]{1,0:T(8,128)(2,1)S(1)} %get-tuple-element.57), channel_id=1, source_target_pairs={{0,24},{1,97},{8,0},{9,105},{16,8},{17,113},{24,16},{25,121},{32,5... | collective-permute-start | bytes 737288 | tf_op jit(solution)/shard_map/ppermute | solution.py:26
  109.2 8.7 %collective-permute-start.22 = (bf16[40,3072]{1,0:T(8,128)(2,1)S(1)}, bf16[40,3072]{1,0:T(8,128)(2,1)S(1)}, u32[]{:S(2)}, u32[]{:S(2)}) collective-permute-start(bf16[40,3072]{1,0:T(8,128)(2,1)S(1)} %add_convert_fusion.7), channel_id=1, source_target_pairs={{4,0},{6,2},{0,4},{2,6},{3,1},{5,3},{7,5},{1,7},{12,8},{14,10},{8,... | collective-permute-start | bytes 737288 | tf_op jit(solution)/shard_map/ppermute | solution.py:192
  112.3 6.9 %collective-permute-start.31 = (bf16[40,3072]{1,0:T(8,128)(2,1)S(1)}, bf16[40,3072]{1,0:T(8,128)(2,1)S(1)}, u32[]{:S(2)}, u32[]{:S(2)}) collective-permute-start(bf16[40,3072]{1,0:T(8,128)(2,1)S(1)} %get-tuple-element.54), channel_id=1, source_target_pairs={{0,16},{1,65},{8,24},{9,73},{16,0},{17,81},{24,8},{25,89},{32,48},... | collective-permute-start | bytes 737288 | tf_op jit(solution)/shard_map/ppermute | solution.py:26
  115.2 6.7 %collective-permute-start.30 = (bf16[40,3072]{1,0:T(8,128)(2,1)S(1)}, bf16[40,3072]{1,0:T(8,128)(2,1)S(1)}, u32[]{:S(2)}, u32[]{:S(2)}) collective-permute-start(bf16[40,3072]{1,0:T(8,128)(2,1)S(1)} %get-tuple-element.55), channel_id=1, source_target_pairs={{0,8},{1,33},{8,16},{9,41},{16,24},{17,49},{24,0},{25,57},{32,40},... | collective-permute-start | bytes 737288 | tf_op jit(solution)/shard_map/ppermute | solution.py:26
  116.2 6.5 %collective-permute-start.29 = (bf16[40,3072]{1,0:T(8,128)(2,1)S(1)}, bf16[40,3072]{1,0:T(8,128)(2,1)S(1)}, u32[]{:S(2)}, u32[]{:S(2)}) collective-permute-start(bf16[40,3072]{1,0:T(8,128)(2,1)S(1)} %get-tuple-element.56), channel_id=1, source_target_pairs={{0,24},{1,97},{8,0},{9,105},{16,8},{17,113},{24,16},{25,121},{32,5... | collective-permute-start | bytes 737288 | tf_op jit(solution)/shard_map/ppermute | solution.py:26
  122.8 8.2 %collective-permute-start.32 = (bf16[40,3072]{1,0:T(8,128)(2,1)S(1)}, bf16[40,3072]{1,0:T(8,128)(2,1)S(1)}, u32[]{:S(2)}, u32[]{:S(2)}) collective-permute-start(bf16[40,3072]{1,0:T(8,128)(2,1)S(1)} %add_convert_fusion.6), channel_id=1, source_target_pairs={{0,0},{2,2},{4,4},{6,6},{7,1},{1,3},{3,5},{5,7},{8,8},{10,10},{12,... | collective-permute-start | bytes 737288 | tf_op jit(solution)/shard_map/ppermute | solution.py:194
  (7 other events, 41.1 us)

commit v5 on v4

--- a/solution.py
+++ b/solution.py
@@ -191,17 +191,19 @@
     done0 = collect(add(p_own0, from_l0, from_r0))
     back0 = lax.ppermute(done0, ("expert", "et"), [(b, a) for a, b in send[0]])
     done1 = collect(tie(add(p_own1, from_l1, from_r1), done0), back0)
-    back1 = lax.ppermute(done1, ("expert", "et"), [(b, a) for a, b in send[1]])
-
-    def combine(cols):
-        total = jnp.zeros((tok_rows, half), F32)
-        for back, (pick, score) in zip((back0, back1), picks):
-            rows = lax.dot_general(pick, back[:, cols], (((0,), (0,)), ((), ())), preferred_element_type=F32)
-            total = total + rows * score[:, None]
-        return total
-
-    theirs = swap(combine(slice(half, 2 * half)).astype(BF))
-    return (combine(slice(0, half)) + theirs.astype(F32)).astype(BF)
+    def combine(back, choice):
+        pick, score = choice
+        rows = lax.dot_general(pick, back, (((0,), (0,)), ((), ())), preferred_element_type=F32)
+        return rows * score[:, None]
+
+    theirs = swap(combine(back0[:, half:], picks[0]).astype(BF))
+    done1 = tie(done1, theirs)
+    kept = lax.ppermute(done1[:, :half], ("expert", "et"), [(b, a) for a, b in send[1]])
+    crossed = lax.ppermute(done1[:, half:], ("expert", "et"), [(b, a ^ 1) for a, b in send[1]])
+
+    total = combine(back0[:, :half], picks[0]) + theirs.astype(F32)
+    total = total + combine(kept, picks[1]) + combine(crossed, choose((z - 1 + c) % n_expert))
+    return total.astype(BF)
 
 
 def solution(mesh):

time: 134 us -> 136 us (1.015)
  starting transfers between devices: 49.2 us -> 59.1 us
  waiting for transfers between devices: 57.6 us -> 49 us
    ppermute x1 -> x2, starting transfers between devices: 1.92 us -> 9.3 us  [the longest x1 7.75 us: on_device(): lax.ppermute(done1[:, :half], ('expert', 'et'), [(b, a) for a, b in send[...]
    ppermute x1 -> x2, waiting for transfers between devices: 6.18 us -> 1.61 us  [the longest x1 1.43 us: on_device(): lax.ppermute(done1[:, half:], ('expert', 'et'), [(b, a ^ 1) for a, b in s...]
    ppermute x25, waiting for transfers between devices: 44.1 us -> 41.3 us  [shift(): return lax.ppermute(a, ('dp', 'et'), plane_perm(first, step))]
    ppermute x5, starting transfers between devices: 2.39 us -> 4.85 us  [swap(): return lax.ppermute(a, 'et', [(0, 1), (1, 0)])]
  transfers between devices with their start and end apart: 34 -> 35, of which waited for: 19 -> 18; matrix products, arithmetic and copies ran while one was open for 6% -> 7% of each run, Pallas kernels for 11% -> 11%
where the time goes in v5:
time: 136 us; the launch traced here: 135 us
  starting transfers between devices  59.1 us (43%)
  waiting for transfers between devices  49 us (36%)
  Pallas kernels  14.3 us (11%)
  other arithmetic  5.13 us (4%)
  local copies, waits for them, and re-layouts  3.97 us (3%)
  matrix products  3.44 us (3%)
    ppermute x25, waiting for transfers between devices, shift(): return lax.ppermute(a, ('dp', 'et'), plane_perm(first, step))  41.3 us
    ppermute x25, starting transfers between devices, shift(): return lax.ppermute(a, ('dp', 'et'), plane_perm(first, step))  36.2 us
    pallas_call x6, Pallas kernels, ffn(): pl.pallas_call(ffn_body, in_specs=[pl.BlockSpec(memory_space=pltpu.SMEM)]...  14.3 us
    ppermute x1, starting transfers between devices, on_device(): lax.ppermute(done1[:, :half], ('expert', 'et'), [(b, a) for a, b in send[...  7.75 us
    ppermute x2, waiting for transfers between devices, dispatch(): lax.ppermute(tie(rows, *after) if after else rows, ('expert', 'et'), send...  5.79 us
    ppermute x2, starting transfers between devices, dispatch(): lax.ppermute(tie(rows, *after) if after else rows, ('expert', 'et'), send...  5.74 us
    ppermute x5, starting transfers between devices, swap(): return lax.ppermute(a, 'et', [(0, 1), (1, 0)])  4.85 us
    ppermute x1, starting transfers between devices, on_device(): back0 = lax.ppermute(done0, ('expert', 'et'), [(b, a) for a, b in send[0]])  3 us
  transfers between devices with their start and end apart: 35, of which 18 were waited for; matrix products, arithmetic and copies ran while one was open for 7% of the time, Pallas kernels for 11%

profile of v5, /device:TPU:1, one launch (start us, length us, event | category | flops | bytes accessed | tf_op | source)
XLA Modules:
  0.0 135.4 jit_solution(13272416778544063350)
XLA Ops:
  5.7 1.7 %collective-permute-start.5 = (bf16[40,3072]{1,0:T(8,128)(2,1)}, bf16[40,3072]{1,0:T(8,128)(2,1)}, u32[]{:S(2)}, u32[]{:S(2)}) collective-permute-start(bf16[40,3072]{1,0:T(8,128)(2,1)} %get-tuple-element.73), channel_id=1, source_target_pairs={{0,4},{2,6},{4,0},{6,2},{1,3},{3,5},{5,7},{7,1},{8,12},{10,14},{12... | collective-permute-start | bytes 737288 | tf_op jit(solution)/shard_map/ppermute | solution.py:144
  7.4 4.0 %collective-permute-start.4 = (bf16[40,3072]{1,0:T(8,128)(2,1)S(1)}, bf16[40,3072]{1,0:T(8,128)(2,1)}, u32[]{:S(2)}, u32[]{:S(2)}) collective-permute-start(bf16[40,3072]{1,0:T(8,128)(2,1)S(1)} %get-tuple-element.72), channel_id=1, source_target_pairs={{0,0},{2,2},{4,4},{6,6},{1,7},{3,1},{5,3},{7,5},{8,8},{10,10},{12,... | collective-permute-start | bytes 737288 | tf_op jit(solution)/shard_map/ppermute | solution.py:144
  11.4 4.6 %collective-permute-done.5 = bf16[40,3072]{1,0:T(8,128)(2,1)} collective-permute-done((bf16[40,3072]{1,0:T(8,128)(2,1)}, bf16[40,3072]{1,0:T(8,128)(2,1)}, u32[]{:S(2)}, u32[]{:S(2)}) %collective-permute-start.5) | collective-permute-done | bytes 245792 | tf_op jit(solution)/shard_map/ppermute | solution.py:144
  18.3 3.0 %collective-permute-start.8 = (bf16[80,3072]{1,0:T(8,128)(2,1)S(1)}, bf16[80,3072]{1,0:T(8,128)(2,1)S(1)}, u32[]{:S(2)}, u32[]{:S(2)}) collective-permute-start(bf16[80,3072]{1,0:T(8,128)(2,1)S(1)} %pad_maximum_fusion.6), channel_id=1, source_target_pairs={{0,16},{1,65},{8,24},{9,73},{16,0},{17,81},{24,8},{25,89},{32,48},... | collective-permute-start | bytes 1474568 | tf_op jit(solution)/shard_map/ppermute | solution.py:26
  24.3 3.4 %collective-permute-done.8 = bf16[80,3072]{1,0:T(8,128)(2,1)S(1)} collective-permute-done((bf16[80,3072]{1,0:T(8,128)(2,1)S(1)}, bf16[80,3072]{1,0:T(8,128)(2,1)S(1)}, u32[]{:S(2)}, u32[]{:S(2)}) %collective-permute-start.8) | collective-permute-done | bytes 491552 | tf_op jit(solution)/shard_map/ppermute | solution.py:26
  27.7 5.5 %collective-permute-done.7 = bf16[80,3072]{1,0:T(8,128)(2,1)S(1)} collective-permute-done((bf16[80,3072]{1,0:T(8,128)(2,1)S(1)}, bf16[80,3072]{1,0:T(8,128)(2,1)S(1)}, u32[]{:S(2)}, u32[]{:S(2)}) %collective-permute-start.7) | collective-permute-done | bytes 491552 | tf_op jit(solution)/shard_map/ppermute | solution.py:26
  36.3 2.7 %collective-permute-start.13 = (bf16[160,3072]{1,0:T(8,128)(2,1)S(1)}, bf16[160,3072]{1,0:T(8,128)(2,1)S(1)}, u32[]{:S(2)}, u32[]{:S(2)}) collective-permute-start(bf16[160,3072]{1,0:T(8,128)(2,1)S(1)} %pad_maximum_fusion.1.refs_6_), channel_id=1, source_target_pairs={{0,96},{1,25},{8,104},{9,1},{16,112},{17,9},{24,120},{25,17},{32,0... | collective-permute-start | bytes 2949128 | tf_op jit(solution)/shard_map/ppermute | solution.py:26
  41.3 1.8 %ffn.6 = bf16[160,3072]{1,0:T(8,128)(2,1)S(1)} custom-call(s32[1]{0:T(128)} %bitcast.2.core, bf16[3072,256]{1,0:T(8,128)(2,1)S(1)} %bitcast.30, bf16[3072,256]{1,0:T(8,128)(2,1)S(1)} %collective-permute-done.1.refs_1_, bf16[3072,256]{1,0:T(8,128)(2,1)S(1)} %bitcast.37, bf16[3072,256]{1,0:T(8,128)(2,1)S(1)} %collective-permute-done.2.refs_3_, ...), custom_call_target="tpu_custom_call" | custom-call | flops 1509949440 | bytes 11403264 | tf_op jit(solution)/shard_map/ffn/pallas_call | solution.py:95
  43.2 1.8 %ffn.7 = bf16[160,3072]{1,0:T(8,128)(2,1)S(1)} custom-call(s32[1]{0:T(128)} %bitcast.2.core, bf16[3072,256]{1,0:T(8,128)(2,1)S(1)} %bitcast.31, bf16[3072,256]{1,0:T(8,128)(2,1)S(1)} %collective-permute-done.1.refs_1_, bf16[3072,256]{1,0:T(8,128)(2,1)S(1)} %bitcast.38, bf16[3072,256]{1,0:T(8,128)(2,1)S(1)} %collective-permute-done.2.refs_3_, ...), custom_call_target="tpu_custom_call" | custom-call | flops 1509949440 | bytes 11403264 | tf_op jit(solution)/shard_map/ffn/pallas_call | solution.py:95
  45.0 2.9 %collective-permute-done.9.refs_6_ = bf16[160,3072]{1,0:T(8,128)(2,1)S(1)} collective-permute-done((bf16[160,3072]{1,0:T(8,128)(2,1)S(1)}, bf16[160,3072]{1,0:T(8,128)(2,1)S(1)}, u32[]{:S(2)}, u32[]{:S(2)}) %collective-permute-start.9) | collective-permute-done | bytes 983072 | tf_op jit(solution)/shard_map/ppermute | solution.py:26
  49.3 1.7 %collective-permute-start.14 = (bf16[160,1536]{1,0:T(8,128)(2,1)S(1)}, bf16[160,1536]{1,0:T(8,128)(2,1)S(1)}, u32[]{:S(2)}, u32[]{:S(2)}) collective-permute-start(bf16[160,1536]{1,0:T(8,128)(2,1)S(1)} %slice.106), channel_id=1, source_target_pairs={{0,96},{1,25},{8,104},{9,1},{16,112},{17,9},{24,120},{25,17},{32,0... | collective-permute-start | bytes 1474568 | tf_op jit(solution)/shard_map/ppermute | solution.py:26
  51.0 3.5 %ffn.8 = (bf16[160,3072]{1,0:T(8,128)(2,1)S(1)}, bf16[160,3072]{1,0:T(8,128)(2,1)S(1)}) custom-call(s32[1]{0:T(128)} %bitcast.2.core, bf16[3072,256]{1,0:T(8,128)(2,1)S(1)} %bitcast.32, bf16[3072,256]{1,0:T(8,128)(2,1)S(1)} %collective-permute-done.1.refs_1_, bf16[3072,256]{1,0:T(8,128)(2,1)S(1)} %bitcast.39, ...), custom_call_target="tpu_custom_call" | custom-call | flops 3019898880 | bytes 13369344 | tf_op jit(solution)/shard_map/ffn/pallas_call | solution.py:95
  54.5 4.0 %collective-permute-done.12.refs_6_ = bf16[160,3072]{1,0:T(8,128)(2,1)S(1)} collective-permute-done((bf16[160,3072]{1,0:T(8,128)(2,1)S(1)}, bf16[160,3072]{1,0:T(8,128)(2,1)S(1)}, u32[]{:S(2)}, u32[]{:S(2)}) %collective-permute-start.12) | collective-permute-done | bytes 983072 | tf_op jit(solution)/shard_map/ppermute | solution.py:26
  58.6 2.7 %collective-permute-start.25 = (bf16[160,1536]{1,0:T(8,128)(2,1)S(1)}, bf16[160,1536]{1,0:T(8,128)(2,1)S(1)}, u32[]{:S(2)}, u32[]{:S(2)}) collective-permute-start(bf16[160,1536]{1,0:T(8,128)(2,1)S(1)} %slice.114), channel_id=1, source_target_pairs={{0,96},{1,25},{8,104},{9,1},{16,112},{17,9},{24,120},{25,17},{32,0... | collective-permute-start | bytes 1474568 | tf_op jit(solution)/shard_map/ppermute | solution.py:26
  61.4 3.5 %ffn.9 = (bf16[160,3072]{1,0:T(8,128)(2,1)S(1)}, bf16[160,3072]{1,0:T(8,128)(2,1)S(1)}) custom-call(s32[1]{0:T(128)} %bitcast.2.core, bf16[3072,256]{1,0:T(8,128)(2,1)S(1)} %bitcast.33, bf16[3072,256]{1,0:T(8,128)(2,1)S(1)} %collective-permute-done.1.refs_1_, bf16[3072,256]{1,0:T(8,128)(2,1)S(1)} %bitcast.40, ...), custom_call_target="tpu_custom_call" | custom-call | flops 3019898880 | bytes 13369344 | tf_op jit(solution)/shard_map/ffn/pallas_call | solution.py:95
  64.9 1.8 %ffn.10 = (bf16[160,1536]{1,0:T(8,128)(2,1)S(1)}, bf16[160,1536]{1,0:T(8,128)(2,1)S(1)}) custom-call(s32[1]{0:T(128)} %bitcast.2.core, bf16[3072,256]{1,0:T(8,128)(2,1)S(1)} %bitcast.34, bf16[3072,256]{1,0:T(8,128)(2,1)S(1)} %collective-permute-done.1.refs_1_, bf16[3072,256]{1,0:T(8,128)(2,1)S(1)} %bitcast.41, ...), custom_call_target="tpu_custom_call" | custom-call | flops 1509949440 | bytes 11403264 | tf_op jit(solution)/shard_map/ffn/pallas_call | solution.py:95
  69.0 1.8 %ffn.11 = (bf16[160,1536]{1,0:T(8,128)(2,1)S(1)}, bf16[160,1536]{1,0:T(8,128)(2,1)S(1)}) custom-call(s32[1]{0:T(128)} %bitcast.2.core, bf16[3072,256]{1,0:T(8,128)(2,1)S(1)} %bitcast.35, bf16[3072,256]{1,0:T(8,128)(2,1)S(1)} %collective-permute-done.1.refs_1_, bf16[3072,256]{1,0:T(8,128)(2,1)S(1)} %bitcast.42, ...), custom_call_target="tpu_custom_call" | custom-call | flops 1509949440 | bytes 11403264 | tf_op jit(solution)/shard_map/ffn/pallas_call | solution.py:95
  70.8 2.5 %collective-permute-start.28 = (bf16[160,1536]{1,0:T(8,128)(2,1)S(1)}, bf16[160,1536]{1,0:T(8,128)(2,1)S(1)}, u32[]{:S(2)}, u32[]{:S(2)}) collective-permute-start(bf16[160,1536]{1,0:T(8,128)(2,1)S(1)} %get-tuple-element.45), channel_id=1, source_target_pairs={{0,96},{1,25},{8,104},{9,1},{16,112},{17,9},{24,120},{25,17},{32,0... | collective-permute-start | bytes 1474568 | tf_op jit(solution)/shard_map/ppermute | solution.py:26
  75.0 2.8 %collective-permute-start.18 = (bf16[160,3072]{1,0:T(8,128)(2,1)S(1)}, bf16[160,3072]{1,0:T(8,128)(2,1)S(1)}, u32[]{:S(2)}, u32[]{:S(2)}) collective-permute-start(bf16[160,3072]{1,0:T(8,128)(2,1)S(1)} %pad_maximum_fusion.3), channel_id=1, source_target_pairs={{0,96},{1,25},{8,104},{9,1},{16,112},{17,9},{24,120},{25,17},{32,0... | collective-permute-start | bytes 2949128 | tf_op jit(solution)/shard_map/ppermute | solution.py:26
  78.3 1.7 %collective-permute-done.28 = bf16[160,1536]{1,0:T(8,128)(2,1)S(1)} collective-permute-done((bf16[160,1536]{1,0:T(8,128)(2,1)S(1)}, bf16[160,1536]{1,0:T(8,128)(2,1)S(1)}, u32[]{:S(2)}, u32[]{:S(2)}) %collective-permute-start.28) | collective-permute-done | bytes 491552 | tf_op jit(solution)/shard_map/ppermute | solution.py:26
  80.3 2.8 %collective-permute-start.29 = (bf16[160,3072]{1,0:T(8,128)(2,1)S(1)}, bf16[160,3072]{1,0:T(8,128)(2,1)S(1)}, u32[]{:S(2)}, u32[]{:S(2)}) collective-permute-start(bf16[160,3072]{1,0:T(8,128)(2,1)S(1)} %pad_maximum_fusion.5), channel_id=1, source_target_pairs={{0,96},{1,25},{8,104},{9,1},{16,112},{17,9},{24,120},{25,17},{32,0... | collective-permute-start | bytes 2949128 | tf_op jit(solution)/shard_map/ppermute | solution.py:26
  83.4 7.2 %collective-permute-done.18 = bf16[160,3072]{1,0:T(8,128)(2,1)S(1)} collective-permute-done((bf16[160,3072]{1,0:T(8,128)(2,1)S(1)}, bf16[160,3072]{1,0:T(8,128)(2,1)S(1)}, u32[]{:S(2)}, u32[]{:S(2)}) %collective-permute-start.18) | collective-permute-done | bytes 983072 | tf_op jit(solution)/shard_map/ppermute | solution.py:26
  90.6 3.0 %collective-permute-done.16 = bf16[160,3072]{1,0:T(8,128)(2,1)S(1)} collective-permute-done((bf16[160,3072]{1,0:T(8,128)(2,1)S(1)}, bf16[160,3072]{1,0:T(8,128)(2,1)S(1)}, u32[]{:S(2)}, u32[]{:S(2)}) %collective-permute-start.16) | collective-permute-done | bytes 983072 | tf_op jit(solution)/shard_map/ppermute | solution.py:26
  94.1 2.0 %collective-permute-start.21 = (bf16[40,3072]{1,0:T(8,128)(2,1)S(1)}, bf16[40,3072]{1,0:T(8,128)(2,1)S(1)}, u32[]{:S(2)}, u32[]{:S(2)}) collective-permute-start(bf16[40,3072]{1,0:T(8,128)(2,1)S(1)} %get-tuple-element.62), channel_id=1, source_target_pairs={{0,16},{1,65},{8,24},{9,73},{16,0},{17,81},{24,8},{25,89},{32,48},... | collective-permute-start | bytes 737288 | tf_op jit(solution)/shard_map/ppermute | solution.py:26
  97.1 1.6 %collective-permute-start.19 = (bf16[40,3072]{1,0:T(8,128)(2,1)S(1)}, bf16[40,3072]{1,0:T(8,128)(2,1)S(1)}, u32[]{:S(2)}, u32[]{:S(2)}) collective-permute-start(bf16[40,3072]{1,0:T(8,128)(2,1)S(1)} %get-tuple-element.61), channel_id=1, source_target_pairs={{0,24},{1,97},{8,0},{9,105},{16,8},{17,113},{24,16},{25,121},{32,5... | collective-permute-start | bytes 737288 | tf_op jit(solution)/shard_map/ppermute | solution.py:26
  98.7 4.3 %collective-permute-done.29 = bf16[160,3072]{1,0:T(8,128)(2,1)S(1)} collective-permute-done((bf16[160,3072]{1,0:T(8,128)(2,1)S(1)}, bf16[160,3072]{1,0:T(8,128)(2,1)S(1)}, u32[]{:S(2)}, u32[]{:S(2)}) %collective-permute-start.29) | collective-permute-done | bytes 983072 | tf_op jit(solution)/shard_map/ppermute | solution.py:26
  103.1 5.4 %collective-permute-done.27 = bf16[160,3072]{1,0:T(8,128)(2,1)S(1)} collective-permute-done((bf16[160,3072]{1,0:T(8,128)(2,1)S(1)}, bf16[160,3072]{1,0:T(8,128)(2,1)S(1)}, u32[]{:S(2)}, u32[]{:S(2)}) %collective-permute-start.27) | collective-permute-done | bytes 983072 | tf_op jit(solution)/shard_map/ppermute | solution.py:26
  109.2 3.0 %collective-permute-start.22 = (bf16[40,3072]{1,0:T(8,128)(2,1)S(1)}, bf16[40,3072]{1,0:T(8,128)(2,1)S(1)}, u32[]{:S(2)}, u32[]{:S(2)}) collective-permute-start(bf16[40,3072]{1,0:T(8,128)(2,1)S(1)} %add_convert_fusion.7), channel_id=1, source_target_pairs={{4,0},{6,2},{0,4},{2,6},{3,1},{5,3},{7,5},{1,7},{12,8},{14,10},{8,... | collective-permute-start | bytes 737288 | tf_op jit(solution)/shard_map/ppermute | solution.py:192
  112.2 2.9 %collective-permute-start.32 = (bf16[40,3072]{1,0:T(8,128)(2,1)S(1)}, bf16[40,3072]{1,0:T(8,128)(2,1)S(1)}, u32[]{:S(2)}, u32[]{:S(2)}) collective-permute-start(bf16[40,3072]{1,0:T(8,128)(2,1)S(1)} %get-tuple-element.58), channel_id=1, source_target_pairs={{0,16},{1,65},{8,24},{9,73},{16,0},{17,81},{24,8},{25,89},{32,48},... | collective-permute-start | bytes 737288 | tf_op jit(solution)/shard_map/ppermute | solution.py:26
  116.2 1.7 %collective-permute-start.30 = (bf16[40,3072]{1,0:T(8,128)(2,1)S(1)}, bf16[40,3072]{1,0:T(8,128)(2,1)S(1)}, u32[]{:S(2)}, u32[]{:S(2)}) collective-permute-start(bf16[40,3072]{1,0:T(8,128)(2,1)S(1)} %get-tuple-element.60), channel_id=1, source_target_pairs={{0,24},{1,97},{8,0},{9,105},{16,8},{17,113},{24,16},{25,121},{32,5... | collective-permute-start | bytes 737288 | tf_op jit(solution)/shard_map/ppermute | solution.py:26
  118.1 2.5 %collective-permute-start.23 = (bf16[64,1536]{1,0:T(8,128)(2,1)S(1)}, bf16[64,1536]{1,0:T(8,128)(2,1)S(1)}, u32[]{:S(2)}, u32[]{:S(2)}) collective-permute-start(bf16[64,1536]{1,0:T(8,128)(2,1)S(1)} %fusion.4), channel_id=1, source_target_pairs={{0,1},{1,0},{2,3},{3,2},{4,5},{5,4},{6,7},{7,6},{8,9},{9,8},{10,11... | collective-permute-start | bytes 589832 | tf_op jit(solution)/shard_map/ppermute | solution.py:30
  122.8 7.8 %collective-permute-start.33 = (bf16[40,1536]{1,0:T(8,128)(2,1)S(1)}, bf16[40,1536]{1,0:T(8,128)(2,1)S(1)}, u32[]{:S(2)}, u32[]{:S(2)}) collective-permute-start(bf16[40,1536]{1,0:T(8,128)(2,1)S(1)} %get-tuple-element.74), channel_id=1, source_target_pairs={{0,0},{2,2},{4,4},{6,6},{7,1},{1,3},{3,5},{5,7},{8,8},{10,10},{12,... | collective-permute-start | bytes 368648 | tf_op jit(solution)/shard_map/ppermute | solution.py:201
  (99 shorter events, 33.0 us)
Async XLA Ops:
  2.7 15.6 %collective-permute-start.1 = (bf16[3072,256]{1,0:T(8,128)(2,1)}, bf16[3072,256]{1,0:T(8,128)(2,1)S(1)}, u32[]{:S(2)}, u32[]{:S(2)}) collective-permute-start(bf16[3072,256]{1,0:T(8,128)(2,1)} %bitcast.29), channel_id=1, source_target_pairs={{0,1},{1,0},{2,3},{3,2},{4,5},{5,4},{6,7},{7,6},{8,9},{9,8},{10,11... | collective-permute-start | bytes 4718600 | tf_op jit(solution)/shard_map/ppermute | solution.py:30
  3.1 15.2 %collective-permute-start.2 = (bf16[3072,256]{1,0:T(8,128)(2,1)}, bf16[3072,256]{1,0:T(8,128)(2,1)S(1)}, u32[]{:S(2)}, u32[]{:S(2)}) collective-permute-start(bf16[3072,256]{1,0:T(8,128)(2,1)} %bitcast.36), channel_id=1, source_target_pairs={{0,1},{1,0},{2,3},{3,2},{4,5},{5,4},{6,7},{7,6},{8,9},{9,8},{10,11... | collective-permute-start | bytes 4718600 | tf_op jit(solution)/shard_map/ppermute | solution.py:30
  3.2 15.1 %collective-permute-start.3 = (bf16[512,1536]{1,0:T(8,128)(2,1)}, bf16[512,1536]{1,0:T(8,128)(2,1)}, u32[]{:S(2)}, u32[]{:S(2)}) collective-permute-start(bf16[512,1536]{1,0:T(8,128)(2,1)} %bitcast.43), channel_id=1, source_target_pairs={{0,1},{1,0},{2,3},{3,2},{4,5},{5,4},{6,7},{7,6},{8,9},{9,8},{10,11... | collective-permute-start | bytes 4718600 | tf_op jit(solution)/shard_map/ppermute | solution.py:30
  5.7 10.4 %collective-permute-start.5 = (bf16[40,3072]{1,0:T(8,128)(2,1)}, bf16[40,3072]{1,0:T(8,128)(2,1)}, u32[]{:S(2)}, u32[]{:S(2)}) collective-permute-start(bf16[40,3072]{1,0:T(8,128)(2,1)} %get-tuple-element.73), channel_id=1, source_target_pairs={{0,4},{2,6},{4,0},{6,2},{1,3},{3,5},{5,7},{7,1},{8,12},{10,14},{12... | collective-permute-start | bytes 737288 | tf_op jit(solution)/shard_map/ppermute | solution.py:144
  7.4 9.8 %collective-permute-start.4 = (bf16[40,3072]{1,0:T(8,128)(2,1)S(1)}, bf16[40,3072]{1,0:T(8,128)(2,1)}, u32[]{:S(2)}, u32[]{:S(2)}) collective-permute-start(bf16[40,3072]{1,0:T(8,128)(2,1)S(1)} %get-tuple-element.72), channel_id=1, source_target_pairs={{0,0},{2,2},{4,4},{6,6},{1,7},{3,1},{5,3},{7,5},{8,8},{10,10},{12,... | collective-permute-start | bytes 737288 | tf_op jit(solution)/shard_map/ppermute | solution.py:144
  18.3 9.4 %collective-permute-start.8 = (bf16[80,3072]{1,0:T(8,128)(2,1)S(1)}, bf16[80,3072]{1,0:T(8,128)(2,1)S(1)}, u32[]{:S(2)}, u32[]{:S(2)}) collective-permute-start(bf16[80,3072]{1,0:T(8,128)(2,1)S(1)} %pad_maximum_fusion.6), channel_id=1, source_target_pairs={{0,16},{1,65},{8,24},{9,73},{16,0},{17,81},{24,8},{25,89},{32,48},... | collective-permute-start | bytes 1474568 | tf_op jit(solution)/shard_map/ppermute | solution.py:26
  21.3 11.9 %collective-permute-start.7 = (bf16[80,3072]{1,0:T(8,128)(2,1)S(1)}, bf16[80,3072]{1,0:T(8,128)(2,1)S(1)}, u32[]{:S(2)}, u32[]{:S(2)}) collective-permute-start(bf16[80,3072]{1,0:T(8,128)(2,1)S(1)} %pad_maximum_fusion.6), channel_id=1, source_target_pairs={{0,24},{1,97},{8,0},{9,105},{16,8},{17,113},{24,16},{25,121},{32,5... | collective-permute-start | bytes 1474568 | tf_op jit(solution)/shard_map/ppermute | solution.py:26
  22.1 11.2 %collective-permute-start.6 = (bf16[80,3072]{1,0:T(8,128)(2,1)S(1)}, bf16[80,3072]{1,0:T(8,128)(2,1)S(1)}, u32[]{:S(2)}, u32[]{:S(2)}) collective-permute-start(bf16[80,3072]{1,0:T(8,128)(2,1)S(1)} %pad_maximum_fusion.6), channel_id=1, source_target_pairs={{0,8},{1,33},{8,16},{9,41},{16,24},{17,49},{24,0},{25,57},{32,40},... | collective-permute-start | bytes 1474568 | tf_op jit(solution)/shard_map/ppermute | solution.py:26
  33.4 14.5 %collective-permute-start.9 = (bf16[160,3072]{1,0:T(8,128)(2,1)S(1)}, bf16[160,3072]{1,0:T(8,128)(2,1)S(1)}, u32[]{:S(2)}, u32[]{:S(2)}) collective-permute-start(bf16[160,3072]{1,0:T(8,128)(2,1)S(1)} %pad_maximum_fusion.refs_6_), channel_id=1, source_target_pairs={{0,32},{1,9},{8,40},{9,17},{16,48},{17,25},{24,56},{25,1},{32,64},... | collective-permute-start | bytes 2949128 | tf_op jit(solution)/shard_map/ppermute | solution.py:26
  34.7 13.2 %collective-permute-start.10 = (bf16[160,3072]{1,0:T(8,128)(2,1)S(1)}, bf16[160,3072]{1,0:T(8,128)(2,1)S(1)}, u32[]{:S(2)}, u32[]{:S(2)}) collective-permute-start(bf16[160,3072]{1,0:T(8,128)(2,1)S(1)} %pad_maximum_fusion.refs_6_), channel_id=1, source_target_pairs={{0,96},{1,25},{8,104},{9,1},{16,112},{17,9},{24,120},{25,17},{32,0... | collective-permute-start | bytes 2949128 | tf_op jit(solution)/shard_map/ppermute | solution.py:26
  36.2 22.2 %collective-permute-start.12 = (bf16[160,3072]{1,0:T(8,128)(2,1)S(1)}, bf16[160,3072]{1,0:T(8,128)(2,1)S(1)}, u32[]{:S(2)}, u32[]{:S(2)}) collective-permute-start(bf16[160,3072]{1,0:T(8,128)(2,1)S(1)} %pad_maximum_fusion.1.refs_6_), channel_id=1, source_target_pairs={{0,32},{1,9},{8,40},{9,17},{16,48},{17,25},{24,56},{25,1},{32,64},... | collective-permute-start | bytes 2949128 | tf_op jit(solution)/shard_map/ppermute | solution.py:26
  36.3 22.3 %collective-permute-start.13 = (bf16[160,3072]{1,0:T(8,128)(2,1)S(1)}, bf16[160,3072]{1,0:T(8,128)(2,1)S(1)}, u32[]{:S(2)}, u32[]{:S(2)}) collective-permute-start(bf16[160,3072]{1,0:T(8,128)(2,1)S(1)} %pad_maximum_fusion.1.refs_6_), channel_id=1, source_target_pairs={{0,96},{1,25},{8,104},{9,1},{16,112},{17,9},{24,120},{25,17},{32,0... | collective-permute-start | bytes 2949128 | tf_op jit(solution)/shard_map/ppermute | solution.py:26
  48.0 16.9 %collective-permute-start.11 = (bf16[160,1536]{1,0:T(8,128)(2,1)S(1)}, bf16[160,1536]{1,0:T(8,128)(2,1)S(1)}, u32[]{:S(2)}, u32[]{:S(2)}) collective-permute-start(bf16[160,1536]{1,0:T(8,128)(2,1)S(1)} %slice.105), channel_id=1, source_target_pairs={{0,32},{1,9},{8,40},{9,17},{16,48},{17,25},{24,56},{25,1},{32,64},... | collective-permute-start | bytes 1474568 | tf_op jit(solution)/shard_map/ppermute | solution.py:26
  49.3 15.6 %collective-permute-start.14 = (bf16[160,1536]{1,0:T(8,128)(2,1)S(1)}, bf16[160,1536]{1,0:T(8,128)(2,1)S(1)}, u32[]{:S(2)}, u32[]{:S(2)}) collective-permute-start(bf16[160,1536]{1,0:T(8,128)(2,1)S(1)} %slice.106), channel_id=1, source_target_pairs={{0,96},{1,25},{8,104},{9,1},{16,112},{17,9},{24,120},{25,17},{32,0... | collective-permute-start | bytes 1474568 | tf_op jit(solution)/shard_map/ppermute | solution.py:26
  58.5 10.5 %collective-permute-start.24 = (bf16[160,1536]{1,0:T(8,128)(2,1)S(1)}, bf16[160,1536]{1,0:T(8,128)(2,1)S(1)}, u32[]{:S(2)}, u32[]{:S(2)}) collective-permute-start(bf16[160,1536]{1,0:T(8,128)(2,1)S(1)} %slice.113), channel_id=1, source_target_pairs={{0,32},{1,9},{8,40},{9,17},{16,48},{17,25},{24,56},{25,1},{32,64},... | collective-permute-start | bytes 1474568 | tf_op jit(solution)/shard_map/ppermute | solution.py:26
  58.6 10.4 %collective-permute-start.25 = (bf16[160,1536]{1,0:T(8,128)(2,1)S(1)}, bf16[160,1536]{1,0:T(8,128)(2,1)S(1)}, u32[]{:S(2)}, u32[]{:S(2)}) collective-permute-start(bf16[160,1536]{1,0:T(8,128)(2,1)S(1)} %slice.114), channel_id=1, source_target_pairs={{0,96},{1,25},{8,104},{9,1},{16,112},{17,9},{24,120},{25,17},{32,0... | collective-permute-start | bytes 1474568 | tf_op jit(solution)/shard_map/ppermute | solution.py:26
  66.7 8.0 %collective-permute-start.17 = (bf16[160,1536]{1,0:T(8,128)(2,1)S(1)}, bf16[160,1536]{1,0:T(8,128)(2,1)S(1)}, u32[]{:S(2)}, u32[]{:S(2)}) collective-permute-start(bf16[160,1536]{1,0:T(8,128)(2,1)S(1)} %get-tuple-element.39), channel_id=1, source_target_pairs={{0,96},{1,25},{8,104},{9,1},{16,112},{17,9},{24,120},{25,17},{32,0... | collective-permute-start | bytes 1474568 | tf_op jit(solution)/shard_map/ppermute | solution.py:26
  68.5 9.3 %collective-permute-start.15 = (bf16[160,1536]{1,0:T(8,128)(2,1)S(1)}, bf16[160,1536]{1,0:T(8,128)(2,1)S(1)}, u32[]{:S(2)}, u32[]{:S(2)}) collective-permute-start(bf16[160,1536]{1,0:T(8,128)(2,1)S(1)} %get-tuple-element.37), channel_id=1, source_target_pairs={{0,32},{1,9},{8,40},{9,17},{16,48},{17,25},{24,56},{25,1},{32,64},... | collective-permute-start | bytes 1474568 | tf_op jit(solution)/shard_map/ppermute | solution.py:26
  70.8 9.2 %collective-permute-start.28 = (bf16[160,1536]{1,0:T(8,128)(2,1)S(1)}, bf16[160,1536]{1,0:T(8,128)(2,1)S(1)}, u32[]{:S(2)}, u32[]{:S(2)}) collective-permute-start(bf16[160,1536]{1,0:T(8,128)(2,1)S(1)} %get-tuple-element.45), channel_id=1, source_target_pairs={{0,96},{1,25},{8,104},{9,1},{16,112},{17,9},{24,120},{25,17},{32,0... | collective-permute-start | bytes 1474568 | tf_op jit(solution)/shard_map/ppermute | solution.py:26
  73.4 9.7 %collective-permute-start.26 = (bf16[160,1536]{1,0:T(8,128)(2,1)S(1)}, bf16[160,1536]{1,0:T(8,128)(2,1)S(1)}, u32[]{:S(2)}, u32[]{:S(2)}) collective-permute-start(bf16[160,1536]{1,0:T(8,128)(2,1)S(1)} %get-tuple-element.44), channel_id=1, source_target_pairs={{0,32},{1,9},{8,40},{9,17},{16,48},{17,25},{24,56},{25,1},{32,64},... | collective-permute-start | bytes 1474568 | tf_op jit(solution)/shard_map/ppermute | solution.py:26
  75.0 15.6 %collective-permute-start.18 = (bf16[160,3072]{1,0:T(8,128)(2,1)S(1)}, bf16[160,3072]{1,0:T(8,128)(2,1)S(1)}, u32[]{:S(2)}, u32[]{:S(2)}) collective-permute-start(bf16[160,3072]{1,0:T(8,128)(2,1)S(1)} %pad_maximum_fusion.3), channel_id=1, source_target_pairs={{0,96},{1,25},{8,104},{9,1},{16,112},{17,9},{24,120},{25,17},{32,0... | collective-permute-start | bytes 2949128 | tf_op jit(solution)/shard_map/ppermute | solution.py:26
  78.0 15.5 %collective-permute-start.16 = (bf16[160,3072]{1,0:T(8,128)(2,1)S(1)}, bf16[160,3072]{1,0:T(8,128)(2,1)S(1)}, u32[]{:S(2)}, u32[]{:S(2)}) collective-permute-start(bf16[160,3072]{1,0:T(8,128)(2,1)S(1)} %pad_maximum_fusion.2), channel_id=1, source_target_pairs={{0,32},{1,9},{8,40},{9,17},{16,48},{17,25},{24,56},{25,1},{32,64},... | collective-permute-start | bytes 2949128 | tf_op jit(solution)/shard_map/ppermute | solution.py:26
  80.3 22.8 %collective-permute-start.29 = (bf16[160,3072]{1,0:T(8,128)(2,1)S(1)}, bf16[160,3072]{1,0:T(8,128)(2,1)S(1)}, u32[]{:S(2)}, u32[]{:S(2)}) collective-permute-start(bf16[160,3072]{1,0:T(8,128)(2,1)S(1)} %pad_maximum_fusion.5), channel_id=1, source_target_pairs={{0,96},{1,25},{8,104},{9,1},{16,112},{17,9},{24,120},{25,17},{32,0... | collective-permute-start | bytes 2949128 | tf_op jit(solution)/shard_map/ppermute | solution.py:26
  83.3 25.2 %collective-permute-start.27 = (bf16[160,3072]{1,0:T(8,128)(2,1)S(1)}, bf16[160,3072]{1,0:T(8,128)(2,1)S(1)}, u32[]{:S(2)}, u32[]{:S(2)}) collective-permute-start(bf16[160,3072]{1,0:T(8,128)(2,1)S(1)} %pad_maximum_fusion.4), channel_id=1, source_target_pairs={{0,32},{1,9},{8,40},{9,17},{16,48},{17,25},{24,56},{25,1},{32,64},... | collective-permute-start | bytes 2949128 | tf_op jit(solution)/shard_map/ppermute | solution.py:26
  94.1 14.9 %collective-permute-start.21 = (bf16[40,3072]{1,0:T(8,128)(2,1)S(1)}, bf16[40,3072]{1,0:T(8,128)(2,1)S(1)}, u32[]{:S(2)}, u32[]{:S(2)}) collective-permute-start(bf16[40,3072]{1,0:T(8,128)(2,1)S(1)} %get-tuple-element.62), channel_id=1, source_target_pairs={{0,16},{1,65},{8,24},{9,73},{16,0},{17,81},{24,8},{25,89},{32,48},... | collective-permute-start | bytes 737288 | tf_op jit(solution)/shard_map/ppermute | solution.py:26
  96.1 13.0 %collective-permute-start.20 = (bf16[40,3072]{1,0:T(8,128)(2,1)S(1)}, bf16[40,3072]{1,0:T(8,128)(2,1)S(1)}, u32[]{:S(2)}, u32[]{:S(2)}) collective-permute-start(bf16[40,3072]{1,0:T(8,128)(2,1)S(1)} %get-tuple-element.63), channel_id=1, source_target_pairs={{0,8},{1,33},{8,16},{9,41},{16,24},{17,49},{24,0},{25,57},{32,40},... | collective-permute-start | bytes 737288 | tf_op jit(solution)/shard_map/ppermute | solution.py:26
  97.1 11.9 %collective-permute-start.19 = (bf16[40,3072]{1,0:T(8,128)(2,1)S(1)}, bf16[40,3072]{1,0:T(8,128)(2,1)S(1)}, u32[]{:S(2)}, u32[]{:S(2)}) collective-permute-start(bf16[40,3072]{1,0:T(8,128)(2,1)S(1)} %get-tuple-element.61), channel_id=1, source_target_pairs={{0,24},{1,97},{8,0},{9,105},{16,8},{17,113},{24,16},{25,121},{32,5... | collective-permute-start | bytes 737288 | tf_op jit(solution)/shard_map/ppermute | solution.py:26
  109.2 8.7 %collective-permute-start.22 = (bf16[40,3072]{1,0:T(8,128)(2,1)S(1)}, bf16[40,3072]{1,0:T(8,128)(2,1)S(1)}, u32[]{:S(2)}, u32[]{:S(2)}) collective-permute-start(bf16[40,3072]{1,0:T(8,128)(2,1)S(1)} %add_convert_fusion.7), channel_id=1, source_target_pairs={{4,0},{6,2},{0,4},{2,6},{3,1},{5,3},{7,5},{1,7},{12,8},{14,10},{8,... | collective-permute-start | bytes 737288 | tf_op jit(solution)/shard_map/ppermute | solution.py:192
  112.2 8.4 %collective-permute-start.32 = (bf16[40,3072]{1,0:T(8,128)(2,1)S(1)}, bf16[40,3072]{1,0:T(8,128)(2,1)S(1)}, u32[]{:S(2)}, u32[]{:S(2)}) collective-permute-start(bf16[40,3072]{1,0:T(8,128)(2,1)S(1)} %get-tuple-element.58), channel_id=1, source_target_pairs={{0,16},{1,65},{8,24},{9,73},{16,0},{17,81},{24,8},{25,89},{32,48},... | collective-permute-start | bytes 737288 | tf_op jit(solution)/shard_map/ppermute | solution.py:26
  115.2 6.6 %collective-permute-start.31 = (bf16[40,3072]{1,0:T(8,128)(2,1)S(1)}, bf16[40,3072]{1,0:T(8,128)(2,1)S(1)}, u32[]{:S(2)}, u32[]{:S(2)}) collective-permute-start(bf16[40,3072]{1,0:T(8,128)(2,1)S(1)} %get-tuple-element.59), channel_id=1, source_target_pairs={{0,8},{1,33},{8,16},{9,41},{16,24},{17,49},{24,0},{25,57},{32,40},... | collective-permute-start | bytes 737288 | tf_op jit(solution)/shard_map/ppermute | solution.py:26
  116.2 6.5 %collective-permute-start.30 = (bf16[40,3072]{1,0:T(8,128)(2,1)S(1)}, bf16[40,3072]{1,0:T(8,128)(2,1)S(1)}, u32[]{:S(2)}, u32[]{:S(2)}) collective-permute-start(bf16[40,3072]{1,0:T(8,128)(2,1)S(1)} %get-tuple-element.60), channel_id=1, source_target_pairs={{0,24},{1,97},{8,0},{9,105},{16,8},{17,113},{24,16},{25,121},{32,5... | collective-permute-start | bytes 737288 | tf_op jit(solution)/shard_map/ppermute | solution.py:26
  122.8 9.6 %collective-permute-start.33 = (bf16[40,1536]{1,0:T(8,128)(2,1)S(1)}, bf16[40,1536]{1,0:T(8,128)(2,1)S(1)}, u32[]{:S(2)}, u32[]{:S(2)}) collective-permute-start(bf16[40,1536]{1,0:T(8,128)(2,1)S(1)} %get-tuple-element.74), channel_id=1, source_target_pairs={{0,0},{2,2},{4,4},{6,6},{7,1},{1,3},{3,5},{5,7},{8,8},{10,10},{12,... | collective-permute-start | bytes 368648 | tf_op jit(solution)/shard_map/ppermute | solution.py:201
  (8 other events, 34.1 us)
